TPU v7x, 128 devices: a whole 4x4x4 slice. The times are simulated.
128 devices in a mesh: blk: 32 (over x, y, core), rep: 4 (over z).
Axes of the slice: x: 4, y: 4, z: 4, core: 2. Of those that a mesh axis runs over, the one named last changes fastest.
Arguments:
- tracers: float32 [12, 524288], P(None, 'blk'), may hold values from -6 to 6
- explicit_blocks: bfloat16 [4096, 12, 128, 128], P('blk', 'rep'), may hold values from -0.15625 to 0.15625
- explicit_cols: int32 [4096, 12], P('blk', 'rep'), may hold values from 0 to 4095, as said below
- explicit_sends: int32 [32, 4, 4, 64], P('blk', 'rep'), may hold values from -1 to 127, as said below
- implicit_blocks: bfloat16 [4096, 12, 128, 128], P('blk', 'rep'), may hold values from -0.15625 to 0.15625
- implicit_cols: int32 [4096, 12], P('blk', 'rep'), may hold values from 0 to 4095, as said below
- implicit_sends: int32 [32, 4, 4, 64], P('blk', 'rep'), may hold values from -1 to 127, as said below
- coupling: float32 [12, 12], replicated, may hold values from -1.75 to 1.75
- wet: int32 [524288], P('blk'), may hold values 0 or 1
Outputs:
- updated: float32 [12, 524288], P(None, ('blk', 'rep'))
Inputs may be any that keep to these rules, and one draw needn't show every extreme that they name: `explicit_cols`: for block row b on device d = b // 128 and rep index r, slot r * 3 names a block of device d; every other slot of that rep index names a block of a device d' != d with |d' - d| <= 2, listed in that owner's send list for rep index r and direction d - d'. `explicit_sends`: entry (s, r, j, e) is a block index local to device s of a block that device s + o_j reads in its slots of rep index r, with o_j the j-th of -2 .. -1, 1 .. 2; the entries of one list are distinct, used ones first and -1 after them; every listed block is read and every block read from another device is listed; lists toward devices outside the axis are empty; for every sender and rep index one list holds 64 entries. `implicit_cols`: as for explicit_cols, with implicit_sends. `implicit_sends`: as for explicit_sends, for implicit_cols.
All inputs are finite; a program needn't handle non-finite values. No bound on the sum of `wet` on one device may be relied on, other than what follows from the above.
Results may differ from a plain program's by a relative error of at most 0.0029.
Values may be sent and summed in bfloat16 or wider, within the bound.
No kernel may reach another device: no remote copies, remote signals or barrier semaphores. Data moves between devices by JAX's collectives and lax.ppermute only.
A program may use at most 128 MiB of HBM per device.

v0:
```python
import jax
import jax.numpy as jnp
from jax import lax
from jax.sharding import PartitionSpec as P

REACH = 2


def passed_along(block, axis, distance):
    devices = range(lax.axis_size(axis))
    route = [(i - distance, i) for i in devices if i - distance in devices]
    return lax.ppermute(block, axis, route)


def reach_offsets():
    return [offset for offset in range(-REACH, REACH + 1) if offset != 0]


def outgoing(planes, sends):
    send_rows = sends[0, 0]
    outbound = []
    labels = []
    for lane_no in range(send_rows.shape[0]):
        outbound.append(jnp.take(planes, jnp.maximum(send_rows[lane_no], 0), axis=1))
        labels.append(send_rows[lane_no] + 1)
    return (outbound, labels)


def incoming(planes, blocks, columns, pieces, labels, offsets):
    device_rank = lax.axis_index("blk")
    row_count = planes.shape[1]
    known_parts = []
    for lane_no, offset in enumerate(offsets):
        owner_base = (device_rank - offset) * row_count
        known_parts.append(jnp.where(labels[lane_no] > 0, owner_base + labels[lane_no] - 1, -1))
    known_ids = jnp.concatenate(known_parts)
    zero_plane = jnp.zeros((planes.shape[0], 1, planes.shape[2]), planes.dtype)
    block_table = jnp.concatenate([planes] + pieces + [zero_plane], axis=1)
    zero_spot = block_table.shape[1] - 1
    wanted = columns.reshape(-1)
    matches = (wanted[:, None] == known_ids[None, :]).astype(jnp.int32)
    found_slot = jnp.sum(matches * jnp.arange(known_ids.shape[0], dtype=jnp.int32)[None, :], axis=1)
    found_any = jnp.sum(matches, axis=1) > 0
    owners = wanted // row_count
    remote_spot = jnp.where(found_any, row_count + found_slot, zero_spot)
    position = jnp.where(owners == device_rank, wanted - device_rank * row_count, remote_spot)
    picked = jnp.take(block_table, position, axis=1)
    picked = picked.reshape(planes.shape[0], row_count, columns.shape[1], planes.shape[2])
    products = jnp.einsum("bkij,tbkj->tbi", blocks, picked, preferred_element_type=jnp.float32)
    return products.reshape(planes.shape[0], -1)


def on_device(
    tracers,
    explicit_blocks,
    explicit_cols,
    explicit_sends,
    implicit_blocks,
    implicit_cols,
    implicit_sends,
    coupling,
    wet,
):
    offsets = reach_offsets()
    block_width = explicit_blocks.shape[-1]
    tracer_count = tracers.shape[0]
    quarter = tracers.shape[1] // lax.axis_size("rep")
    share_start = lax.axis_index("rep") * quarter
    wet_share = lax.dynamic_slice_in_dim(wet, share_start, quarter, 0).astype(jnp.float32)
    state_b = tracers.astype(jnp.bfloat16)
    planes = state_b.reshape(tracer_count, -1, block_width)
    outbound, labels = outgoing(planes, explicit_sends)
    pieces = []
    got_labels = []
    for lane_no, offset in enumerate(offsets):
        piece, label = passed_along((outbound[lane_no], labels[lane_no]), "blk", offset)
        pieces.append(piece)
        got_labels.append(label)
    explicit_part = incoming(planes, explicit_blocks, explicit_cols, pieces, got_labels, offsets)
    explicit_sum = lax.psum(explicit_part, "rep")
    middle = tracers + explicit_sum
    wet_float = wet.astype(jnp.float32)
    sources = wet_float[None, :] * jnp.tanh(
        jnp.dot(coupling, middle, precision=lax.Precision.HIGHEST)
    )
    before = middle + sources
    before_b = before.astype(jnp.bfloat16)
    before_share = lax.dynamic_slice_in_dim(before, share_start, quarter, 1)
    planes = before_b.reshape(tracer_count, -1, block_width)
    outbound, labels = outgoing(planes, implicit_sends)
    pieces = []
    got_labels = []
    for lane_no, offset in enumerate(offsets):
        piece, label = passed_along((outbound[lane_no], labels[lane_no]), "blk", offset)
        pieces.append(piece)
        got_labels.append(label)
    implicit_part = incoming(planes, implicit_blocks, implicit_cols, pieces, got_labels, offsets)
    implicit_sum = lax.psum_scatter(implicit_part, "rep", scatter_dimension=1, tiled=True)
    return wet_share[None, :] * (before_share + implicit_sum)


def solution(mesh):
    in_specs = (
        P(None, "blk"),
        P("blk", "rep", None, None),
        P("blk", "rep"),
        P("blk", "rep", None, None),
        P("blk", "rep", None, None),
        P("blk", "rep"),
        P("blk", "rep", None, None),
        P(),
        P("blk"),
    )
    out_specs = P(None, ("blk", "rep"))
    return jax.shard_map(
        on_device, mesh=mesh, in_specs=in_specs, out_specs=out_specs, check_vma=False
    )
```

profile of v0, /device:TPU:6, one launch (start us, length us, event | category | flops | bytes accessed | tf_op | source)
XLA Modules:
  0.0 206.5 jit_solution(10541807580460183330)
XLA Ops:
  6.5 1.4 add_bitcast_fusion.7
  8.0 3.5 %collective-permute-start.7 = (s32[64]{0:T(128)}, s32[64]{0:T(128)}, u32[]{:S(2)}, u32[]{:S(2)}) collective-permute-start(s32[64]{0:T(128)} %get-tuple-element.48), channel_id=1, source_target_pairs={{0,8},{4,12},{8,16},{12,20},{16,24},{20,28},{24,32},{28,36},{32,40... | collective-permute-start | bytes 776 | tf_op jit(solution)/shard_map/ppermute | solution.py:12
  11.4 1.9 collective-permute-start.6
  13.4 5.8 %collective-permute-start.5 = (s32[64]{0:T(128)}, s32[64]{0:T(128)}, u32[]{:S(2)}, u32[]{:S(2)}) collective-permute-start(s32[64]{0:T(128)} %get-tuple-element.46), channel_id=1, source_target_pairs={{4,0},{8,4},{12,8},{16,12},{20,16},{24,20},{28,24},{32,28},{36,32}... | collective-permute-start | bytes 776 | tf_op jit(solution)/shard_map/ppermute | solution.py:12
  19.1 2.4 %collective-permute-start.4 = (s32[64]{0:T(128)}, s32[64]{0:T(128)}, u32[]{:S(2)}, u32[]{:S(2)}) collective-permute-start(s32[64]{0:T(128)} %get-tuple-element.45), channel_id=1, source_target_pairs={{8,0},{12,4},{16,8},{20,12},{24,16},{28,20},{32,24},{36,28},{40,32... | collective-permute-start | bytes 776 | tf_op jit(solution)/shard_map/ppermute | solution.py:12
  21.5 1.4 compare_and_fusion.6
  22.9 1.3 convert_element_type.19
  25.5 3.2 %collective-permute-start = (bf16[12,64,128]{2,0,1:T(8,128)(2,1)S(1)}, bf16[12,64,128]{2,0,1:T(8,128)(2,1)}, u32[]{:S(2)}, u32[]{:S(2)}) collective-permute-start(bf16[12,64,128]{2,0,1:T(8,128)(2,1)S(1)} %select_bitcast_fusion.7), channel_id=1, source_target_pairs={{8,0},{12,4},{16,8},{20,12},{24,16},{28,20},{32,24},{36,28},{40,32... | collective-permute-start | bytes 589832 | tf_op jit(solution)/shard_map/ppermute | solution.py:12
  30.1 0.8 reshape.89
  35.1 0.8 select_bitcast_fusion.6
  35.9 0.8 select_bitcast_fusion.5
  36.7 0.8 select_bitcast_fusion.4
  37.5 0.8 copy.43
  38.6 1.9 collective-permute-start.1
  41.1 2.4 %collective-permute-start.2 = (bf16[12,64,128]{2,0,1:T(8,128)(2,1)S(1)}, bf16[12,64,128]{2,0,1:T(8,128)(2,1)S(1)}, u32[]{:S(2)}, u32[]{:S(2)}) collective-permute-start(bf16[12,64,128]{2,0,1:T(8,128)(2,1)S(1)} %select_bitcast_fusion.5), channel_id=1, source_target_pairs={{0,4},{4,8},{8,12},{12,16},{16,20},{20,24},{24,28},{28,32},{32,36}... | collective-permute-start | bytes 589832 | tf_op jit(solution)/shard_map/ppermute | solution.py:12
  44.2 2.8 %collective-permute-start.3 = (bf16[12,64,128]{2,0,1:T(8,128)(2,1)S(1)}, bf16[12,64,128]{2,0,1:T(8,128)(2,1)S(1)}, u32[]{:S(2)}, u32[]{:S(2)}) collective-permute-start(bf16[12,64,128]{2,0,1:T(8,128)(2,1)S(1)} %select_bitcast_fusion.4), channel_id=1, source_target_pairs={{0,8},{4,12},{8,16},{12,20},{16,24},{20,28},{24,32},{28,36},{32,40... | collective-permute-start | bytes 589832 | tf_op jit(solution)/shard_map/ppermute | solution.py:12
  47.6 3.5 %collective-permute-start.15 = (s32[64]{0:T(128)}, s32[64]{0:T(128)S(1)}, u32[]{:S(2)}, u32[]{:S(2)}) collective-permute-start(s32[64]{0:T(128)} %get-tuple-element.38), channel_id=1, source_target_pairs={{0,8},{4,12},{8,16},{12,20},{16,24},{20,28},{24,32},{28,36},{32,40... | collective-permute-start | bytes 776 | tf_op jit(solution)/shard_map/ppermute | solution.py:12
  51.8 0.9 fusion.4
  52.7 1.3 compare_and_fusion.5
  54.0 2.9 %collective-permute-done.15 = s32[64]{0:T(128)S(1)} collective-permute-done((s32[64]{0:T(128)}, s32[64]{0:T(128)S(1)}, u32[]{:S(2)}, u32[]{:S(2)}) %collective-permute-start.15) | collective-permute-done | bytes 288 | tf_op jit(solution)/shard_map/ppermute | solution.py:12
  56.9 1.9 collective-permute-start.14
  59.4 4.7 %collective-permute-done.14 = s32[64]{0:T(128)S(1)} collective-permute-done((s32[64]{0:T(128)}, s32[64]{0:T(128)S(1)}, u32[]{:S(2)}, u32[]{:S(2)}) %collective-permute-start.14) | collective-permute-done | bytes 288 | tf_op jit(solution)/shard_map/ppermute | solution.py:12
  64.1 1.9 collective-permute-start.13
  66.6 0.9 collective-permute-done.13
  67.5 1.9 collective-permute-start.12
  70.5 1.0 constant_dynamic-update-slice_fusion.4
  71.7 1.9 gather_fusion.4
  73.7 1.3 broadcast_select_fusion.1
  75.0 7.4 %convolution_bitcast_fusion.1 = f32[12,128,128]{2,0,1:T(8,128)S(1)} fusion(bf16[12,128,3,128]{3,0,2,1:T(8,128)(2,1)S(1)} %bitcast.93, bf16[128,3,128,128]{3,2,1,0:T(8,128)(2,1)} %param.14), kind=kOutput, calls=%fused_computation.17 | convolution fusion | flops 150994944 | bytes 14548992 | tf_op jit(solution)/shard_map/bkij,tbkj->tbi/dot_general | solution.py:49
  82.7 1.6 copy.53
  85.5 48.2 %all-reduce.2.cloned.1.call-done = f32[12,16384]{1,0:T(8,128)} async-done(((f32[12,16384]{1,0:T(8,128)}), f32[12,16384]{1,0:T(8,128)}) %all-reduce.2.cloned.1.call-update) | async-done | bytes 786448 | tf_op jit(solution)/shard_map/psum | solution.py:80
  133.8 3.9 %fusion.16 = (bf16[12,16384]{1,0:T(8,128)(2,1)S(1)}, f32[12,16384]{1,0:T(8,128)}) fusion(f32[12,12]{1,0:T(8,128)S(1)} %copy-done, f32[12,16384]{1,0:T(8,128)S(1)} %copy-done.1, f32[12,16384]{1,0:T(8,128)} %all-reduce.2.cloned.1.call-done, f32[16384]{0:T(1024)S(1)} %convert_element_type.21), kind=kOutput, calls=%fused_computation.115 | convolution fusion | flops 29294592 | bytes 2818624 | tf_op jit(solution)/shard_map/dot_general | solution.py:84
  139.1 5.1 %collective-permute-start.8 = (bf16[12,64,128]{2,0,1:T(8,128)(2,1)S(1)}, bf16[12,64,128]{2,0,1:T(8,128)(2,1)S(1)}, u32[]{:S(2)}, u32[]{:S(2)}) collective-permute-start(bf16[12,64,128]{2,0,1:T(8,128)(2,1)S(1)} %select_bitcast_fusion.3), channel_id=1, source_target_pairs={{8,0},{12,4},{16,8},{20,12},{24,16},{28,20},{32,24},{36,28},{40,32... | collective-permute-start | bytes 589832 | tf_op jit(solution)/shard_map/ppermute | solution.py:12
  145.0 1.9 collective-permute-start.9
  147.0 0.8 gather_fusion.7
  147.9 2.4 %collective-permute-start.10 = (bf16[12,64,128]{2,0,1:T(8,128)(2,1)S(1)}, bf16[12,64,128]{2,0,1:T(8,128)(2,1)}, u32[]{:S(2)}, u32[]{:S(2)}) collective-permute-start(bf16[12,64,128]{2,0,1:T(8,128)(2,1)S(1)} %select_bitcast_fusion.1), channel_id=1, source_target_pairs={{0,4},{4,8},{8,12},{12,16},{16,20},{20,24},{24,28},{28,32},{32,36}... | collective-permute-start | bytes 589832 | tf_op jit(solution)/shard_map/ppermute | solution.py:12
  150.3 0.8 gather_fusion.8
  151.2 2.1 %collective-permute-start.11 = (bf16[12,64,128]{2,0,1:T(8,128)(2,1)S(1)}, bf16[12,64,128]{2,0,1:T(8,128)(2,1)S(1)}, u32[]{:S(2)}, u32[]{:S(2)}) collective-permute-start(bf16[12,64,128]{2,0,1:T(8,128)(2,1)S(1)} %select_bitcast_fusion), channel_id=1, source_target_pairs={{0,8},{4,12},{8,16},{12,20},{16,24},{20,28},{24,32},{28,36},{32,40... | collective-permute-start | bytes 589832 | tf_op jit(solution)/shard_map/ppermute | solution.py:12
  153.4 1.0 constant_dynamic-update-slice_fusion.9
  154.4 3.4 %collective-permute-done.10 = bf16[12,64,128]{2,0,1:T(8,128)(2,1)} collective-permute-done((bf16[12,64,128]{2,0,1:T(8,128)(2,1)S(1)}, bf16[12,64,128]{2,0,1:T(8,128)(2,1)}, u32[]{:S(2)}, u32[]{:S(2)}) %collective-permute-start.10) | collective-permute-done | bytes 196640 | tf_op jit(solution)/shard_map/ppermute | solution.py:12
  157.8 1.0 constant_dynamic-update-slice_fusion.8
  158.8 4.7 %collective-permute-done.11 = bf16[12,64,128]{2,0,1:T(8,128)(2,1)S(1)} collective-permute-done((bf16[12,64,128]{2,0,1:T(8,128)(2,1)S(1)}, bf16[12,64,128]{2,0,1:T(8,128)(2,1)S(1)}, u32[]{:S(2)}, u32[]{:S(2)}) %collective-permute-start.11) | collective-permute-done | bytes 196640 | tf_op jit(solution)/shard_map/ppermute | solution.py:12
  163.5 1.9 gather_fusion.9
  165.4 1.3 broadcast_select_fusion
  166.7 7.4 %convolution_bitcast_fusion = f32[12,128,128]{2,0,1:T(8,128)S(1)} fusion(bf16[12,128,3,128]{3,0,2,1:T(8,128)(2,1)S(1)} %bitcast.94, bf16[128,3,128,128]{3,2,1,0:T(8,128)(2,1)} %param.17), kind=kOutput, calls=%fused_computation.16 | convolution fusion | flops 150994944 | bytes 14548992 | tf_op jit(solution)/shard_map/bkij,tbkj->tbi/dot_general | solution.py:49
  174.4 1.6 copy.55
  176.1 21.9 %reduce-scatter.2.cloned.1.call-done = f32[12,4096]{1,0:T(8,128)} async-done(((f32[12,16384]{1,0:T(8,128)}), f32[12,4096]{1,0:T(8,128)}) %reduce-scatter.2.cloned.1.call-update) | async-done | bytes 196624 | tf_op jit(solution)/shard_map/reduce_scatter | solution.py:98
  197.9 1.8 add_multiply_fusion
  (99 shorter events, 16.6 us)
Async XLA Ops:
  6.5 127.2 %copy-start = (f32[12,12]{1,0:T(8,128)S(1)}, f32[12,12]{1,0:T(8,128)}, u32[]{:S(2)}) copy-start(f32[12,12]{1,0:T(8,128)} %param.20) | copy-start | bytes 1732
  6.5 127.2 %all-reduce.2.cloned.1.call-start = ((), (), s32[]{:S(2)}) async-start(), calls=%async_computation.1 | async-start | bytes 2097152 | tf_op jit(solution)/shard_map/psum | solution.py:80
  8.0 30.6 %collective-permute-start.7 = (s32[64]{0:T(128)}, s32[64]{0:T(128)}, u32[]{:S(2)}, u32[]{:S(2)}) collective-permute-start(s32[64]{0:T(128)} %get-tuple-element.48), channel_id=1, source_target_pairs={{0,8},{4,12},{8,16},{12,20},{16,24},{20,28},{24,32},{28,36},{32,40... | collective-permute-start | bytes 776 | tf_op jit(solution)/shard_map/ppermute | solution.py:12
  11.4 29.7 %collective-permute-start.6 = (s32[64]{0:T(128)}, s32[64]{0:T(128)}, u32[]{:S(2)}, u32[]{:S(2)}) collective-permute-start(s32[64]{0:T(128)} %get-tuple-element.47), channel_id=1, source_target_pairs={{0,4},{4,8},{8,12},{12,16},{16,20},{20,24},{24,28},{28,32},{32,36}... | collective-permute-start | bytes 776 | tf_op jit(solution)/shard_map/ppermute | solution.py:12
  13.4 30.8 %collective-permute-start.5 = (s32[64]{0:T(128)}, s32[64]{0:T(128)}, u32[]{:S(2)}, u32[]{:S(2)}) collective-permute-start(s32[64]{0:T(128)} %get-tuple-element.46), channel_id=1, source_target_pairs={{4,0},{8,4},{12,8},{16,12},{20,16},{24,20},{28,24},{32,28},{36,32}... | collective-permute-start | bytes 776 | tf_op jit(solution)/shard_map/ppermute | solution.py:12
  19.1 28.5 %collective-permute-start.4 = (s32[64]{0:T(128)}, s32[64]{0:T(128)}, u32[]{:S(2)}, u32[]{:S(2)}) collective-permute-start(s32[64]{0:T(128)} %get-tuple-element.45), channel_id=1, source_target_pairs={{8,0},{12,4},{16,8},{20,12},{24,16},{28,20},{32,24},{36,28},{40,32... | collective-permute-start | bytes 776 | tf_op jit(solution)/shard_map/ppermute | solution.py:12
  24.3 4.4 %copy-start.4 = (s32[1,1,4,64]{3,2,1,0:T(4,128)S(1)}, s32[1,1,4,64]{3,2,1,0:T(4,128)}, u32[]{:S(2)}) copy-start(s32[1,1,4,64]{3,2,1,0:T(4,128)} %param.19) | copy-start | bytes 3076
  24.3 5.6 %copy-start.9 = (s32[128,3]{0,1:T(4,128)S(1)}, s32[128,3]{0,1:T(4,128)}, u32[]{:S(2)}) copy-start(s32[128,3]{0,1:T(4,128)} %param.15) | copy-start | bytes 4612
  25.5 12.0 %copy-start.2 = (s32[16384]{0:T(1024)S(1)}, s32[16384]{0:T(1024)}, u32[]{:S(2)}) copy-start(s32[16384]{0:T(1024)} %param.21) | copy-start | bytes 196612
  25.5 45.0 %collective-permute-start = (bf16[12,64,128]{2,0,1:T(8,128)(2,1)S(1)}, bf16[12,64,128]{2,0,1:T(8,128)(2,1)}, u32[]{:S(2)}, u32[]{:S(2)}) collective-permute-start(bf16[12,64,128]{2,0,1:T(8,128)(2,1)S(1)} %select_bitcast_fusion.7), channel_id=1, source_target_pairs={{8,0},{12,4},{16,8},{20,12},{24,16},{28,20},{32,24},{36,28},{40,32... | collective-permute-start | bytes 589832 | tf_op jit(solution)/shard_map/ppermute | solution.py:12
  38.6 33.0 %collective-permute-start.1 = (bf16[12,64,128]{2,0,1:T(8,128)(2,1)S(1)}, bf16[12,64,128]{2,0,1:T(8,128)(2,1)S(1)}, u32[]{:S(2)}, u32[]{:S(2)}) collective-permute-start(bf16[12,64,128]{2,0,1:T(8,128)(2,1)S(1)} %select_bitcast_fusion.6), channel_id=1, source_target_pairs={{4,0},{8,4},{12,8},{16,12},{20,16},{24,20},{28,24},{32,28},{36,32}... | collective-permute-start | bytes 589832 | tf_op jit(solution)/shard_map/ppermute | solution.py:12
  41.1 30.5 %collective-permute-start.2 = (bf16[12,64,128]{2,0,1:T(8,128)(2,1)S(1)}, bf16[12,64,128]{2,0,1:T(8,128)(2,1)S(1)}, u32[]{:S(2)}, u32[]{:S(2)}) collective-permute-start(bf16[12,64,128]{2,0,1:T(8,128)(2,1)S(1)} %select_bitcast_fusion.5), channel_id=1, source_target_pairs={{0,4},{4,8},{8,12},{12,16},{16,20},{20,24},{24,28},{28,32},{32,36}... | collective-permute-start | bytes 589832 | tf_op jit(solution)/shard_map/ppermute | solution.py:12
  44.2 27.5 %collective-permute-start.3 = (bf16[12,64,128]{2,0,1:T(8,128)(2,1)S(1)}, bf16[12,64,128]{2,0,1:T(8,128)(2,1)S(1)}, u32[]{:S(2)}, u32[]{:S(2)}) collective-permute-start(bf16[12,64,128]{2,0,1:T(8,128)(2,1)S(1)} %select_bitcast_fusion.4), channel_id=1, source_target_pairs={{0,8},{4,12},{8,16},{12,20},{16,24},{20,28},{24,32},{28,36},{32,40... | collective-permute-start | bytes 589832 | tf_op jit(solution)/shard_map/ppermute | solution.py:12
  47.6 9.3 %collective-permute-start.15 = (s32[64]{0:T(128)}, s32[64]{0:T(128)S(1)}, u32[]{:S(2)}, u32[]{:S(2)}) collective-permute-start(s32[64]{0:T(128)} %get-tuple-element.38), channel_id=1, source_target_pairs={{0,8},{4,12},{8,16},{12,20},{16,24},{20,28},{24,32},{28,36},{32,40... | collective-permute-start | bytes 776 | tf_op jit(solution)/shard_map/ppermute | solution.py:12
  56.9 7.2 %collective-permute-start.14 = (s32[64]{0:T(128)}, s32[64]{0:T(128)S(1)}, u32[]{:S(2)}, u32[]{:S(2)}) collective-permute-start(s32[64]{0:T(128)} %get-tuple-element.37), channel_id=1, source_target_pairs={{0,4},{4,8},{8,12},{12,16},{16,20},{20,24},{24,28},{28,32},{32,36}... | collective-permute-start | bytes 776 | tf_op jit(solution)/shard_map/ppermute | solution.py:12
  64.1 3.4 %collective-permute-start.13 = (s32[64]{0:T(128)}, s32[64]{0:T(128)S(1)}, u32[]{:S(2)}, u32[]{:S(2)}) collective-permute-start(s32[64]{0:T(128)} %get-tuple-element.36), channel_id=1, source_target_pairs={{4,0},{8,4},{12,8},{16,12},{20,16},{24,20},{28,24},{32,28},{36,32}... | collective-permute-start | bytes 776 | tf_op jit(solution)/shard_map/ppermute | solution.py:12
  67.5 16.9 %collective-permute-start.12 = (s32[64]{0:T(128)}, s32[64]{0:T(128)}, u32[]{:S(2)}, u32[]{:S(2)}) collective-permute-start(s32[64]{0:T(128)} %get-tuple-element.35), channel_id=1, source_target_pairs={{8,0},{12,4},{16,8},{20,12},{24,16},{28,20},{32,24},{36,28},{40,32... | collective-permute-start | bytes 776 | tf_op jit(solution)/shard_map/ppermute | solution.py:12
  70.5 1.2 copy-start.3
  71.6 2.1 %copy-start.10 = (pred[384]{0:T(512)(128)(4,1)S(1)}, pred[384]{0:T(512)(128)(4,1)}, u32[]{:S(2)}) copy-start(pred[384]{0:T(512)(128)(4,1)} %get-tuple-element.21) | copy-start | bytes 1156
  82.7 2.4 %copy-start.11 = (s32[64]{0:T(128)S(1)}, s32[64]{0:T(128)}, u32[]{:S(2)}) copy-start(s32[64]{0:T(128)} %compare_select_fusion.12) | copy-start | bytes 772
  82.7 2.4 %copy-start.12 = (s32[64]{0:T(128)S(1)}, s32[64]{0:T(128)}, u32[]{:S(2)}) copy-start(s32[64]{0:T(128)} %compare_select_fusion.13) | copy-start | bytes 772
  82.7 2.4 %copy-start.13 = (s32[64]{0:T(128)S(1)}, s32[64]{0:T(128)}, u32[]{:S(2)}) copy-start(s32[64]{0:T(128)} %compare_select_fusion.14) | copy-start | bytes 772
  82.7 51.0 %copy-start.1 = (f32[12,16384]{1,0:T(8,128)S(1)}, f32[12,16384]{1,0:T(8,128)}, u32[]{:S(2)}) copy-start(f32[12,16384]{1,0:T(8,128)} %param.13) | copy-start | bytes 2359300
  84.4 113.6 %reduce-scatter.2.cloned.1.call-start = ((), (), s32[]{:S(2)}) async-start(), calls=%async_computation.2 | async-start | bytes 1310720 | tf_op jit(solution)/shard_map/reduce_scatter | solution.py:98
  137.7 1.3 copy-start.8
  137.8 7.1 %copy-start.7 = (pred[64]{0:T(512)(128)(4,1)S(1)}, pred[64]{0:T(512)(128)(4,1)}, u32[]{:S(2)}) copy-start(pred[64]{0:T(512)(128)(4,1)} %get-tuple-element.39) | copy-start | bytes 196
  137.8 9.9 %copy-start.6 = (pred[64]{0:T(512)(128)(4,1)S(1)}, pred[64]{0:T(512)(128)(4,1)}, u32[]{:S(2)}) copy-start(pred[64]{0:T(512)(128)(4,1)} %get-tuple-element.43) | copy-start | bytes 196
  138.2 12.9 %copy-start.5 = (pred[64]{0:T(512)(128)(4,1)S(1)}, pred[64]{0:T(512)(128)(4,1)}, u32[]{:S(2)}) copy-start(pred[64]{0:T(512)(128)(4,1)} %get-tuple-element.13) | copy-start | bytes 196
  139.1 14.2 %collective-permute-start.8 = (bf16[12,64,128]{2,0,1:T(8,128)(2,1)S(1)}, bf16[12,64,128]{2,0,1:T(8,128)(2,1)S(1)}, u32[]{:S(2)}, u32[]{:S(2)}) collective-permute-start(bf16[12,64,128]{2,0,1:T(8,128)(2,1)S(1)} %select_bitcast_fusion.3), channel_id=1, source_target_pairs={{8,0},{12,4},{16,8},{20,12},{24,16},{28,20},{32,24},{36,28},{40,32... | collective-permute-start | bytes 589832 | tf_op jit(solution)/shard_map/ppermute | solution.py:12
  145.0 8.3 %collective-permute-start.9 = (bf16[12,64,128]{2,0,1:T(8,128)(2,1)S(1)}, bf16[12,64,128]{2,0,1:T(8,128)(2,1)}, u32[]{:S(2)}, u32[]{:S(2)}) collective-permute-start(bf16[12,64,128]{2,0,1:T(8,128)(2,1)S(1)} %select_bitcast_fusion.2), channel_id=1, source_target_pairs={{4,0},{8,4},{12,8},{16,12},{20,16},{24,20},{28,24},{32,28},{36,32}... | collective-permute-start | bytes 589832 | tf_op jit(solution)/shard_map/ppermute | solution.py:12
  147.9 9.9 %collective-permute-start.10 = (bf16[12,64,128]{2,0,1:T(8,128)(2,1)S(1)}, bf16[12,64,128]{2,0,1:T(8,128)(2,1)}, u32[]{:S(2)}, u32[]{:S(2)}) collective-permute-start(bf16[12,64,128]{2,0,1:T(8,128)(2,1)S(1)} %select_bitcast_fusion.1), channel_id=1, source_target_pairs={{0,4},{4,8},{8,12},{12,16},{16,20},{20,24},{24,28},{28,32},{32,36}... | collective-permute-start | bytes 589832 | tf_op jit(solution)/shard_map/ppermute | solution.py:12
  151.2 12.2 %collective-permute-start.11 = (bf16[12,64,128]{2,0,1:T(8,128)(2,1)S(1)}, bf16[12,64,128]{2,0,1:T(8,128)(2,1)S(1)}, u32[]{:S(2)}, u32[]{:S(2)}) collective-permute-start(bf16[12,64,128]{2,0,1:T(8,128)(2,1)S(1)} %select_bitcast_fusion), channel_id=1, source_target_pairs={{0,8},{4,12},{8,16},{12,20},{16,24},{20,28},{24,32},{28,36},{32,40... | collective-permute-start | bytes 589832 | tf_op jit(solution)/shard_map/ppermute | solution.py:12
Sparse Core Ops, SparseCore 0:
  84.5 49.2 all-reduce.1
  176.2 21.7 reduce-scatter.1
where the time goes:
time: 208 us; the launch traced here: 207 us
  waiting for transfers between devices  86.7 us (42%)
  starting transfers between devices  44.5 us (21%)
  other arithmetic  23.4 us (11%)
  local copies, waits for them, and re-layouts  19.3 us (9%)
  matrix products  18.6 us (9%)
  between operations  14.1 us (7%)
    psum x1, waiting for transfers between devices, on_device(): explicit_sum = lax.psum(explicit_part, 'rep')  48.2 us
    ppermute x16, starting transfers between devices, passed_along(): return lax.ppermute(block, axis, route)  44.5 us
    reduce_scatter x1, waiting for transfers between devices, on_device(): lax.psum_scatter(implicit_part, 'rep', scatter_dimension=1, tiled=True)  21.9 us
    ppermute x16, waiting for transfers between devices, passed_along(): return lax.ppermute(block, axis, route)  16.6 us
    dot_general x2, matrix products, incoming(): jnp.einsum('bkij,tbkj->tbi', blocks, picked, preferred_element_type=jnp.f...  14.7 us
    unnamed x44, local copies, waits for them, and re-layouts  7.63 us
    gather x8, local copies, waits for them, and re-layouts, outgoing(): jnp.take(planes, jnp.maximum(send_rows[lane_no], 0), axis=1)  5.55 us
    select_n x8, other arithmetic, incoming(): jnp.where(labels[lane_no] > 0, owner_base + labels[lane_no] - 1, -1)  4.98 us
  transfers between devices with their start and end apart: 18, of which 7 were waited for; matrix products, arithmetic and copies ran while one was open for 19% of the time, Pallas kernels for 0%

commit v1 on v0

v1 whole, which is shorter than its diff:
```python
import functools

import jax
import jax.numpy as jnp
from jax import lax
from jax.experimental import pallas as pl
from jax.experimental.pallas import tpu as pltpu
from jax.sharding import PartitionSpec as P

NTR = 12
BS = 128
NBD = 128
CAP = 64
REP = 4
SHARE = NBD // REP
OFFSETS = (-2, -1, 1, 2)
LIST_ROWS = CAP * NTR
SHARE_ROWS = SHARE * NTR
TABLE = NBD + len(OFFSETS) * CAP
F32 = jnp.float32
BF16 = jnp.bfloat16
I32 = jnp.int32
MIB = 1 << 20

VMEM = pl.BlockSpec(memory_space=pltpu.VMEM)
SMEM = pl.BlockSpec(memory_space=pltpu.SMEM)
ANY = pl.BlockSpec(memory_space=pl.ANY)


def nt(a, b):
    return lax.dot_general(a, b, (((1,), (1,)), ((), ())), preferred_element_type=F32)


def pack4(tiles):
    return jnp.concatenate([t[0:8] for t in tiles] + [t[8:12] for t in tiles], axis=0)


def unpack4(rows):
    return [
        jnp.concatenate([rows[8 * m : 8 * m + 8], rows[32 + 4 * m : 36 + 4 * m]], axis=0)
        for m in range(4)
    ]


def tile16(t):
    return jnp.concatenate([t, jnp.zeros((4, BS), F32)], axis=0).astype(BF16)


def iotas(rows):
    sub = lax.broadcasted_iota(I32, (rows, BS), 0)
    lane = lax.broadcasted_iota(I32, (rows, BS), 1)
    return sub, lane


def before_matrix():
    sub, lane = iotas(BS)
    return jnp.where(sub < lane, 1.0, 0.0).astype(BF16)


def list_order(sends_ref, lane_no):
    entries = sends_ref[lane_no : lane_no + 1, :]
    ids = lax.broadcasted_iota(I32, (BS, CAP), 0)
    hit = jnp.where(ids == entries, 1.0, 0.0).astype(BF16)
    listed = nt(jnp.ones((8, CAP), BF16), hit)
    rank = jnp.dot(listed.astype(BF16), before_matrix(), preferred_element_type=F32)
    spot = lax.broadcasted_iota(I32, (CAP, BS), 0).astype(F32)
    chosen = jnp.where((rank[0:1] == spot) & (listed[0:1] > 0.5), 1.0, 0.0).astype(BF16)
    block = lax.broadcasted_iota(I32, (8, BS), 1).astype(F32).astype(BF16)
    return nt(block, chosen)[0:1].astype(I32)


def table_spots(cols_ref, out_ref, first_block):
    sub, lane = iotas(BS)
    near = lax.broadcasted_iota(I32, (8, BS), 1)
    for row in range(5):
        if row == 2:
            out_ref[row : row + 1, :] = near[0:1]
            continue
        ids = sub + (first_block + row * NBD)
        read = (ids == cols_ref[1:2, :]) | (ids == cols_ref[2:3, :])
        read = jnp.where(read, 1.0, 0.0).astype(BF16)
        read = nt(jnp.ones((8, BS), BF16), read)
        read = jnp.where(read > 0.5, 1.0, 0.0).astype(BF16)
        rank = jnp.dot(read, before_matrix(), preferred_element_type=F32)
        lane_no = OFFSETS.index(2 - row)
        out_ref[row : row + 1, :] = rank[0:1].astype(I32) + (NBD + lane_no * CAP)


def gather_lists(order_ref, load_tile, out_refs):
    for lane_no, out_ref in enumerate(out_refs):

        def group(g, _, lane_no=lane_no, out_ref=out_ref):
            tiles = [load_tile(order_ref[lane_no, 4 * g + m]) for m in range(4)]
            rows = pl.ds(pl.multiple_of(48 * g, 16), 48)
            out_ref[rows, :] = pack4(tiles).astype(BF16)
            return 0

        lax.fori_loop(0, CAP // 4, group, 0, unroll=4)


def first_kernel(sends_ref, tracers_ref, *rest):
    outs, local_ref, order_v, order_s, sem = rest[0:4], rest[4], rest[5], rest[6], rest[7]
    order_v[...] = jnp.zeros((8, BS), I32)
    for lane_no in range(4):
        order_v[lane_no : lane_no + 1, 0:CAP] = list_order(sends_ref, lane_no)
    copy = pltpu.make_async_copy(order_v, order_s, sem)
    copy.start()

    def local(b, _):
        lanes = pl.ds(pl.multiple_of(b * BS, BS), BS)
        local_ref[b] = tile16(tracers_ref[:, lanes])
        return 0

    lax.fori_loop(0, NBD, local, 0, unroll=8)
    copy.wait()

    def load_tile(i):
        return tracers_ref[:, pl.ds(pl.multiple_of(i * BS, BS), BS)]

    gather_lists(order_s, load_tile, outs)


def index_kernel(ecols_ref, icols_ref, isends_ref, espots_ref, ispots_ref, order_ref):
    first_block = (lax.axis_index("blk") - 2) * NBD
    espots_ref[...] = jnp.zeros((8, BS), I32)
    ispots_ref[...] = jnp.zeros((8, BS), I32)
    order_ref[...] = jnp.zeros((8, BS), I32)
    table_spots(ecols_ref, espots_ref, first_block)
    table_spots(icols_ref, ispots_ref, first_block)
    for lane_no in range(4):
        order_ref[lane_no : lane_no + 1, 0:CAP] = list_order(isends_ref, lane_no)


CHUNK = 8


def start_chunks(blocks_ref, held_ref, sems, first_slot, slots, order):
    copies = {}
    for c in order:
        copies[c] = pltpu.make_async_copy(
            blocks_ref.at[pl.ds(c * CHUNK, CHUNK), pl.ds(first_slot, slots)],
            held_ref.at[pl.ds(c * CHUNK, CHUNK)],
            sems.at[c],
        )
        copies[c].start()
    return copies


def local_kernel(cols_ref, table_ref, blocks_ref, out_ref, held_ref, sems):
    base = lax.axis_index("blk") * NBD
    chunks = NBD // CHUNK
    copies = start_chunks(blocks_ref, held_ref, sems, 0, 1, range(chunks))

    for c in range(chunks):
        copies[c].wait()

        def group(g, _):
            tiles = []
            for m in range(4):
                b = 4 * g + m
                tiles.append(nt(table_ref[cols_ref[0, b] - base], held_ref[b, 0]))
            out_ref[pl.ds(pl.multiple_of(48 * g, 16), 48), :] = pack4(tiles)
            return 0

        lax.fori_loop(c * CHUNK // 4, (c + 1) * CHUNK // 4, group, 0, unroll=True)


def remote_kernel(cols_ref, spots_ref, local_ref, blocks_ref, p0, p1, p2, p3,
                  own_ref, o1, o2, o3, held_ref, table_ref, sems):
    me = lax.axis_index("rep")
    first_block = (lax.axis_index("blk") - 2) * NBD
    per_share = SHARE // CHUNK
    copies = []
    for step in (2, 1, 3, 0):
        share = lax.rem(me + step, REP)
        for part in range(per_share):
            b0 = (share * per_share + part) * CHUNK
            slot = len(copies)
            copies.append(pltpu.make_async_copy(
                blocks_ref.at[pl.ds(b0, CHUNK), pl.ds(1, 2)],
                held_ref.at[pl.ds(slot * CHUNK, CHUNK)],
                sems.at[slot],
            ))
            copies[-1].start()

    for lane_no, piece in enumerate((p0, p1, p2, p3)):

        def spread(g, _, lane_no=lane_no, piece=piece):
            rows = piece[pl.ds(pl.multiple_of(48 * g, 16), 48), :].astype(F32)
            for m, tile in enumerate(unpack4(rows)):
                table_ref[lane_no * CAP + 4 * g + m] = tile16(tile)
            return 0

        lax.fori_loop(0, CAP // 4, spread, 0, unroll=4)

    def spot(k, b):
        c = cols_ref[k, b] - first_block
        return spots_ref[lax.shift_right_logical(c, 7), c & (NBD - 1)] - NBD

    slot = 0
    for step, out_ref in ((2, o2), (1, o1), (3, o3), (0, own_ref)):
        share = lax.rem(me + step, REP)
        for part in range(per_share):
            copies[slot].wait()

            def group(g, _, part=part, slot=slot, out_ref=out_ref, share=share):
                tiles = []
                for m in range(4):
                    row = 4 * g + m
                    b = share * SHARE + part * CHUNK + row
                    x = jnp.concatenate([table_ref[spot(1, b)], table_ref[spot(2, b)]], axis=1)
                    h = slot * CHUNK + row
                    w = jnp.concatenate([held_ref[h, 0], held_ref[h, 1]], axis=1)
                    tiles.append(nt(x, w))
                at = part * (CHUNK // 4) + g
                there = pl.ds(pl.multiple_of((share * (SHARE // 4) + at) * 48, 16), 48)
                total = pack4(tiles) + local_ref[there, :]
                out_ref[pl.ds(pl.multiple_of(48 * at, 16), 48), :] = total.astype(out_ref.dtype)
                return 0

            lax.fori_loop(0, CHUNK // 4, group, 0, unroll=True)
            slot += 1


def middle_kernel(own_ref, g1, g2, g3, tracers_ref, coupling_ref, wet_ref,
                  before_ref, packed_ref, tr_ref, wet_v, mid_ref, sems):
    me = lax.axis_index("rep")
    cells = SHARE * BS
    c1 = pltpu.make_async_copy(
        tracers_ref.at[:, pl.ds(pl.multiple_of(me * cells, cells), cells)], tr_ref, sems.at[0])
    c1.start()
    c2 = pltpu.make_async_copy(
        wet_ref.at[pl.ds(pl.multiple_of(me * SHARE, SHARE), SHARE)], wet_v, sems.at[1])
    c2.start()
    c1.wait()
    c2.wait()
    mid_ref[NTR:16, :] = jnp.zeros((16 - NTR, cells), F32)
    for g in range(SHARE // 4):
        rows = pl.ds(48 * g, 48)
        total = own_ref[rows, :] + g1[rows, :].astype(F32) + g2[rows, :].astype(F32) + g3[rows, :].astype(F32)
        for m, tile in enumerate(unpack4(total)):
            lanes = pl.ds((4 * g + m) * BS, BS)
            mid_ref[0:NTR, lanes] = tr_ref[:, lanes] + tile
    pushed = lax.dot_general(coupling_ref[...], mid_ref[...], (((1,), (0,)), ((), ())),
                             precision=lax.Precision.HIGHEST, preferred_element_type=F32)
    for g in range(SHARE // 4):
        tiles = []
        for m in range(4):
            b = 4 * g + m
            lanes = pl.ds(b * BS, BS)
            wet = wet_v[b : b + 1, :].astype(F32)
            tile = mid_ref[0:NTR, lanes] + wet * jnp.tanh(pushed[0:NTR, b * BS : (b + 1) * BS])
            before_ref[:, lanes] = tile
            tiles.append(tile)
        packed_ref[pl.ds(48 * g, 48), :] = pack4(tiles).astype(BF16)


def second_kernel(order_ref, own, g1, g2, g3, *rest):
    outs, table_ref = rest[0:4], rest[4]
    me = lax.axis_index("rep")
    for step, packed in enumerate((own, g1, g2, g3)):
        share = lax.rem(me - step + REP, REP)

        def spread(g, _, packed=packed, share=share):
            rows = packed[pl.ds(pl.multiple_of(48 * g, 16), 48), :].astype(F32)
            for m, tile in enumerate(unpack4(rows)):
                table_ref[share * SHARE + 4 * g + m] = tile16(tile)
            return 0

        lax.fori_loop(0, SHARE // 4, spread, 0, unroll=4)
    gather_lists(order_ref, lambda i: table_ref[i].astype(F32), outs)


def last_kernel(own_ref, g1, g2, g3, before_ref, wet_ref, out_ref, wet_v, sem):
    me = lax.axis_index("rep")
    copy = pltpu.make_async_copy(
        wet_ref.at[pl.ds(pl.multiple_of(me * SHARE, SHARE), SHARE)], wet_v, sem)
    copy.start()
    copy.wait()
    for g in range(SHARE // 4):
        rows = pl.ds(48 * g, 48)
        total = own_ref[rows, :] + g1[rows, :].astype(F32) + g2[rows, :].astype(F32) + g3[rows, :].astype(F32)
        for m, tile in enumerate(unpack4(total)):
            b = 4 * g + m
            lanes = pl.ds(b * BS, BS)
            wet = wet_v[b : b + 1, :].astype(F32)
            out_ref[:, lanes] = wet * (before_ref[:, lanes] + tile)


def sds(shape, dtype):
    return jax.ShapeDtypeStruct(shape, dtype)


def call(body, outs, in_specs, scratch, name, mib, flops=0, bytes_accessed=0):
    return pl.pallas_call(
        body,
        out_shape=outs,
        in_specs=in_specs,
        out_specs=jax.tree.map(lambda _: VMEM, outs),
        scratch_shapes=scratch,
        compiler_params=pltpu.CompilerParams(vmem_limit_bytes=mib * MIB),
        cost_estimate=pl.CostEstimate(flops=flops, bytes_accessed=bytes_accessed, transcendentals=0),
        name=name,
    )


def shift_blk(x, distance):
    n = lax.axis_size("blk")
    return lax.ppermute(x, "blk", [(i - distance, i) for i in range(n) if 0 <= i - distance < n])


def shift_rep(x, distance):
    n = lax.axis_size("rep")
    return lax.ppermute(x, "rep", [(i, (i + distance) % n) for i in range(n)])


def lists_out():
    return [sds((LIST_ROWS, BS), BF16)] * 4


def products(cols, spots, table, blocks, pieces):
    local = call(
        local_kernel, sds((NBD * NTR, BS), F32), [SMEM, VMEM, ANY],
        [pltpu.VMEM((NBD, 1, BS, BS), BF16), pltpu.SemaphoreType.DMA((NBD // CHUNK,))],
        "local_product", 16, flops=50_000_000, bytes_accessed=5_000_000,
    )(cols, table, blocks)
    share = sds((SHARE_ROWS, BS), BF16)
    return call(
        remote_kernel, [sds((SHARE_ROWS, BS), F32), share, share, share],
        [SMEM, SMEM, VMEM, ANY, VMEM, VMEM, VMEM, VMEM],
        [pltpu.VMEM((NBD, 2, BS, BS), BF16), pltpu.VMEM((4 * CAP, 16, BS), BF16),
         pltpu.SemaphoreType.DMA((NBD // CHUNK,))],
        "remote_product", 24, flops=100_000_000, bytes_accessed=10_000_000,
    )(cols, spots, local, blocks, *pieces)


def on_device(tracers, explicit_blocks, explicit_cols, explicit_sends,
              implicit_blocks, implicit_cols, implicit_sends, coupling, wet):
    ecols, icols = explicit_cols.T, implicit_cols.T
    esends, isends = explicit_sends.reshape(4, CAP), implicit_sends.reshape(4, CAP)
    wet = wet.reshape(NBD, BS)
    coupling = jnp.pad(coupling, ((0, 4), (0, 4)))
    cells = SHARE * BS

    *outbound, table = call(
        first_kernel, lists_out() + [sds((NBD, 16, BS), BF16)], [VMEM, VMEM],
        [pltpu.VMEM((8, BS), I32), pltpu.SMEM((8, BS), I32), pltpu.SemaphoreType.DMA],
        "first_lists", 16,
    )(esends, tracers)
    espots, ispots, iorder = call(
        index_kernel, [sds((8, BS), I32)] * 3, [VMEM, VMEM, VMEM], [], "indices", 8,
    )(ecols, icols, isends)
    pieces = [shift_blk(x, o) for x, o in zip(outbound, OFFSETS)]
    own, *parts = products(ecols, espots, table, explicit_blocks, pieces)
    got = [shift_rep(x, k + 1) for k, x in enumerate(parts)]
    before, packed = call(
        middle_kernel, [sds((NTR, cells), F32), sds((SHARE_ROWS, BS), BF16)],
        [VMEM, VMEM, VMEM, VMEM, ANY, VMEM, ANY],
        [pltpu.VMEM((NTR, cells), F32), pltpu.VMEM((SHARE, BS), I32),
         pltpu.VMEM((16, cells), F32), pltpu.SemaphoreType.DMA((2,))],
        "middle", 16,
    )(own, *got, tracers, coupling, wet)
    others = [shift_rep(packed, k) for k in (1, 2, 3)]
    *outbound, table = call(
        second_kernel, lists_out() + [sds((NBD, 16, BS), BF16)], [SMEM] + [VMEM] * 4, [],
        "second_lists", 16,
    )(iorder, packed, *others)
    pieces = [shift_blk(x, o) for x, o in zip(outbound, OFFSETS)]
    own, *parts = products(icols, ispots, table, implicit_blocks, pieces)
    got = [shift_rep(x, k + 1) for k, x in enumerate(parts)]
    return call(
        last_kernel, sds((NTR, cells), F32), [VMEM] * 5 + [ANY],
        [pltpu.VMEM((SHARE, BS), I32), pltpu.SemaphoreType.DMA], "last", 16,
    )(own, *got, before, wet)


def solution(mesh):
    in_specs = (
        P(None, "blk"),
        P("blk", "rep", None, None),
        P("blk", "rep"),
        P("blk", "rep", None, None),
        P("blk", "rep", None, None),
        P("blk", "rep"),
        P("blk", "rep", None, None),
        P(),
        P("blk"),
    )
    out_specs = P(None, ("blk", "rep"))
    return jax.shard_map(
        on_device, mesh=mesh, in_specs=in_specs, out_specs=out_specs, check_vma=False
    )
```

time: 208 us -> 95 us (0.46)
  waiting for transfers between devices: 86.7 us -> 17.3 us
  Pallas kernels: 0 us -> 28.7 us
  other arithmetic: 23.4 us -> 0 us
  matrix products: 18.6 us -> 0 us
  between operations: 14.1 us -> 0.43 us
  local copies, waits for them, and re-layouts: 19.3 us -> 9.26 us
  starting transfers between devices: 44.5 us -> 38.9 us
    psum x1 -> x0, waiting for transfers between devices: 48.2 us -> none  [on_device(): explicit_sum = lax.psum(explicit_part, 'rep')]
    pallas_call x0 -> x9, Pallas kernels: none -> 28.7 us  [the longest x2 11.4 us: products(): call(remote_kernel, [sds((SHARE_ROWS, BS), F32), share, share, share], [S...]
    reduce_scatter x1 -> x0, waiting for transfers between devices: 21.9 us -> none  [on_device(): lax.psum_scatter(implicit_part, 'rep', scatter_dimension=1, tiled=True)]
    dot_general x3 -> x0, matrix products: 18.6 us -> none  [the longest x2 14.7 us: incoming(): jnp.einsum('bkij,tbkj->tbi', blocks, picked, preferred_element_type=jnp.f...]
    select_n x18 -> x0, other arithmetic: 10.6 us -> none  [the longest x8 4.98 us: incoming(): jnp.where(labels[lane_no] > 0, owner_base + labels[lane_no] - 1, -1)]
    gather x10 -> x0, local copies, waits for them, and re-layouts: 9.38 us -> none  [the longest x8 5.55 us: outgoing(): jnp.take(planes, jnp.maximum(send_rows[lane_no], 0), axis=1)]
    ppermute x16 -> x17, starting transfers between devices: 44.5 us -> 38.9 us  [the longest x8 24.7 us: shift_blk(): lax.ppermute(x, 'blk', [(i - distance, i) for i in range(n) if 0 <= i - d...]
    and x4 -> x0, other arithmetic: 3.33 us -> none  [the longest x2 2.03 us: outgoing(): jnp.take(planes, jnp.maximum(send_rows[lane_no], 0), axis=1)]
  transfers between devices with their start and end apart: 18 -> 17, of which waited for: 7 -> 8; matrix products, arithmetic and copies ran while one was open for 19% -> 0% of each run, Pallas kernels for 0% -> 13%
where the time goes in v1:
time: 95 us; the launch traced here: 94.6 us
  starting transfers between devices  38.9 us (41%)
  Pallas kernels  28.7 us (30%)
  waiting for transfers between devices  17.3 us (18%)
  local copies, waits for them, and re-layouts  9.26 us (10%)
    ppermute x8, starting transfers between devices, shift_blk(): lax.ppermute(x, 'blk', [(i - distance, i) for i in range(n) if 0 <= i - d...  24.7 us
    ppermute x9, starting transfers between devices, shift_rep(): return lax.ppermute(x, 'rep', [(i, (i + distance) % n) for i in range(n)])  14.1 us
    ppermute x9, waiting for transfers between devices, shift_rep(): return lax.ppermute(x, 'rep', [(i, (i + distance) % n) for i in range(n)])  13.6 us
    pallas_call x2, Pallas kernels, products(): call(remote_kernel, [sds((SHARE_ROWS, BS), F32), share, share, share], [S...  11.4 us
    pallas_call x2, Pallas kernels, products(): call(local_kernel, sds((NBD * NTR, BS), F32), [SMEM, VMEM, ANY], [pltpu.V...  10.2 us
    unnamed x28, local copies, waits for them, and re-layouts  9.26 us
    ppermute x8, waiting for transfers between devices, shift_blk(): lax.ppermute(x, 'blk', [(i - distance, i) for i in range(n) if 0 <= i - d...  3.67 us
    pallas_call x1, Pallas kernels, on_device(): call(first_kernel, lists_out() + [sds((NBD, 16, BS), BF16)], [VMEM, VMEM]...  2.33 us
  transfers between devices with their start and end apart: 17, of which 8 were waited for; matrix products, arithmetic and copies ran while one was open for 0% of the time, Pallas kernels for 13%

profile of v1, /device:TPU:6, one launch (start us, length us, event | category | flops | bytes accessed | tf_op | source)
XLA Modules:
  0.0 94.6 jit_solution(11579219693183268257)
XLA Ops:
  0.0 1.2 %copy-done.3 = f32[12,16384]{1,0:T(8,128)S(1)} copy-done((f32[12,16384]{1,0:T(8,128)S(1)}, f32[12,16384]{1,0:T(8,128)}, u32[]{:S(2)}) %copy-start.3) | copy-done | bytes 786456
  1.2 0.7 copy-done.11
  1.9 2.3 %first_lists.1 = (bf16[768,128]{1,0:T(8,128)(2,1)S(1)}, bf16[768,128]{1,0:T(8,128)(2,1)S(1)}, bf16[768,128]{1,0:T(8,128)(2,1)S(1)}, bf16[768,128]{1,0:T(8,128)(2,1)S(1)}, bf16[128,16,128]{2,1,0:T(8,128)(2,1)S(1)}) custom-call(s32[4,64]{1,0:T(4,128)S(1)} %bitcast.13, f32[12,16384]{1,0:T(8,128)S(1)} %copy-done.3), custom_call_target="tpu_custom_call" | custom-call | tf_op jit(solution)/shard_map/first_lists/pallas_call | solution.py:345
  4.2 5.2 %collective-permute-start = (bf16[768,128]{1,0:T(8,128)(2,1)S(1)}, bf16[768,128]{1,0:T(8,128)(2,1)S(1)}, u32[]{:S(2)}, u32[]{:S(2)}) collective-permute-start(bf16[768,128]{1,0:T(8,128)(2,1)S(1)} %get-tuple-element.32), channel_id=1, source_target_pairs={{8,0},{12,4},{16,8},{20,12},{24,16},{28,20},{32,24},{36,28},{40,32... | collective-permute-start | bytes 589832 | tf_op jit(solution)/shard_map/ppermute | solution.py:309
  9.4 1.9 %collective-permute-start.1 = (bf16[768,128]{1,0:T(8,128)(2,1)S(1)}, bf16[768,128]{1,0:T(8,128)(2,1)S(1)}, u32[]{:S(2)}, u32[]{:S(2)}) collective-permute-start(bf16[768,128]{1,0:T(8,128)(2,1)S(1)} %get-tuple-element.33), channel_id=1, source_target_pairs={{4,0},{8,4},{12,8},{16,12},{20,16},{24,20},{28,24},{32,28},{36,32}... | collective-permute-start | bytes 589832 | tf_op jit(solution)/shard_map/ppermute | solution.py:309
  11.4 2.4 %collective-permute-start.2 = (bf16[768,128]{1,0:T(8,128)(2,1)S(1)}, bf16[768,128]{1,0:T(8,128)(2,1)S(1)}, u32[]{:S(2)}, u32[]{:S(2)}) collective-permute-start(bf16[768,128]{1,0:T(8,128)(2,1)S(1)} %get-tuple-element.34), channel_id=1, source_target_pairs={{0,4},{4,8},{8,12},{12,16},{16,20},{20,24},{24,28},{28,32},{32,36}... | collective-permute-start | bytes 589832 | tf_op jit(solution)/shard_map/ppermute | solution.py:309
  13.8 2.6 %collective-permute-start.3 = (bf16[768,128]{1,0:T(8,128)(2,1)S(1)}, bf16[768,128]{1,0:T(8,128)(2,1)S(1)}, u32[]{:S(2)}, u32[]{:S(2)}) collective-permute-start(bf16[768,128]{1,0:T(8,128)(2,1)S(1)} %get-tuple-element.35), channel_id=1, source_target_pairs={{0,8},{4,12},{8,16},{12,20},{16,24},{20,28},{24,32},{28,36},{32,40... | collective-permute-start | bytes 589832 | tf_op jit(solution)/shard_map/ppermute | solution.py:309
  16.4 0.0 copy-start.6
  16.4 0.7 copy-done.6
  17.1 0.7 copy-done.9
  17.8 0.7 copy-done.12
  18.4 2.0 %indices.1 = (s32[8,128]{1,0:T(8,128)S(1)}, s32[8,128]{1,0:T(8,128)S(1)}, s32[8,128]{1,0:T(8,128)S(1)}) custom-call(s32[3,128]{1,0:T(4,128)S(1)} %bitcast.7, s32[3,128]{1,0:T(4,128)S(1)} %bitcast.10, s32[4,64]{1,0:T(4,128)S(1)} %bitcast.14), custom_call_target="tpu_custom_call" | custom-call | tf_op jit(solution)/shard_map/indices/pallas_call | solution.py:350
  20.5 4.6 %copy-done = bf16[128,3,128,128]{3,2,1,0:T(8,128)(2,1)S(1)} copy-done((bf16[128,3,128,128]{3,2,1,0:T(8,128)(2,1)S(1)}, bf16[128,3,128,128]{3,2,1,0:T(8,128)(2,1)}, u32[]{:S(2)}) %copy-start) | copy-done | bytes 12582936
  25.1 0.7 copy-done.7
  25.7 0.0 copy-start.2
  25.8 0.0 copy-start.10
  25.8 5.1 %local_product.2.local_ref = f32[1536,128]{1,0:T(8,128)S(1)} custom-call(s32[3,128]{1,0:T(4,128)S(1)} %bitcast.8, bf16[128,16,128]{2,1,0:T(8,128)(2,1)S(1)} %get-tuple-element.31.table_ref, bf16[128,3,128,128]{3,2,1,0:T(8,128)(2,1)S(1)} %copy-done), custom_call_target="tpu_custom_call" | custom-call | flops 50000000 | bytes 5000000 | tf_op jit(solution)/shard_map/local_product/pallas_call | solution.py:322
  30.9 0.0 collective-permute-done.p0
  30.9 0.0 collective-permute-done.2.p2
  30.9 0.0 collective-permute-done.3.p3
  30.9 5.7 %remote_product.2 = (f32[384,128]{1,0:T(8,128)S(1)}, bf16[384,128]{1,0:T(8,128)(2,1)S(1)}, bf16[384,128]{1,0:T(8,128)(2,1)S(1)}, bf16[384,128]{1,0:T(8,128)(2,1)S(1)}) custom-call(s32[3,128]{1,0:T(4,128)S(1)} %bitcast.9, s32[8,128]{1,0:T(8,128)S(1)} %get-tuple-element.30.spots_ref, f32[1536,128]{1,0:T(8,128)S(1)} %local_product.2.local_ref, ...), custom_call_target="tpu_custom_call" | custom-call | flops 100000000 | bytes 10000000 | tf_op jit(solution)/shard_map/remote_product/pallas_call | solution.py:328
  36.6 2.0 %collective-permute-start.4 = (bf16[384,128]{1,0:T(8,128)(2,1)S(1)}, bf16[384,128]{1,0:T(8,128)(2,1)S(1)}, u32[]{:S(2)}, u32[]{:S(2)}) collective-permute-start(bf16[384,128]{1,0:T(8,128)(2,1)S(1)} %get-tuple-element.37), channel_id=1, source_target_pairs={{0,1},{1,2},{2,3},{3,0},{4,5},{5,6},{6,7},{7,4},{8,9},{9,10},{10,1... | collective-permute-start | bytes 294920 | tf_op jit(solution)/shard_map/ppermute | solution.py:314
  38.6 3.6 %collective-permute-start.5 = (bf16[384,128]{1,0:T(8,128)(2,1)S(1)}, bf16[384,128]{1,0:T(8,128)(2,1)S(1)}, u32[]{:S(2)}, u32[]{:S(2)}) collective-permute-start(bf16[384,128]{1,0:T(8,128)(2,1)S(1)} %get-tuple-element.38), channel_id=1, source_target_pairs={{0,2},{1,3},{2,0},{3,1},{4,6},{5,7},{6,4},{7,5},{8,10},{9,11},{10,... | collective-permute-start | bytes 294920 | tf_op jit(solution)/shard_map/ppermute | solution.py:314
  42.2 1.0 %collective-permute-start.6 = (bf16[384,128]{1,0:T(8,128)(2,1)S(1)}, bf16[384,128]{1,0:T(8,128)(2,1)S(1)}, u32[]{:S(2)}, u32[]{:S(2)}) collective-permute-start(bf16[384,128]{1,0:T(8,128)(2,1)S(1)} %get-tuple-element.39), channel_id=1, source_target_pairs={{0,3},{1,0},{2,1},{3,2},{4,7},{5,4},{6,5},{7,6},{8,11},{9,8},{10,9... | collective-permute-start | bytes 294920 | tf_op jit(solution)/shard_map/ppermute | solution.py:314
  43.2 0.6 collective-permute-done.4.g1
  43.8 3.3 %collective-permute-done.5.g2 = bf16[384,128]{1,0:T(8,128)(2,1)S(1)} collective-permute-done((bf16[384,128]{1,0:T(8,128)(2,1)S(1)}, bf16[384,128]{1,0:T(8,128)(2,1)S(1)}, u32[]{:S(2)}, u32[]{:S(2)}) %collective-permute-start.5) | collective-permute-done | bytes 98336 | tf_op jit(solution)/shard_map/ppermute | solution.py:314
  47.1 0.0 collective-permute-done.6.g3
  47.1 0.5 middle.1
  47.6 2.2 %collective-permute-start.9 = (bf16[384,128]{1,0:T(8,128)(2,1)S(1)}, bf16[384,128]{1,0:T(8,128)(2,1)S(1)}, u32[]{:S(2)}, u32[]{:S(2)}) collective-permute-start(bf16[384,128]{1,0:T(8,128)(2,1)S(1)} %get-tuple-element.40.own), channel_id=1, source_target_pairs={{0,3},{1,0},{2,1},{3,2},{4,7},{5,4},{6,5},{7,6},{8,11},{9,8},{10,9... | collective-permute-start | bytes 294920 | tf_op jit(solution)/shard_map/ppermute | solution.py:314
  49.9 1.1 %collective-permute-start.8 = (bf16[384,128]{1,0:T(8,128)(2,1)S(1)}, bf16[384,128]{1,0:T(8,128)(2,1)S(1)}, u32[]{:S(2)}, u32[]{:S(2)}) collective-permute-start(bf16[384,128]{1,0:T(8,128)(2,1)S(1)} %get-tuple-element.40.own), channel_id=1, source_target_pairs={{0,2},{1,3},{2,0},{3,1},{4,6},{5,7},{6,4},{7,5},{8,10},{9,11},{10,... | collective-permute-start | bytes 294920 | tf_op jit(solution)/shard_map/ppermute | solution.py:314
  51.0 0.4 collective-permute-start.7
  51.4 2.1 %collective-permute-done.9.g3 = bf16[384,128]{1,0:T(8,128)(2,1)S(1)} collective-permute-done((bf16[384,128]{1,0:T(8,128)(2,1)S(1)}, bf16[384,128]{1,0:T(8,128)(2,1)S(1)}, u32[]{:S(2)}, u32[]{:S(2)}) %collective-permute-start.9) | collective-permute-done | bytes 98336 | tf_op jit(solution)/shard_map/ppermute | solution.py:314
  53.4 2.6 %collective-permute-done.8.g2 = bf16[384,128]{1,0:T(8,128)(2,1)S(1)} collective-permute-done((bf16[384,128]{1,0:T(8,128)(2,1)S(1)}, bf16[384,128]{1,0:T(8,128)(2,1)S(1)}, u32[]{:S(2)}, u32[]{:S(2)}) %collective-permute-start.8) | collective-permute-done | bytes 98336 | tf_op jit(solution)/shard_map/ppermute | solution.py:314
  56.1 1.0 %collective-permute-done.7.g1 = bf16[384,128]{1,0:T(8,128)(2,1)S(1)} collective-permute-done((bf16[384,128]{1,0:T(8,128)(2,1)S(1)}, bf16[384,128]{1,0:T(8,128)(2,1)S(1)}, u32[]{:S(2)}, u32[]{:S(2)}) %collective-permute-start.7) | collective-permute-done | bytes 98336 | tf_op jit(solution)/shard_map/ppermute | solution.py:314
  57.1 1.5 %second_lists.1 = (bf16[768,128]{1,0:T(8,128)(2,1)S(1)}, bf16[768,128]{1,0:T(8,128)(2,1)S(1)}, bf16[768,128]{1,0:T(8,128)(2,1)S(1)}, bf16[768,128]{1,0:T(8,128)(2,1)S(1)}, bf16[128,16,128]{2,1,0:T(8,128)(2,1)S(1)}) custom-call(s32[8,128]{1,0:T(8,128)S(1)} %get-tuple-element.29.order_ref, bf16[384,128]{1,0:T(8,128)(2,1)S(1)} %get-tuple-element.40.own, ...), custom_call_target="tpu_custom_call" | custom-call | tf_op jit(solution)/shard_map/second_lists/pallas_call | solution.py:364
  58.6 6.2 %collective-permute-start.10 = (bf16[768,128]{1,0:T(8,128)(2,1)S(1)}, bf16[768,128]{1,0:T(8,128)(2,1)S(1)}, u32[]{:S(2)}, u32[]{:S(2)}) collective-permute-start(bf16[768,128]{1,0:T(8,128)(2,1)S(1)} %get-tuple-element.42), channel_id=1, source_target_pairs={{8,0},{12,4},{16,8},{20,12},{24,16},{28,20},{32,24},{36,28},{40,32... | collective-permute-start | bytes 589832 | tf_op jit(solution)/shard_map/ppermute | solution.py:309
  64.8 1.9 %collective-permute-start.11 = (bf16[768,128]{1,0:T(8,128)(2,1)S(1)}, bf16[768,128]{1,0:T(8,128)(2,1)S(1)}, u32[]{:S(2)}, u32[]{:S(2)}) collective-permute-start(bf16[768,128]{1,0:T(8,128)(2,1)S(1)} %get-tuple-element.43), channel_id=1, source_target_pairs={{4,0},{8,4},{12,8},{16,12},{20,16},{24,20},{28,24},{32,28},{36,32}... | collective-permute-start | bytes 589832 | tf_op jit(solution)/shard_map/ppermute | solution.py:309
  66.7 2.4 %collective-permute-start.12 = (bf16[768,128]{1,0:T(8,128)(2,1)S(1)}, bf16[768,128]{1,0:T(8,128)(2,1)S(1)}, u32[]{:S(2)}, u32[]{:S(2)}) collective-permute-start(bf16[768,128]{1,0:T(8,128)(2,1)S(1)} %get-tuple-element.44), channel_id=1, source_target_pairs={{0,4},{4,8},{8,12},{12,16},{16,20},{20,24},{24,28},{28,32},{32,36}... | collective-permute-start | bytes 589832 | tf_op jit(solution)/shard_map/ppermute | solution.py:309
  69.1 2.1 %collective-permute-start.13 = (bf16[768,128]{1,0:T(8,128)(2,1)S(1)}, bf16[768,128]{1,0:T(8,128)(2,1)S(1)}, u32[]{:S(2)}, u32[]{:S(2)}) collective-permute-start(bf16[768,128]{1,0:T(8,128)(2,1)S(1)} %get-tuple-element.45), channel_id=1, source_target_pairs={{0,8},{4,12},{8,16},{12,20},{16,24},{20,28},{24,32},{28,36},{32,40... | collective-permute-start | bytes 589832 | tf_op jit(solution)/shard_map/ppermute | solution.py:309
  71.3 5.1 %local_product.3.local_ref = f32[1536,128]{1,0:T(8,128)S(1)} custom-call(s32[3,128]{1,0:T(4,128)S(1)} %bitcast.11, bf16[128,16,128]{2,1,0:T(8,128)(2,1)S(1)} %get-tuple-element.41.table_ref, bf16[128,3,128,128]{3,2,1,0:T(8,128)(2,1)S(1)} %copy-done.2), custom_call_target="tpu_custom_call" | custom-call | flops 50000000 | bytes 5000000 | tf_op jit(solution)/shard_map/local_product/pallas_call | solution.py:322
  76.4 3.7 %collective-permute-done.13.p3 = bf16[768,128]{1,0:T(8,128)(2,1)S(1)} collective-permute-done((bf16[768,128]{1,0:T(8,128)(2,1)S(1)}, bf16[768,128]{1,0:T(8,128)(2,1)S(1)}, u32[]{:S(2)}, u32[]{:S(2)}) %collective-permute-start.13) | collective-permute-done | bytes 196640 | tf_op jit(solution)/shard_map/ppermute | solution.py:309
  80.0 5.7 %remote_product.3 = (f32[384,128]{1,0:T(8,128)S(1)}, bf16[384,128]{1,0:T(8,128)(2,1)S(1)}, bf16[384,128]{1,0:T(8,128)(2,1)S(1)}, bf16[384,128]{1,0:T(8,128)(2,1)S(1)}) custom-call(s32[3,128]{1,0:T(4,128)S(1)} %bitcast.12, s32[8,128]{1,0:T(8,128)S(1)} %get-tuple-element.28.spots_ref, f32[1536,128]{1,0:T(8,128)S(1)} %local_product.3.local_ref, ...), custom_call_target="tpu_custom_call" | custom-call | flops 100000000 | bytes 10000000 | tf_op jit(solution)/shard_map/remote_product/pallas_call | solution.py:328
  85.7 0.1 collective-permute-start.14
  85.8 2.0 %collective-permute-start.15 = (bf16[384,128]{1,0:T(8,128)(2,1)S(1)}, bf16[384,128]{1,0:T(8,128)(2,1)S(1)}, u32[]{:S(2)}, u32[]{:S(2)}) collective-permute-start(bf16[384,128]{1,0:T(8,128)(2,1)S(1)} %get-tuple-element.48), channel_id=1, source_target_pairs={{0,2},{1,3},{2,0},{3,1},{4,6},{5,7},{6,4},{7,5},{8,10},{9,11},{10,... | collective-permute-start | bytes 294920 | tf_op jit(solution)/shard_map/ppermute | solution.py:314
  87.8 1.8 %collective-permute-start.16 = (bf16[384,128]{1,0:T(8,128)(2,1)S(1)}, bf16[384,128]{1,0:T(8,128)(2,1)S(1)}, u32[]{:S(2)}, u32[]{:S(2)}) collective-permute-start(bf16[384,128]{1,0:T(8,128)(2,1)S(1)} %get-tuple-element.49), channel_id=1, source_target_pairs={{0,3},{1,0},{2,1},{3,2},{4,7},{5,4},{6,5},{7,6},{8,11},{9,8},{10,9... | collective-permute-start | bytes 294920 | tf_op jit(solution)/shard_map/ppermute | solution.py:314
  89.6 3.4 %collective-permute-done.14.g1 = bf16[384,128]{1,0:T(8,128)(2,1)S(1)} collective-permute-done((bf16[384,128]{1,0:T(8,128)(2,1)S(1)}, bf16[384,128]{1,0:T(8,128)(2,1)S(1)}, u32[]{:S(2)}, u32[]{:S(2)}) %collective-permute-start.14) | collective-permute-done | bytes 98336 | tf_op jit(solution)/shard_map/ppermute | solution.py:314
  93.0 0.6 collective-permute-done.16.g3
  93.6 0.8 last.1
  (24 shorter events, 0.1 us)
Async XLA Ops:
  0.0 1.2 %copy-start.3 = (f32[12,16384]{1,0:T(8,128)S(1)}, f32[12,16384]{1,0:T(8,128)}, u32[]{:S(2)}) copy-start(f32[12,16384]{1,0:T(8,128)} %tracers_ref.3) | copy-start | bytes 2359300
  1.2 0.7 copy-start.11
  1.9 29.0 %copy-start.8 = (s32[128,3]{0,1:T(4,128)S(1)}, s32[128,3]{0,1:T(4,128)}, u32[]{:S(2)}) copy-start(s32[128,3]{0,1:T(4,128)} %param.11) | copy-start | bytes 4612
  4.2 26.6 %collective-permute-start = (bf16[768,128]{1,0:T(8,128)(2,1)S(1)}, bf16[768,128]{1,0:T(8,128)(2,1)S(1)}, u32[]{:S(2)}, u32[]{:S(2)}) collective-permute-start(bf16[768,128]{1,0:T(8,128)(2,1)S(1)} %get-tuple-element.32), channel_id=1, source_target_pairs={{8,0},{12,4},{16,8},{20,12},{24,16},{28,20},{32,24},{36,28},{40,32... | collective-permute-start | bytes 589832 | tf_op jit(solution)/shard_map/ppermute | solution.py:309
  9.4 21.4 %collective-permute-start.1 = (bf16[768,128]{1,0:T(8,128)(2,1)S(1)}, bf16[768,128]{1,0:T(8,128)(2,1)S(1)}, u32[]{:S(2)}, u32[]{:S(2)}) collective-permute-start(bf16[768,128]{1,0:T(8,128)(2,1)S(1)} %get-tuple-element.33), channel_id=1, source_target_pairs={{4,0},{8,4},{12,8},{16,12},{20,16},{24,20},{28,24},{32,28},{36,32}... | collective-permute-start | bytes 589832 | tf_op jit(solution)/shard_map/ppermute | solution.py:309
  11.4 19.5 %collective-permute-start.2 = (bf16[768,128]{1,0:T(8,128)(2,1)S(1)}, bf16[768,128]{1,0:T(8,128)(2,1)S(1)}, u32[]{:S(2)}, u32[]{:S(2)}) collective-permute-start(bf16[768,128]{1,0:T(8,128)(2,1)S(1)} %get-tuple-element.34), channel_id=1, source_target_pairs={{0,4},{4,8},{8,12},{12,16},{16,20},{20,24},{24,28},{28,32},{32,36}... | collective-permute-start | bytes 589832 | tf_op jit(solution)/shard_map/ppermute | solution.py:309
  13.8 17.1 %collective-permute-start.3 = (bf16[768,128]{1,0:T(8,128)(2,1)S(1)}, bf16[768,128]{1,0:T(8,128)(2,1)S(1)}, u32[]{:S(2)}, u32[]{:S(2)}) collective-permute-start(bf16[768,128]{1,0:T(8,128)(2,1)S(1)} %get-tuple-element.35), channel_id=1, source_target_pairs={{0,8},{4,12},{8,16},{12,20},{16,24},{20,28},{24,32},{28,36},{32,40... | collective-permute-start | bytes 589832 | tf_op jit(solution)/shard_map/ppermute | solution.py:309
  16.4 0.7 copy-start.6
  17.1 0.7 copy-start.9
  17.8 0.7 copy-start.12
  20.5 4.6 %copy-start = (bf16[128,3,128,128]{3,2,1,0:T(8,128)(2,1)S(1)}, bf16[128,3,128,128]{3,2,1,0:T(8,128)(2,1)}, u32[]{:S(2)}) copy-start(bf16[128,3,128,128]{3,2,1,0:T(8,128)(2,1)} %blocks_ref.5) | copy-start | bytes 37748740
  25.1 0.7 copy-start.7
  25.7 5.2 %copy-start.1 = (bf16[128,3,128,128]{3,2,1,0:T(8,128)(2,1)S(1)}, bf16[128,3,128,128]{3,2,1,0:T(8,128)(2,1)}, u32[]{:S(2)}) copy-start(bf16[128,3,128,128]{3,2,1,0:T(8,128)(2,1)} %blocks_ref.5) | copy-start | bytes 37748740
  25.7 17.5 %copy-start.13 = (f32[12,12]{1,0:T(8,128)S(1)}, f32[12,12]{1,0:T(8,128)}, u32[]{:S(2)}) copy-start(f32[12,12]{1,0:T(8,128)} %param.16) | copy-start | bytes 1732
  25.7 21.4 %copy-start.4 = (f32[12,16384]{1,0:T(8,128)S(1)}, f32[12,16384]{1,0:T(8,128)}, u32[]{:S(2)}) copy-start(f32[12,16384]{1,0:T(8,128)} %tracers_ref.3) | copy-start | bytes 2359300
  25.7 21.4 %copy-start.5 = (s32[16384]{0:T(1024)S(1)}, s32[16384]{0:T(1024)}, u32[]{:S(2)}) copy-start(s32[16384]{0:T(1024)} %param.17) | copy-start | bytes 196612
  25.7 45.5 %copy-start.2 = (bf16[128,3,128,128]{3,2,1,0:T(8,128)(2,1)S(1)}, bf16[128,3,128,128]{3,2,1,0:T(8,128)(2,1)}, u32[]{:S(2)}) copy-start(bf16[128,3,128,128]{3,2,1,0:T(8,128)(2,1)} %blocks_ref.7) | copy-start | bytes 37748740
  25.8 45.5 %copy-start.10 = (s32[128,3]{0,1:T(4,128)S(1)}, s32[128,3]{0,1:T(4,128)}, u32[]{:S(2)}) copy-start(s32[128,3]{0,1:T(4,128)} %param.14) | copy-start | bytes 4612
  36.6 7.2 %collective-permute-start.4 = (bf16[384,128]{1,0:T(8,128)(2,1)S(1)}, bf16[384,128]{1,0:T(8,128)(2,1)S(1)}, u32[]{:S(2)}, u32[]{:S(2)}) collective-permute-start(bf16[384,128]{1,0:T(8,128)(2,1)S(1)} %get-tuple-element.37), channel_id=1, source_target_pairs={{0,1},{1,2},{2,3},{3,0},{4,5},{5,6},{6,7},{7,4},{8,9},{9,10},{10,1... | collective-permute-start | bytes 294920 | tf_op jit(solution)/shard_map/ppermute | solution.py:314
  38.6 8.5 %collective-permute-start.5 = (bf16[384,128]{1,0:T(8,128)(2,1)S(1)}, bf16[384,128]{1,0:T(8,128)(2,1)S(1)}, u32[]{:S(2)}, u32[]{:S(2)}) collective-permute-start(bf16[384,128]{1,0:T(8,128)(2,1)S(1)} %get-tuple-element.38), channel_id=1, source_target_pairs={{0,2},{1,3},{2,0},{3,1},{4,6},{5,7},{6,4},{7,5},{8,10},{9,11},{10,... | collective-permute-start | bytes 294920 | tf_op jit(solution)/shard_map/ppermute | solution.py:314
  42.2 4.9 %collective-permute-start.6 = (bf16[384,128]{1,0:T(8,128)(2,1)S(1)}, bf16[384,128]{1,0:T(8,128)(2,1)S(1)}, u32[]{:S(2)}, u32[]{:S(2)}) collective-permute-start(bf16[384,128]{1,0:T(8,128)(2,1)S(1)} %get-tuple-element.39), channel_id=1, source_target_pairs={{0,3},{1,0},{2,1},{3,2},{4,7},{5,4},{6,5},{7,6},{8,11},{9,8},{10,9... | collective-permute-start | bytes 294920 | tf_op jit(solution)/shard_map/ppermute | solution.py:314
  47.6 5.8 %collective-permute-start.9 = (bf16[384,128]{1,0:T(8,128)(2,1)S(1)}, bf16[384,128]{1,0:T(8,128)(2,1)S(1)}, u32[]{:S(2)}, u32[]{:S(2)}) collective-permute-start(bf16[384,128]{1,0:T(8,128)(2,1)S(1)} %get-tuple-element.40.own), channel_id=1, source_target_pairs={{0,3},{1,0},{2,1},{3,2},{4,7},{5,4},{6,5},{7,6},{8,11},{9,8},{10,9... | collective-permute-start | bytes 294920 | tf_op jit(solution)/shard_map/ppermute | solution.py:314
  49.9 6.2 %collective-permute-start.8 = (bf16[384,128]{1,0:T(8,128)(2,1)S(1)}, bf16[384,128]{1,0:T(8,128)(2,1)S(1)}, u32[]{:S(2)}, u32[]{:S(2)}) collective-permute-start(bf16[384,128]{1,0:T(8,128)(2,1)S(1)} %get-tuple-element.40.own), channel_id=1, source_target_pairs={{0,2},{1,3},{2,0},{3,1},{4,6},{5,7},{6,4},{7,5},{8,10},{9,11},{10,... | collective-permute-start | bytes 294920 | tf_op jit(solution)/shard_map/ppermute | solution.py:314
  51.0 6.1 %collective-permute-start.7 = (bf16[384,128]{1,0:T(8,128)(2,1)S(1)}, bf16[384,128]{1,0:T(8,128)(2,1)S(1)}, u32[]{:S(2)}, u32[]{:S(2)}) collective-permute-start(bf16[384,128]{1,0:T(8,128)(2,1)S(1)} %get-tuple-element.40.own), channel_id=1, source_target_pairs={{0,1},{1,2},{2,3},{3,0},{4,5},{5,6},{6,7},{7,4},{8,9},{9,10},{10,1... | collective-permute-start | bytes 294920 | tf_op jit(solution)/shard_map/ppermute | solution.py:314
  58.6 17.8 %collective-permute-start.10 = (bf16[768,128]{1,0:T(8,128)(2,1)S(1)}, bf16[768,128]{1,0:T(8,128)(2,1)S(1)}, u32[]{:S(2)}, u32[]{:S(2)}) collective-permute-start(bf16[768,128]{1,0:T(8,128)(2,1)S(1)} %get-tuple-element.42), channel_id=1, source_target_pairs={{8,0},{12,4},{16,8},{20,12},{24,16},{28,20},{32,24},{36,28},{40,32... | collective-permute-start | bytes 589832 | tf_op jit(solution)/shard_map/ppermute | solution.py:309
  64.8 11.6 %collective-permute-start.11 = (bf16[768,128]{1,0:T(8,128)(2,1)S(1)}, bf16[768,128]{1,0:T(8,128)(2,1)S(1)}, u32[]{:S(2)}, u32[]{:S(2)}) collective-permute-start(bf16[768,128]{1,0:T(8,128)(2,1)S(1)} %get-tuple-element.43), channel_id=1, source_target_pairs={{4,0},{8,4},{12,8},{16,12},{20,16},{24,20},{28,24},{32,28},{36,32}... | collective-permute-start | bytes 589832 | tf_op jit(solution)/shard_map/ppermute | solution.py:309
  66.7 9.6 %collective-permute-start.12 = (bf16[768,128]{1,0:T(8,128)(2,1)S(1)}, bf16[768,128]{1,0:T(8,128)(2,1)S(1)}, u32[]{:S(2)}, u32[]{:S(2)}) collective-permute-start(bf16[768,128]{1,0:T(8,128)(2,1)S(1)} %get-tuple-element.44), channel_id=1, source_target_pairs={{0,4},{4,8},{8,12},{12,16},{16,20},{20,24},{24,28},{28,32},{32,36}... | collective-permute-start | bytes 589832 | tf_op jit(solution)/shard_map/ppermute | solution.py:309
  69.1 10.9 %collective-permute-start.13 = (bf16[768,128]{1,0:T(8,128)(2,1)S(1)}, bf16[768,128]{1,0:T(8,128)(2,1)S(1)}, u32[]{:S(2)}, u32[]{:S(2)}) collective-permute-start(bf16[768,128]{1,0:T(8,128)(2,1)S(1)} %get-tuple-element.45), channel_id=1, source_target_pairs={{0,8},{4,12},{8,16},{12,20},{16,24},{20,28},{24,32},{28,36},{32,40... | collective-permute-start | bytes 589832 | tf_op jit(solution)/shard_map/ppermute | solution.py:309
  85.7 7.3 %collective-permute-start.14 = (bf16[384,128]{1,0:T(8,128)(2,1)S(1)}, bf16[384,128]{1,0:T(8,128)(2,1)S(1)}, u32[]{:S(2)}, u32[]{:S(2)}) collective-permute-start(bf16[384,128]{1,0:T(8,128)(2,1)S(1)} %get-tuple-element.47), channel_id=1, source_target_pairs={{0,1},{1,2},{2,3},{3,0},{4,5},{5,6},{6,7},{7,4},{8,9},{9,10},{10,1... | collective-permute-start | bytes 294920 | tf_op jit(solution)/shard_map/ppermute | solution.py:314
  85.8 7.2 %collective-permute-start.15 = (bf16[384,128]{1,0:T(8,128)(2,1)S(1)}, bf16[384,128]{1,0:T(8,128)(2,1)S(1)}, u32[]{:S(2)}, u32[]{:S(2)}) collective-permute-start(bf16[384,128]{1,0:T(8,128)(2,1)S(1)} %get-tuple-element.48), channel_id=1, source_target_pairs={{0,2},{1,3},{2,0},{3,1},{4,6},{5,7},{6,4},{7,5},{8,10},{9,11},{10,... | collective-permute-start | bytes 294920 | tf_op jit(solution)/shard_map/ppermute | solution.py:314
  87.8 5.8 %collective-permute-start.16 = (bf16[384,128]{1,0:T(8,128)(2,1)S(1)}, bf16[384,128]{1,0:T(8,128)(2,1)S(1)}, u32[]{:S(2)}, u32[]{:S(2)}) collective-permute-start(bf16[384,128]{1,0:T(8,128)(2,1)S(1)} %get-tuple-element.49), channel_id=1, source_target_pairs={{0,3},{1,0},{2,1},{3,2},{4,7},{5,4},{6,5},{7,6},{8,11},{9,8},{10,9... | collective-permute-start | bytes 294920 | tf_op jit(solution)/shard_map/ppermute | solution.py:314

commit v2 on v1

v2 whole, which is shorter than its diff:
```python
import jax
import jax.numpy as jnp
from jax import lax
from jax.experimental import pallas as pl
from jax.experimental.pallas import tpu as pltpu
from jax.sharding import PartitionSpec as P

NTR = 12
BS = 128
NBD = 128
CAP = 64
REP = 4
SHARE = NBD // REP
LIST_ROWS = CAP * NTR
SHARE_ROWS = SHARE * NTR
F32 = jnp.float32
BF16 = jnp.bfloat16
I32 = jnp.int32
MIB = 1 << 20

VMEM = pl.BlockSpec(memory_space=pltpu.VMEM)
SMEM = pl.BlockSpec(memory_space=pltpu.SMEM)
HBM = pl.BlockSpec(memory_space=pltpu.HBM)


def nt(a, b):
    return lax.dot_general(a, b, (((1,), (1,)), ((), ())), preferred_element_type=F32)


def pack4(tiles):
    return jnp.concatenate([t[0:8] for t in tiles] + [t[8:12] for t in tiles], axis=0)


def unpack4(rows):
    return [
        jnp.concatenate([rows[8 * m : 8 * m + 8], rows[32 + 4 * m : 36 + 4 * m]], axis=0)
        for m in range(4)
    ]


def tile16(t):
    return jnp.concatenate([t, jnp.zeros((4, BS), F32)], axis=0).astype(BF16)


def iotas(rows):
    sub = lax.broadcasted_iota(I32, (rows, BS), 0)
    lane = lax.broadcasted_iota(I32, (rows, BS), 1)
    return sub, lane


def before_matrix():
    sub, lane = iotas(BS)
    return jnp.where(sub < lane, 1.0, 0.0).astype(BF16)


def list_order(sends_ref, lane_no):
    entries = sends_ref[lane_no : lane_no + 1, :]
    ids = lax.broadcasted_iota(I32, (BS, CAP), 0)
    hit = jnp.where(ids == entries, 1.0, 0.0).astype(BF16)
    listed = nt(jnp.ones((8, CAP), BF16), hit)
    rank = jnp.dot(listed.astype(BF16), before_matrix(), preferred_element_type=F32)
    spot = lax.broadcasted_iota(I32, (CAP, BS), 0).astype(F32)
    chosen = jnp.where((rank[0:1] == spot) & (listed[0:1] > 0.5), 1.0, 0.0).astype(BF16)
    block = lax.broadcasted_iota(I32, (8, BS), 1).astype(F32).astype(BF16)
    return nt(block, chosen)[0:1].astype(I32)


def route_lanes():
    me = lax.axis_index("blk")
    core = me & 1
    odd = lax.shift_right_logical(me, 1) & 1
    return (2 - core, 1 + core, 3 * odd, 3 - 3 * odd)


def table_spots(cols_ref, out_ref, first_block):
    sub, lane = iotas(BS)
    me = lax.axis_index("blk")
    core = me & 1
    odd = lax.shift_right_logical(me, 1) & 1
    message = {0: 2 + odd, 1: 1 - core, 3: core, 4: 3 - odd}
    out_ref[2:3, :] = lane[0:1]
    for row in (0, 1, 3, 4):
        ids = sub + (first_block + row * NBD)
        read = (ids == cols_ref[1:2, :]) | (ids == cols_ref[2:3, :])
        read = jnp.where(read, 1.0, 0.0).astype(BF16)
        read = nt(jnp.ones((8, BS), BF16), read)
        read = jnp.where(read > 0.5, 1.0, 0.0).astype(BF16)
        rank = jnp.dot(read, before_matrix(), preferred_element_type=F32)
        out_ref[row : row + 1, :] = rank[0:1].astype(I32) + message[row] * CAP


def gather_lists(order_ref, load_tile, out_refs):
    for lane_no, out_ref in zip(route_lanes(), out_refs):

        def group(g, _, lane_no=lane_no, out_ref=out_ref):
            tiles = [load_tile(order_ref[lane_no, 4 * g + m]) for m in range(4)]
            rows = pl.ds(pl.multiple_of(48 * g, 16), 48)
            out_ref[rows, :] = pack4(tiles).astype(BF16)
            return 0

        lax.fori_loop(0, CAP // 4, group, 0, unroll=4)


def fetch(pairs, sems):
    copies = [pltpu.make_async_copy(src, dst, sems.at[n]) for n, (src, dst) in enumerate(pairs)]
    for copy in copies:
        copy.start()
    return copies


def first_kernel(sends_ref, tracers_ref, *rest):
    outs = rest[0:4]
    sends_v, tracers_v, order_v, order_s, sems, sem = rest[4:]
    copies = fetch([(sends_ref, sends_v), (tracers_ref, tracers_v)], sems)
    order_v[...] = jnp.zeros((8, BS), I32)
    copies[0].wait()
    for lane_no in range(4):
        order_v[lane_no : lane_no + 1, 0:CAP] = list_order(sends_v, lane_no)
    copy = pltpu.make_async_copy(order_v, order_s, sem)
    copy.start()
    copies[1].wait()
    copy.wait()

    def load_tile(i):
        return tracers_v[:, pl.ds(pl.multiple_of(i * BS, BS), BS)]

    gather_lists(order_s, load_tile, outs)


def fetch_local(blocks_ref, held_ref, sems):
    return fetch(
        [(blocks_ref.at[pl.ds(q * SHARE, SHARE), pl.ds(0, 1)], held_ref.at[pl.ds(q * SHARE, SHARE)])
         for q in range(REP)], sems)


def local_groups(copies, cols_s, load_tile, held_ref, out_ref):
    base = lax.axis_index("blk") * NBD
    for q in range(REP):
        copies[q].wait()

        def group(g, _):
            tiles = []
            for m in range(4):
                b = 4 * g + m
                tiles.append(nt(load_tile(cols_s[0, b] - base), held_ref[b, 0]))
            out_ref[pl.ds(pl.multiple_of(48 * g, 16), 48), :] = pack4(tiles)
            return 0

        lax.fori_loop(q * SHARE // 4, (q + 1) * SHARE // 4, group, 0, unroll=True)


def first_local_kernel(ecols_ref, icols_ref, isends_ref, tracers_ref, wet_ref, blocks_ref,
                       out_ref, espots_ref, ispots_ref, order_ref, share_ref, wet_share_ref,
                       ecols_v, icols_v, isends_v, wet_v, ecols_s, tracers_v, held_ref, sems, block_sems):
    me = lax.axis_index("rep")
    first_block = (lax.axis_index("blk") - 2) * NBD
    cells = SHARE * BS
    copies = fetch([
        (ecols_ref, ecols_v), (icols_ref, icols_v), (isends_ref, isends_v), (ecols_ref, ecols_s),
        (tracers_ref, tracers_v),
        (tracers_ref.at[:, pl.ds(pl.multiple_of(me * cells, cells), cells)], share_ref),
        (wet_ref.at[pl.ds(pl.multiple_of(me * SHARE, SHARE), SHARE)], wet_v),
    ], sems)
    block_copies = fetch_local(blocks_ref, held_ref, block_sems)
    for ref in (espots_ref, ispots_ref, order_ref):
        ref[...] = jnp.zeros((8, BS), I32)
    for copy in copies:
        copy.wait()
    wet_share_ref[...] = wet_v[...].astype(F32)
    table_spots(ecols_v, espots_ref, first_block)
    table_spots(icols_v, ispots_ref, first_block)
    for lane_no in range(4):
        order_ref[lane_no : lane_no + 1, 0:CAP] = list_order(isends_v, lane_no)

    def load_tile(i):
        return tile16(tracers_v[:, pl.ds(pl.multiple_of(i * BS, BS), BS)])

    local_groups(block_copies, ecols_s, load_tile, held_ref, out_ref)


def second_local_kernel(cols_ref, table_ref, blocks_ref, out_ref, cols_s, held_ref, sems, block_sems):
    copies = fetch([(cols_ref, cols_s)], sems)
    block_copies = fetch_local(blocks_ref, held_ref, block_sems)
    copies[0].wait()
    local_groups(block_copies, cols_s, lambda i: table_ref[i], held_ref, out_ref)


def remote_kernel(cols_ref, spots_ref, local_ref, blocks_ref, p0, p1, p2, p3,
                  own_ref, o1, o2, o3, cols_s, held_ref, table_ref, sems, block_sems):
    me = lax.axis_index("rep")
    first_block = (lax.axis_index("blk") - 2) * NBD
    steps = ((1, o1), (3, o3), (2, o2), (0, own_ref))
    shares = [me ^ step for step, _ in steps]
    copies = fetch([(cols_ref, cols_s)], sems)
    block_copies = fetch(
        [(blocks_ref.at[pl.ds(share * SHARE, SHARE), pl.ds(1, 2)], held_ref.at[pl.ds(n * SHARE, SHARE)])
         for n, share in enumerate(shares)], block_sems)

    for lane_no, piece in enumerate((p0, p1, p2, p3)):

        def spread(g, _, lane_no=lane_no, piece=piece):
            rows = piece[pl.ds(pl.multiple_of(48 * g, 16), 48), :].astype(F32)
            for m, tile in enumerate(unpack4(rows)):
                table_ref[lane_no * CAP + 4 * g + m] = tile16(tile)
            return 0

        lax.fori_loop(0, CAP // 4, spread, 0, unroll=4)

    def tile(k, b):
        c = cols_s[k, b] - first_block
        return table_ref[spots_ref[lax.shift_right_logical(c, 7), c & (NBD - 1)]]

    copies[0].wait()
    for n, (_, out_ref) in enumerate(steps):
        share = shares[n]
        block_copies[n].wait()

        def group(g, _, n=n, out_ref=out_ref, share=share):
            tiles = []
            for pair in range(2):
                xs, ws = [], []
                for half in range(2):
                    row = 4 * g + 2 * pair + half
                    b = share * SHARE + row
                    h = n * SHARE + row
                    xs.append(jnp.concatenate([tile(1, b), tile(2, b)], axis=1))
                    ws.append(jnp.concatenate([held_ref[h, 0], held_ref[h, 1]], axis=1))
                y = nt(jnp.concatenate(xs, axis=0), jnp.concatenate(ws, axis=0))
                tiles += [y[0:16, 0:BS], y[16:32, BS:]]
            there = pl.ds(pl.multiple_of((share * (SHARE // 4) + g) * 48, 16), 48)
            total = pack4(tiles) + local_ref[there, :]
            out_ref[pl.ds(pl.multiple_of(48 * g, 16), 48), :] = total.astype(out_ref.dtype)
            return 0

        lax.fori_loop(0, SHARE // 4, group, 0, unroll=True)


def middle_kernel(own_ref, g1, g2, g3, share_ref, coupling_ref, wet_ref,
                  before_ref, packed_ref, coupling_v, mid_ref, sem):
    copy = pltpu.make_async_copy(coupling_ref, coupling_v, sem)
    copy.start()
    for g in range(SHARE // 4):
        rows = pl.ds(48 * g, 48)
        total = own_ref[rows, :] + g1[rows, :].astype(F32) + g2[rows, :].astype(F32) + g3[rows, :].astype(F32)
        for m, tile in enumerate(unpack4(total)):
            lanes = pl.ds((4 * g + m) * BS, BS)
            mid_ref[:, lanes] = share_ref[:, lanes] + tile
    copy.wait()
    pushed = lax.dot_general(coupling_v[...], mid_ref[...], (((1,), (0,)), ((), ())),
                             precision=lax.Precision.HIGHEST, preferred_element_type=F32)
    for g in range(SHARE // 4):
        tiles = []
        for m in range(4):
            b = 4 * g + m
            lanes = pl.ds(b * BS, BS)
            tile = mid_ref[:, lanes] + wet_ref[b : b + 1, :] * jnp.tanh(pushed[:, b * BS : (b + 1) * BS])
            before_ref[:, lanes] = tile
            tiles.append(tile)
        packed_ref[pl.ds(48 * g, 48), :] = pack4(tiles).astype(BF16)


def second_kernel(order_ref, own, g2, g3, g1, *rest):
    outs, table_ref = rest[0:4], rest[4]
    me = lax.axis_index("rep")
    for step, packed in ((0, own), (2, g2), (3, g3), (1, g1)):
        share = me ^ step

        def spread(g, _, packed=packed, share=share):
            rows = packed[pl.ds(pl.multiple_of(48 * g, 16), 48), :].astype(F32)
            for m, tile in enumerate(unpack4(rows)):
                table_ref[share * SHARE + 4 * g + m] = tile16(tile)
            return 0

        lax.fori_loop(0, SHARE // 4, spread, 0, unroll=4)
    gather_lists(order_ref, lambda i: table_ref[i].astype(F32), outs)


def last_kernel(own_ref, g1, g2, g3, before_ref, wet_ref, out_ref):
    for g in range(SHARE // 4):
        rows = pl.ds(48 * g, 48)
        total = own_ref[rows, :] + g1[rows, :].astype(F32) + g2[rows, :].astype(F32) + g3[rows, :].astype(F32)
        for m, tile in enumerate(unpack4(total)):
            b = 4 * g + m
            lanes = pl.ds(b * BS, BS)
            out_ref[:, lanes] = wet_ref[b : b + 1, :] * (before_ref[:, lanes] + tile)


def sds(shape, dtype):
    return jax.ShapeDtypeStruct(shape, dtype)


def call(body, outs, in_specs, scratch, name, mib, flops=0, bytes_accessed=0):
    kernel = pl.pallas_call(
        body,
        out_shape=outs,
        in_specs=in_specs,
        out_specs=jax.tree.map(lambda _: VMEM, outs),
        scratch_shapes=scratch,
        compiler_params=pltpu.CompilerParams(vmem_limit_bytes=mib * MIB),
        cost_estimate=pl.CostEstimate(flops=flops, bytes_accessed=bytes_accessed, transcendentals=0),
        name=name,
    )

    def run(*operands):
        return kernel(*(
            pltpu.with_memory_space_constraint(x, pltpu.HBM) if spec is HBM else x
            for x, spec in zip(operands, in_specs)))

    return run


def swap_blk(messages):
    n = lax.axis_size("blk")
    partners = (
        lambda i: i ^ 1,
        lambda i: i + 1 if i & 1 else i - 1,
        lambda i: i + 2 if i & 2 else i - 2,
        lambda i: i ^ 2,
    )
    return [
        lax.ppermute(x, "blk", [(i, to(i)) for i in range(n) if 0 <= to(i) < n])
        for x, to in zip(messages, partners)
    ]


def swap_rep(x, distance):
    n = lax.axis_size("rep")
    return lax.ppermute(x, "rep", [(i, i ^ distance) for i in range(n)])


def lists_out():
    return [sds((LIST_ROWS, BS), BF16)] * 4


def dma(n):
    return pltpu.SemaphoreType.DMA((n,))


def held(slots):
    return pltpu.VMEM((NBD, slots, BS, BS), BF16)


def remote_product(cols, spots, local, blocks, pieces):
    share = sds((SHARE_ROWS, BS), BF16)
    return call(
        remote_kernel, [sds((SHARE_ROWS, BS), F32), share, share, share],
        [HBM, SMEM, VMEM, HBM, VMEM, VMEM, VMEM, VMEM],
        [pltpu.SMEM((3, BS), I32), held(2), pltpu.VMEM((4 * CAP, 16, BS), BF16), dma(1), dma(REP)],
        "remote_product", 24, flops=100_000_000, bytes_accessed=10_000_000,
    )(cols, spots, local, blocks, *pieces)


def on_device(tracers, explicit_blocks, explicit_cols, explicit_sends,
              implicit_blocks, implicit_cols, implicit_sends, coupling, wet):
    ecols, icols = explicit_cols.T, implicit_cols.T
    esends, isends = explicit_sends.reshape(4, CAP), implicit_sends.reshape(4, CAP)
    wet = wet.reshape(NBD, BS)
    cells = SHARE * BS
    ints = sds((8, BS), I32)
    small = pltpu.VMEM((3, BS), I32)
    local_sum = sds((NBD * NTR, BS), F32)

    outbound = call(
        first_kernel, lists_out(), [HBM, HBM],
        [pltpu.VMEM((4, CAP), I32), pltpu.VMEM((NTR, NBD * BS), F32), pltpu.VMEM((8, BS), I32),
         pltpu.SMEM((8, BS), I32), dma(2), pltpu.SemaphoreType.DMA],
        "first_lists", 16,
    )(esends, tracers)
    pieces = swap_blk(outbound)
    local, espots, ispots, iorder, share, wet_share = call(
        first_local_kernel,
        [local_sum, ints, ints, ints, sds((NTR, cells), F32), sds((SHARE, BS), F32)], [HBM] * 6,
        [small, small, pltpu.VMEM((4, CAP), I32), pltpu.VMEM((SHARE, BS), I32), pltpu.SMEM((3, BS), I32),
         pltpu.VMEM((NTR, NBD * BS), F32), held(1), dma(7), dma(REP)],
        "first_local_product", 20, flops=50_000_000, bytes_accessed=5_000_000,
    )(ecols, icols, isends, tracers, wet, explicit_blocks)
    own, *parts = remote_product(ecols, espots, local, explicit_blocks, pieces)
    got = [swap_rep(parts[k - 1], k) for k in (1, 3, 2)]
    before, packed = call(
        middle_kernel, [sds((NTR, cells), F32), sds((SHARE_ROWS, BS), BF16)],
        [VMEM, VMEM, VMEM, VMEM, VMEM, HBM, VMEM],
        [pltpu.VMEM((NTR, NTR), F32), pltpu.VMEM((NTR, cells), F32), pltpu.SemaphoreType.DMA],
        "middle", 16,
    )(own, *got, share, coupling, wet_share)
    others = [swap_rep(packed, k) for k in (2, 3, 1)]
    *outbound, table = call(
        second_kernel, lists_out() + [sds((NBD, 16, BS), BF16)], [SMEM] + [VMEM] * 4, [],
        "second_lists", 16,
    )(iorder, packed, *others)
    pieces = swap_blk(outbound)
    local = call(
        second_local_kernel, local_sum, [HBM, VMEM, HBM],
        [pltpu.SMEM((3, BS), I32), held(1), dma(1), dma(REP)],
        "second_local_product", 16, flops=50_000_000, bytes_accessed=5_000_000,
    )(icols, table, implicit_blocks)
    own, *parts = remote_product(icols, ispots, local, implicit_blocks, pieces)
    got = [swap_rep(parts[k - 1], k) for k in (1, 3, 2)]
    return call(
        last_kernel, sds((NTR, cells), F32), [VMEM] * 6, [], "last", 16,
    )(own, *got, before, wet_share)


def solution(mesh):
    in_specs = (
        P(None, "blk"),
        P("blk", "rep", None, None),
        P("blk", "rep"),
        P("blk", "rep", None, None),
        P("blk", "rep", None, None),
        P("blk", "rep"),
        P("blk", "rep", None, None),
        P(),
        P("blk"),
    )
    out_specs = P(None, ("blk", "rep"))
    return jax.shard_map(
        on_device, mesh=mesh, in_specs=in_specs, out_specs=out_specs, check_vma=False
    )
```

time: 95 us -> 75.3 us (0.79)
  local copies, waits for them, and re-layouts: 9.26 us -> 0 us
  starting transfers between devices: 38.9 us -> 31.1 us
  waiting for transfers between devices: 17.3 us -> 16 us
    unnamed x28 -> x0, local copies, waits for them, and re-layouts: 9.26 us -> none
    ppermute x17, starting transfers between devices: 38.9 us -> 31.1 us  [the longest x8 17.1 us: swap_blk(): lax.ppermute(x, 'blk', [(i, to(i)) for i in range(n) if 0 <= to(i) < n])]
    ppermute x17, waiting for transfers between devices: 17.3 us -> 16 us  [the longest x9 14.2 us: swap_rep(): return lax.ppermute(x, 'rep', [(i, i ^ distance) for i in range(n)])]
    pallas_call x9 -> x8, Pallas kernels: 28.7 us -> 27.8 us  [run(): kernel(*(pltpu.with_memory_space_constraint(x, pltpu.HBM) if spec is HBM...]
  transfers between devices with their start and end apart: 17 -> 17, of which waited for: 8 -> 9; matrix products, arithmetic and copies ran while one was open for 0% -> 0% of each run, Pallas kernels for 13% -> 14%
where the time goes in v2:
time: 75.3 us; the launch traced here: 75 us
  starting transfers between devices  31.1 us (41%)
  Pallas kernels  27.8 us (37%)
  waiting for transfers between devices  16 us (21%)
    pallas_call x8, Pallas kernels, run(): kernel(*(pltpu.with_memory_space_constraint(x, pltpu.HBM) if spec is HBM...  27.8 us
    ppermute x8, starting transfers between devices, swap_blk(): lax.ppermute(x, 'blk', [(i, to(i)) for i in range(n) if 0 <= to(i) < n])  17.1 us
    ppermute x9, waiting for transfers between devices, swap_rep(): return lax.ppermute(x, 'rep', [(i, i ^ distance) for i in range(n)])  14.2 us
    ppermute x9, starting transfers between devices, swap_rep(): return lax.ppermute(x, 'rep', [(i, i ^ distance) for i in range(n)])  13.9 us
    ppermute x8, waiting for transfers between devices, swap_blk(): lax.ppermute(x, 'blk', [(i, to(i)) for i in range(n) if 0 <= to(i) < n])  1.8 us
  transfers between devices with their start and end apart: 17, of which 9 were waited for; matrix products, arithmetic and copies ran while one was open for 0% of the time, Pallas kernels for 14%

profile of v2, /device:TPU:6, one launch (start us, length us, event | category | flops | bytes accessed | tf_op | source)
XLA Modules:
  0.0 75.0 jit_solution(14906565148390935357)
XLA Ops:
  0.0 3.1 %first_lists.1 = (bf16[768,128]{1,0:T(8,128)(2,1)S(1)}, bf16[768,128]{1,0:T(8,128)(2,1)S(1)}, bf16[768,128]{1,0:T(8,128)(2,1)S(1)}, bf16[768,128]{1,0:T(8,128)(2,1)S(1)}) custom-call(s32[4,64]{1,0:T(4,128)} %bitcast.11, f32[12,16384]{1,0:T(8,128)} %tracers_ref.3), custom_call_target="tpu_custom_call" | custom-call | tf_op jit(solution)/shard_map/first_lists/pallas_call | solution.py:305
  3.1 0.1 collective-permute-start
  3.2 5.3 %collective-permute-start.1 = (bf16[768,128]{1,0:T(8,128)(2,1)S(1)}, bf16[768,128]{1,0:T(8,128)(2,1)S(1)}, u32[]{:S(2)}, u32[]{:S(2)}) collective-permute-start(bf16[768,128]{1,0:T(8,128)(2,1)S(1)} %get-tuple-element.35), channel_id=1, source_target_pairs={{4,8},{8,4},{12,16},{16,12},{20,24},{24,20},{28,32},{32,28},{36,40... | collective-permute-start | bytes 589832 | tf_op jit(solution)/shard_map/ppermute | solution.py:321
  8.5 2.7 %collective-permute-start.2 = (bf16[768,128]{1,0:T(8,128)(2,1)S(1)}, bf16[768,128]{1,0:T(8,128)(2,1)S(1)}, u32[]{:S(2)}, u32[]{:S(2)}) collective-permute-start(bf16[768,128]{1,0:T(8,128)(2,1)S(1)} %get-tuple-element.36), channel_id=1, source_target_pairs={{8,16},{12,20},{16,8},{20,12},{24,32},{28,36},{32,24},{36,28},{40,... | collective-permute-start | bytes 589832 | tf_op jit(solution)/shard_map/ppermute | solution.py:321
  11.2 0.1 collective-permute-start.3
  11.3 6.9 %first_local_product.1 = (f32[1536,128]{1,0:T(8,128)S(1)}, s32[8,128]{1,0:T(8,128)S(1)}, s32[8,128]{1,0:T(8,128)S(1)}, s32[8,128]{1,0:T(8,128)S(1)}, f32[12,4096]{1,0:T(8,128)S(1)}, /*index=5*/f32[32,128]{1,0:T(8,128)S(1)}) custom-call(s32[3,128]{1,0:T(4,128)} %bitcast.9, s32[3,128]{1,0:T(4,128)} %bitcast.6, s32[4,64]{1,0:T(4,128)} %bitcast.12, ...), custom_call_target="tpu_custom_call" | custom-call | flops 50000000 | bytes 5000000 | tf_op jit(solution)/shard_map/first_local_product/pallas_call | solution.py:305
  18.2 0.0 collective-permute-done.p0
  18.2 0.0 collective-permute-done.1.p1
  18.2 0.0 collective-permute-done.2.p2
  18.2 0.0 collective-permute-done.3.p3
  18.2 5.2 %remote_product.2 = (f32[384,128]{1,0:T(8,128)S(1)}, bf16[384,128]{1,0:T(8,128)(2,1)S(1)}, bf16[384,128]{1,0:T(8,128)(2,1)S(1)}, bf16[384,128]{1,0:T(8,128)(2,1)S(1)}) custom-call(s32[3,128]{1,0:T(4,128)} %bitcast.10, s32[8,128]{1,0:T(8,128)S(1)} %get-tuple-element.32.spots_ref, f32[1536,128]{1,0:T(8,128)S(1)} %get-tuple-element.33.local_ref, ...), custom_call_target="tpu_custom_call" | custom-call | flops 100000000 | bytes 10000000 | tf_op jit(solution)/shard_map/remote_product/pallas_call | solution.py:305
  23.4 2.0 %collective-permute-start.4 = (bf16[384,128]{1,0:T(8,128)(2,1)S(1)}, bf16[384,128]{1,0:T(8,128)(2,1)S(1)}, u32[]{:S(2)}, u32[]{:S(2)}) collective-permute-start(bf16[384,128]{1,0:T(8,128)(2,1)S(1)} %get-tuple-element.39), channel_id=1, source_target_pairs={{0,1},{1,0},{2,3},{3,2},{4,5},{5,4},{6,7},{7,6},{8,9},{9,8},{10,11... | collective-permute-start | bytes 294920 | tf_op jit(solution)/shard_map/ppermute | solution.py:328
  25.4 2.5 %collective-permute-start.5 = (bf16[384,128]{1,0:T(8,128)(2,1)S(1)}, bf16[384,128]{1,0:T(8,128)(2,1)S(1)}, u32[]{:S(2)}, u32[]{:S(2)}) collective-permute-start(bf16[384,128]{1,0:T(8,128)(2,1)S(1)} %get-tuple-element.40), channel_id=1, source_target_pairs={{0,3},{1,2},{2,1},{3,0},{4,7},{5,6},{6,5},{7,4},{8,11},{9,10},{10,... | collective-permute-start | bytes 294920 | tf_op jit(solution)/shard_map/ppermute | solution.py:328
  27.9 1.0 %collective-permute-start.6 = (bf16[384,128]{1,0:T(8,128)(2,1)S(1)}, bf16[384,128]{1,0:T(8,128)(2,1)S(1)}, u32[]{:S(2)}, u32[]{:S(2)}) collective-permute-start(bf16[384,128]{1,0:T(8,128)(2,1)S(1)} %get-tuple-element.41), channel_id=1, source_target_pairs={{0,2},{1,3},{2,0},{3,1},{4,6},{5,7},{6,4},{7,5},{8,10},{9,11},{10,... | collective-permute-start | bytes 294920 | tf_op jit(solution)/shard_map/ppermute | solution.py:328
  29.0 0.0 collective-permute-done.4.g1
  29.0 2.9 %collective-permute-done.5.g2 = bf16[384,128]{1,0:T(8,128)(2,1)S(1)} collective-permute-done((bf16[384,128]{1,0:T(8,128)(2,1)S(1)}, bf16[384,128]{1,0:T(8,128)(2,1)S(1)}, u32[]{:S(2)}, u32[]{:S(2)}) %collective-permute-start.5) | collective-permute-done | bytes 98336 | tf_op jit(solution)/shard_map/ppermute | solution.py:328
  31.9 2.2 %collective-permute-done.6.g3 = bf16[384,128]{1,0:T(8,128)(2,1)S(1)} collective-permute-done((bf16[384,128]{1,0:T(8,128)(2,1)S(1)}, bf16[384,128]{1,0:T(8,128)(2,1)S(1)}, u32[]{:S(2)}, u32[]{:S(2)}) %collective-permute-start.6) | collective-permute-done | bytes 98336 | tf_op jit(solution)/shard_map/ppermute | solution.py:328
  34.1 1.1 %middle.1 = (f32[12,4096]{1,0:T(8,128)S(1)}, bf16[384,128]{1,0:T(8,128)(2,1)S(1)}) custom-call(f32[384,128]{1,0:T(8,128)S(1)} %get-tuple-element.38.own_ref, bf16[384,128]{1,0:T(8,128)(2,1)S(1)} %collective-permute-done.4.g1, bf16[384,128]{1,0:T(8,128)(2,1)S(1)} %collective-permute-done.5.g2, bf16[384,128]{1,0:T(8,128)(2,1)S(1)} %collective-permute-done.6.g3, ...), custom_call_target="tpu_custom_call" | custom-call | tf_op jit(solution)/shard_map/middle/pallas_call | solution.py:305
  35.2 1.1 %collective-permute-start.9 = (bf16[384,128]{1,0:T(8,128)(2,1)S(1)}, bf16[384,128]{1,0:T(8,128)(2,1)S(1)}, u32[]{:S(2)}, u32[]{:S(2)}) collective-permute-start(bf16[384,128]{1,0:T(8,128)(2,1)S(1)} %get-tuple-element.44.own), channel_id=1, source_target_pairs={{0,1},{1,0},{2,3},{3,2},{4,5},{5,4},{6,7},{7,6},{8,9},{9,8},{10,11... | collective-permute-start | bytes 294920 | tf_op jit(solution)/shard_map/ppermute | solution.py:328
  36.3 1.2 %collective-permute-start.8 = (bf16[384,128]{1,0:T(8,128)(2,1)S(1)}, bf16[384,128]{1,0:T(8,128)(2,1)S(1)}, u32[]{:S(2)}, u32[]{:S(2)}) collective-permute-start(bf16[384,128]{1,0:T(8,128)(2,1)S(1)} %get-tuple-element.44.own), channel_id=1, source_target_pairs={{0,3},{1,2},{2,1},{3,0},{4,7},{5,6},{6,5},{7,4},{8,11},{9,10},{10,... | collective-permute-start | bytes 294920 | tf_op jit(solution)/shard_map/ppermute | solution.py:328
  37.5 1.9 %collective-permute-start.7 = (bf16[384,128]{1,0:T(8,128)(2,1)S(1)}, bf16[384,128]{1,0:T(8,128)(2,1)S(1)}, u32[]{:S(2)}, u32[]{:S(2)}) collective-permute-start(bf16[384,128]{1,0:T(8,128)(2,1)S(1)} %get-tuple-element.44.own), channel_id=1, source_target_pairs={{0,2},{1,3},{2,0},{3,1},{4,6},{5,7},{6,4},{7,5},{8,10},{9,11},{10,... | collective-permute-start | bytes 294920 | tf_op jit(solution)/shard_map/ppermute | solution.py:328
  39.4 1.3 %collective-permute-done.9.g1 = bf16[384,128]{1,0:T(8,128)(2,1)S(1)} collective-permute-done((bf16[384,128]{1,0:T(8,128)(2,1)S(1)}, bf16[384,128]{1,0:T(8,128)(2,1)S(1)}, u32[]{:S(2)}, u32[]{:S(2)}) %collective-permute-start.9) | collective-permute-done | bytes 98336 | tf_op jit(solution)/shard_map/ppermute | solution.py:328
  40.7 1.5 %collective-permute-done.8.g3 = bf16[384,128]{1,0:T(8,128)(2,1)S(1)} collective-permute-done((bf16[384,128]{1,0:T(8,128)(2,1)S(1)}, bf16[384,128]{1,0:T(8,128)(2,1)S(1)}, u32[]{:S(2)}, u32[]{:S(2)}) %collective-permute-start.8) | collective-permute-done | bytes 98336 | tf_op jit(solution)/shard_map/ppermute | solution.py:328
  42.1 1.5 %collective-permute-done.7.g2 = bf16[384,128]{1,0:T(8,128)(2,1)S(1)} collective-permute-done((bf16[384,128]{1,0:T(8,128)(2,1)S(1)}, bf16[384,128]{1,0:T(8,128)(2,1)S(1)}, u32[]{:S(2)}, u32[]{:S(2)}) %collective-permute-start.7) | collective-permute-done | bytes 98336 | tf_op jit(solution)/shard_map/ppermute | solution.py:328
  43.6 1.6 %second_lists.1 = (bf16[768,128]{1,0:T(8,128)(2,1)S(1)}, bf16[768,128]{1,0:T(8,128)(2,1)S(1)}, bf16[768,128]{1,0:T(8,128)(2,1)S(1)}, bf16[768,128]{1,0:T(8,128)(2,1)S(1)}, bf16[128,16,128]{2,1,0:T(8,128)(2,1)S(1)}) custom-call(s32[8,128]{1,0:T(8,128)S(1)} %get-tuple-element.31.order_ref, bf16[384,128]{1,0:T(8,128)(2,1)S(1)} %get-tuple-element.44.own, ...), custom_call_target="tpu_custom_call" | custom-call | tf_op jit(solution)/shard_map/second_lists/pallas_call | solution.py:305
  45.2 0.1 collective-permute-start.10
  45.3 5.0 %collective-permute-start.11 = (bf16[768,128]{1,0:T(8,128)(2,1)S(1)}, bf16[768,128]{1,0:T(8,128)(2,1)S(1)}, u32[]{:S(2)}, u32[]{:S(2)}) collective-permute-start(bf16[768,128]{1,0:T(8,128)(2,1)S(1)} %get-tuple-element.47), channel_id=1, source_target_pairs={{4,8},{8,4},{12,16},{16,12},{20,24},{24,20},{28,32},{32,28},{36,40... | collective-permute-start | bytes 589832 | tf_op jit(solution)/shard_map/ppermute | solution.py:321
  50.2 3.9 %collective-permute-start.12 = (bf16[768,128]{1,0:T(8,128)(2,1)S(1)}, bf16[768,128]{1,0:T(8,128)(2,1)S(1)}, u32[]{:S(2)}, u32[]{:S(2)}) collective-permute-start(bf16[768,128]{1,0:T(8,128)(2,1)S(1)} %get-tuple-element.48), channel_id=1, source_target_pairs={{8,16},{12,20},{16,8},{20,12},{24,32},{28,36},{32,24},{36,28},{40,... | collective-permute-start | bytes 589832 | tf_op jit(solution)/shard_map/ppermute | solution.py:321
  54.2 0.1 collective-permute-start.13
  54.3 3.9 %second_local_product.1.local_ref = f32[1536,128]{1,0:T(8,128)S(1)} custom-call(s32[3,128]{1,0:T(4,128)} %bitcast.7, bf16[128,16,128]{2,1,0:T(8,128)(2,1)S(1)} %get-tuple-element.45.table_ref, bf16[128,3,128,128]{3,2,1,0:T(8,128)(2,1)} %blocks_ref.7), custom_call_target="tpu_custom_call" | custom-call | flops 50000000 | bytes 5000000 | tf_op jit(solution)/shard_map/second_local_product/pallas_call | solution.py:305
  58.2 0.0 collective-permute-done.10.p0
  58.2 0.0 collective-permute-done.11.p1
  58.2 1.8 %collective-permute-done.12.p2 = bf16[768,128]{1,0:T(8,128)(2,1)S(1)} collective-permute-done((bf16[768,128]{1,0:T(8,128)(2,1)S(1)}, bf16[768,128]{1,0:T(8,128)(2,1)S(1)}, u32[]{:S(2)}, u32[]{:S(2)}) %collective-permute-start.12) | collective-permute-done | bytes 196640 | tf_op jit(solution)/shard_map/ppermute | solution.py:321
  60.0 0.0 collective-permute-done.13.p3
  60.0 5.2 %remote_product.3 = (f32[384,128]{1,0:T(8,128)S(1)}, bf16[384,128]{1,0:T(8,128)(2,1)S(1)}, bf16[384,128]{1,0:T(8,128)(2,1)S(1)}, bf16[384,128]{1,0:T(8,128)(2,1)S(1)}) custom-call(s32[3,128]{1,0:T(4,128)} %bitcast.8, s32[8,128]{1,0:T(8,128)S(1)} %get-tuple-element.30.spots_ref, f32[1536,128]{1,0:T(8,128)S(1)} %second_local_product.1.local_ref, ...), custom_call_target="tpu_custom_call" | custom-call | flops 100000000 | bytes 10000000 | tf_op jit(solution)/shard_map/remote_product/pallas_call | solution.py:305
  65.2 0.8 %collective-permute-start.14 = (bf16[384,128]{1,0:T(8,128)(2,1)S(1)}, bf16[384,128]{1,0:T(8,128)(2,1)S(1)}, u32[]{:S(2)}, u32[]{:S(2)}) collective-permute-start(bf16[384,128]{1,0:T(8,128)(2,1)S(1)} %get-tuple-element.51), channel_id=1, source_target_pairs={{0,1},{1,0},{2,3},{3,2},{4,5},{5,4},{6,7},{7,6},{8,9},{9,8},{10,11... | collective-permute-start | bytes 294920 | tf_op jit(solution)/shard_map/ppermute | solution.py:328
  65.9 2.1 %collective-permute-start.15 = (bf16[384,128]{1,0:T(8,128)(2,1)S(1)}, bf16[384,128]{1,0:T(8,128)(2,1)S(1)}, u32[]{:S(2)}, u32[]{:S(2)}) collective-permute-start(bf16[384,128]{1,0:T(8,128)(2,1)S(1)} %get-tuple-element.52), channel_id=1, source_target_pairs={{0,3},{1,2},{2,1},{3,0},{4,7},{5,6},{6,5},{7,4},{8,11},{9,10},{10,... | collective-permute-start | bytes 294920 | tf_op jit(solution)/shard_map/ppermute | solution.py:328
  68.1 1.3 %collective-permute-start.16 = (bf16[384,128]{1,0:T(8,128)(2,1)S(1)}, bf16[384,128]{1,0:T(8,128)(2,1)S(1)}, u32[]{:S(2)}, u32[]{:S(2)}) collective-permute-start(bf16[384,128]{1,0:T(8,128)(2,1)S(1)} %get-tuple-element.53), channel_id=1, source_target_pairs={{0,2},{1,3},{2,0},{3,1},{4,6},{5,7},{6,4},{7,5},{8,10},{9,11},{10,... | collective-permute-start | bytes 294920 | tf_op jit(solution)/shard_map/ppermute | solution.py:328
  69.3 1.1 %collective-permute-done.14.g1 = bf16[384,128]{1,0:T(8,128)(2,1)S(1)} collective-permute-done((bf16[384,128]{1,0:T(8,128)(2,1)S(1)}, bf16[384,128]{1,0:T(8,128)(2,1)S(1)}, u32[]{:S(2)}, u32[]{:S(2)}) %collective-permute-start.14) | collective-permute-done | bytes 98336 | tf_op jit(solution)/shard_map/ppermute | solution.py:328
  70.4 1.4 %collective-permute-done.15.g2 = bf16[384,128]{1,0:T(8,128)(2,1)S(1)} collective-permute-done((bf16[384,128]{1,0:T(8,128)(2,1)S(1)}, bf16[384,128]{1,0:T(8,128)(2,1)S(1)}, u32[]{:S(2)}, u32[]{:S(2)}) %collective-permute-start.15) | collective-permute-done | bytes 98336 | tf_op jit(solution)/shard_map/ppermute | solution.py:328
  71.8 2.4 %collective-permute-done.16.g3 = bf16[384,128]{1,0:T(8,128)(2,1)S(1)} collective-permute-done((bf16[384,128]{1,0:T(8,128)(2,1)S(1)}, bf16[384,128]{1,0:T(8,128)(2,1)S(1)}, u32[]{:S(2)}, u32[]{:S(2)}) %collective-permute-start.16) | collective-permute-done | bytes 98336 | tf_op jit(solution)/shard_map/ppermute | solution.py:328
  74.2 0.8 %last.1 = f32[12,4096]{1,0:T(8,128)} custom-call(f32[384,128]{1,0:T(8,128)S(1)} %get-tuple-element.50.own_ref, bf16[384,128]{1,0:T(8,128)(2,1)S(1)} %collective-permute-done.14.g1, bf16[384,128]{1,0:T(8,128)(2,1)S(1)} %collective-permute-done.15.g2, bf16[384,128]{1,0:T(8,128)(2,1)S(1)} %collective-permute-done.16.g3, ...), custom_call_target="tpu_custom_call" | custom-call | tf_op jit(solution)/shard_map/last/pallas_call | solution.py:305
Async XLA Ops:
  3.1 15.0 %collective-permute-start = (bf16[768,128]{1,0:T(8,128)(2,1)S(1)}, bf16[768,128]{1,0:T(8,128)(2,1)S(1)}, u32[]{:S(2)}, u32[]{:S(2)}) collective-permute-start(bf16[768,128]{1,0:T(8,128)(2,1)S(1)} %get-tuple-element.34), channel_id=1, source_target_pairs={{0,4},{4,0},{8,12},{12,8},{16,20},{20,16},{24,28},{28,24},{32,36},... | collective-permute-start | bytes 589832 | tf_op jit(solution)/shard_map/ppermute | solution.py:321
  3.2 15.0 %collective-permute-start.1 = (bf16[768,128]{1,0:T(8,128)(2,1)S(1)}, bf16[768,128]{1,0:T(8,128)(2,1)S(1)}, u32[]{:S(2)}, u32[]{:S(2)}) collective-permute-start(bf16[768,128]{1,0:T(8,128)(2,1)S(1)} %get-tuple-element.35), channel_id=1, source_target_pairs={{4,8},{8,4},{12,16},{16,12},{20,24},{24,20},{28,32},{32,28},{36,40... | collective-permute-start | bytes 589832 | tf_op jit(solution)/shard_map/ppermute | solution.py:321
  8.5 9.7 %collective-permute-start.2 = (bf16[768,128]{1,0:T(8,128)(2,1)S(1)}, bf16[768,128]{1,0:T(8,128)(2,1)S(1)}, u32[]{:S(2)}, u32[]{:S(2)}) collective-permute-start(bf16[768,128]{1,0:T(8,128)(2,1)S(1)} %get-tuple-element.36), channel_id=1, source_target_pairs={{8,16},{12,20},{16,8},{20,12},{24,32},{28,36},{32,24},{36,28},{40,... | collective-permute-start | bytes 589832 | tf_op jit(solution)/shard_map/ppermute | solution.py:321
  11.2 7.0 %collective-permute-start.3 = (bf16[768,128]{1,0:T(8,128)(2,1)S(1)}, bf16[768,128]{1,0:T(8,128)(2,1)S(1)}, u32[]{:S(2)}, u32[]{:S(2)}) collective-permute-start(bf16[768,128]{1,0:T(8,128)(2,1)S(1)} %get-tuple-element.37), channel_id=1, source_target_pairs={{0,8},{4,12},{8,0},{12,4},{16,24},{20,28},{24,16},{28,20},{32,40},... | collective-permute-start | bytes 589832 | tf_op jit(solution)/shard_map/ppermute | solution.py:321
  23.4 5.6 %collective-permute-start.4 = (bf16[384,128]{1,0:T(8,128)(2,1)S(1)}, bf16[384,128]{1,0:T(8,128)(2,1)S(1)}, u32[]{:S(2)}, u32[]{:S(2)}) collective-permute-start(bf16[384,128]{1,0:T(8,128)(2,1)S(1)} %get-tuple-element.39), channel_id=1, source_target_pairs={{0,1},{1,0},{2,3},{3,2},{4,5},{5,4},{6,7},{7,6},{8,9},{9,8},{10,11... | collective-permute-start | bytes 294920 | tf_op jit(solution)/shard_map/ppermute | solution.py:328
  25.4 6.5 %collective-permute-start.5 = (bf16[384,128]{1,0:T(8,128)(2,1)S(1)}, bf16[384,128]{1,0:T(8,128)(2,1)S(1)}, u32[]{:S(2)}, u32[]{:S(2)}) collective-permute-start(bf16[384,128]{1,0:T(8,128)(2,1)S(1)} %get-tuple-element.40), channel_id=1, source_target_pairs={{0,3},{1,2},{2,1},{3,0},{4,7},{5,6},{6,5},{7,4},{8,11},{9,10},{10,... | collective-permute-start | bytes 294920 | tf_op jit(solution)/shard_map/ppermute | solution.py:328
  27.9 6.1 %collective-permute-start.6 = (bf16[384,128]{1,0:T(8,128)(2,1)S(1)}, bf16[384,128]{1,0:T(8,128)(2,1)S(1)}, u32[]{:S(2)}, u32[]{:S(2)}) collective-permute-start(bf16[384,128]{1,0:T(8,128)(2,1)S(1)} %get-tuple-element.41), channel_id=1, source_target_pairs={{0,2},{1,3},{2,0},{3,1},{4,6},{5,7},{6,4},{7,5},{8,10},{9,11},{10,... | collective-permute-start | bytes 294920 | tf_op jit(solution)/shard_map/ppermute | solution.py:328
  35.2 5.4 %collective-permute-start.9 = (bf16[384,128]{1,0:T(8,128)(2,1)S(1)}, bf16[384,128]{1,0:T(8,128)(2,1)S(1)}, u32[]{:S(2)}, u32[]{:S(2)}) collective-permute-start(bf16[384,128]{1,0:T(8,128)(2,1)S(1)} %get-tuple-element.44.own), channel_id=1, source_target_pairs={{0,1},{1,0},{2,3},{3,2},{4,5},{5,4},{6,7},{7,6},{8,9},{9,8},{10,11... | collective-permute-start | bytes 294920 | tf_op jit(solution)/shard_map/ppermute | solution.py:328
  36.3 5.8 %collective-permute-start.8 = (bf16[384,128]{1,0:T(8,128)(2,1)S(1)}, bf16[384,128]{1,0:T(8,128)(2,1)S(1)}, u32[]{:S(2)}, u32[]{:S(2)}) collective-permute-start(bf16[384,128]{1,0:T(8,128)(2,1)S(1)} %get-tuple-element.44.own), channel_id=1, source_target_pairs={{0,3},{1,2},{2,1},{3,0},{4,7},{5,6},{6,5},{7,4},{8,11},{9,10},{10,... | collective-permute-start | bytes 294920 | tf_op jit(solution)/shard_map/ppermute | solution.py:328
  37.5 6.1 %collective-permute-start.7 = (bf16[384,128]{1,0:T(8,128)(2,1)S(1)}, bf16[384,128]{1,0:T(8,128)(2,1)S(1)}, u32[]{:S(2)}, u32[]{:S(2)}) collective-permute-start(bf16[384,128]{1,0:T(8,128)(2,1)S(1)} %get-tuple-element.44.own), channel_id=1, source_target_pairs={{0,2},{1,3},{2,0},{3,1},{4,6},{5,7},{6,4},{7,5},{8,10},{9,11},{10,... | collective-permute-start | bytes 294920 | tf_op jit(solution)/shard_map/ppermute | solution.py:328
  45.2 13.0 %collective-permute-start.10 = (bf16[768,128]{1,0:T(8,128)(2,1)S(1)}, bf16[768,128]{1,0:T(8,128)(2,1)S(1)}, u32[]{:S(2)}, u32[]{:S(2)}) collective-permute-start(bf16[768,128]{1,0:T(8,128)(2,1)S(1)} %get-tuple-element.46), channel_id=1, source_target_pairs={{0,4},{4,0},{8,12},{12,8},{16,20},{20,16},{24,28},{28,24},{32,36},... | collective-permute-start | bytes 589832 | tf_op jit(solution)/shard_map/ppermute | solution.py:321
  45.3 12.9 %collective-permute-start.11 = (bf16[768,128]{1,0:T(8,128)(2,1)S(1)}, bf16[768,128]{1,0:T(8,128)(2,1)S(1)}, u32[]{:S(2)}, u32[]{:S(2)}) collective-permute-start(bf16[768,128]{1,0:T(8,128)(2,1)S(1)} %get-tuple-element.47), channel_id=1, source_target_pairs={{4,8},{8,4},{12,16},{16,12},{20,24},{24,20},{28,32},{32,28},{36,40... | collective-permute-start | bytes 589832 | tf_op jit(solution)/shard_map/ppermute | solution.py:321
  50.2 9.7 %collective-permute-start.12 = (bf16[768,128]{1,0:T(8,128)(2,1)S(1)}, bf16[768,128]{1,0:T(8,128)(2,1)S(1)}, u32[]{:S(2)}, u32[]{:S(2)}) collective-permute-start(bf16[768,128]{1,0:T(8,128)(2,1)S(1)} %get-tuple-element.48), channel_id=1, source_target_pairs={{8,16},{12,20},{16,8},{20,12},{24,32},{28,36},{32,24},{36,28},{40,... | collective-permute-start | bytes 589832 | tf_op jit(solution)/shard_map/ppermute | solution.py:321
  54.2 5.8 %collective-permute-start.13 = (bf16[768,128]{1,0:T(8,128)(2,1)S(1)}, bf16[768,128]{1,0:T(8,128)(2,1)S(1)}, u32[]{:S(2)}, u32[]{:S(2)}) collective-permute-start(bf16[768,128]{1,0:T(8,128)(2,1)S(1)} %get-tuple-element.49), channel_id=1, source_target_pairs={{0,8},{4,12},{8,0},{12,4},{16,24},{20,28},{24,16},{28,20},{32,40},... | collective-permute-start | bytes 589832 | tf_op jit(solution)/shard_map/ppermute | solution.py:321
  65.2 5.2 %collective-permute-start.14 = (bf16[384,128]{1,0:T(8,128)(2,1)S(1)}, bf16[384,128]{1,0:T(8,128)(2,1)S(1)}, u32[]{:S(2)}, u32[]{:S(2)}) collective-permute-start(bf16[384,128]{1,0:T(8,128)(2,1)S(1)} %get-tuple-element.51), channel_id=1, source_target_pairs={{0,1},{1,0},{2,3},{3,2},{4,5},{5,4},{6,7},{7,6},{8,9},{9,8},{10,11... | collective-permute-start | bytes 294920 | tf_op jit(solution)/shard_map/ppermute | solution.py:328
  65.9 5.8 %collective-permute-start.15 = (bf16[384,128]{1,0:T(8,128)(2,1)S(1)}, bf16[384,128]{1,0:T(8,128)(2,1)S(1)}, u32[]{:S(2)}, u32[]{:S(2)}) collective-permute-start(bf16[384,128]{1,0:T(8,128)(2,1)S(1)} %get-tuple-element.52), channel_id=1, source_target_pairs={{0,3},{1,2},{2,1},{3,0},{4,7},{5,6},{6,5},{7,4},{8,11},{9,10},{10,... | collective-permute-start | bytes 294920 | tf_op jit(solution)/shard_map/ppermute | solution.py:328
  68.1 6.1 %collective-permute-start.16 = (bf16[384,128]{1,0:T(8,128)(2,1)S(1)}, bf16[384,128]{1,0:T(8,128)(2,1)S(1)}, u32[]{:S(2)}, u32[]{:S(2)}) collective-permute-start(bf16[384,128]{1,0:T(8,128)(2,1)S(1)} %get-tuple-element.53), channel_id=1, source_target_pairs={{0,2},{1,3},{2,0},{3,1},{4,6},{5,7},{6,4},{7,5},{8,10},{9,11},{10,... | collective-permute-start | bytes 294920 | tf_op jit(solution)/shard_map/ppermute | solution.py:328

commit v3 on v2

v3 whole, which is shorter than its diff:
```python
import jax
import jax.numpy as jnp
from jax import lax
from jax.experimental import pallas as pl
from jax.experimental.pallas import tpu as pltpu
from jax.sharding import PartitionSpec as P

NTR = 12
BS = 128
NBD = 128
CAP = 64
REP = 4
SHARE = NBD // REP
LIST_ROWS = CAP * NTR
LABEL_ROWS = 16
SHARE_ROWS = SHARE * NTR
F32 = jnp.float32
BF16 = jnp.bfloat16
I32 = jnp.int32
MIB = 1 << 20

VMEM = pl.BlockSpec(memory_space=pltpu.VMEM)
HBM = pl.BlockSpec(memory_space=pltpu.HBM)


def nt(a, b):
    return lax.dot_general(a, b, (((1,), (1,)), ((), ())), preferred_element_type=F32)


def pack4(tiles):
    return jnp.concatenate([t[0:8] for t in tiles] + [t[8:12] for t in tiles], axis=0)


def unpack4(rows):
    return [
        jnp.concatenate([rows[8 * m : 8 * m + 8], rows[32 + 4 * m : 36 + 4 * m]], axis=0)
        for m in range(4)
    ]


def tile16(t):
    return jnp.concatenate([t, jnp.zeros((4, BS), F32)], axis=0).astype(BF16)


def route_lanes():
    me = lax.axis_index("blk")
    core = me & 1
    odd = lax.shift_right_logical(me, 1) & 1
    return (2 - core, 1 + core, 3 * odd, 3 - 3 * odd)


def message_spots(pieces, espots_ref, ispots_ref):
    me = lax.axis_index("blk")
    core = me & 1
    odd = lax.shift_right_logical(me, 1) & 1
    sub = lax.broadcasted_iota(I32, (BS, BS), 0).astype(F32)
    spot = lax.broadcasted_iota(I32, (8, BS), 1)
    kind = lax.broadcasted_iota(I32, (8, BS), 0)
    spot = jnp.where(lax.shift_right_logical(spot, 6) == kind, spot & (CAP - 1), 0)
    spot = spot.astype(F32).astype(BF16)
    for n, row in enumerate((3 - 2 * core, 1 + 2 * core, 4 * odd, 4 - 4 * odd)):
        labels = pieces[n][LIST_ROWS : LIST_ROWS + LABEL_ROWS, :].astype(F32)[0:1]
        listed = jnp.where(sub == labels, 1.0, 0.0).astype(BF16)
        found = nt(spot, listed).astype(I32) + n * CAP
        espots_ref[pl.ds(row, 1), :] = found[0:1]
        ispots_ref[pl.ds(row, 1), :] = found[1:2]


def gather_lists(order_ref, load_tile, out_refs):
    for lane_no, out_ref in zip(route_lanes(), out_refs):

        def group(g, _, lane_no=lane_no, out_ref=out_ref):
            tiles = [load_tile(jnp.maximum(order_ref[lane_no, 4 * g + m], 0)) for m in range(4)]
            rows = pl.ds(pl.multiple_of(48 * g, 16), 48)
            out_ref[rows, :] = pack4(tiles).astype(BF16)
            return 0

        lax.fori_loop(0, CAP // 4, group, 0, unroll=4)


def fetch(pairs, sems):
    copies = [pltpu.make_async_copy(src, dst, sems.at[n]) for n, (src, dst) in enumerate(pairs)]
    for copy in copies:
        copy.start()
    return copies


def first_kernel(esends_ref, isends_ref, tracers_ref, *rest):
    outs = rest[0:4]
    esends_v, isends_v, esends_s, tracers_v, sems = rest[4:]
    copies = fetch([(esends_ref, esends_s), (tracers_ref, tracers_v),
                    (esends_ref, esends_v), (isends_ref, isends_v)], sems)
    for copy in copies:
        copy.wait()
    for lane_no, out_ref in zip(route_lanes(), outs):
        row = pl.ds(lane_no, 1)
        labels = jnp.concatenate([esends_v[row, :], isends_v[row, :]], axis=1).astype(F32)
        out_ref[LIST_ROWS : LIST_ROWS + LABEL_ROWS, :] = jnp.broadcast_to(labels, (LABEL_ROWS, BS)).astype(BF16)

    def load_tile(i):
        return tracers_v[:, pl.ds(pl.multiple_of(i * BS, BS), BS)]

    gather_lists(esends_s, load_tile, outs)


def fetch_blocks(blocks_ref, near_ref, far_ref, sems):
    rows = [pl.ds(q * SHARE, SHARE) for q in range(REP)]
    return fetch([(blocks_ref.at[r, pl.ds(0, 1)], near_ref.at[r]) for r in rows]
                 + [(blocks_ref.at[r, pl.ds(1, 2)], far_ref.at[r]) for r in rows], sems)


def local_groups(copies, cols_s, load_tile, near_ref, out_ref):
    base = lax.axis_index("blk") * NBD
    for q in range(REP):
        copies[q].wait()

        def group(g, _):
            tiles = []
            for pair in range(2):
                bs = [4 * g + 2 * pair + half for half in range(2)]
                x = jnp.concatenate([load_tile(cols_s[0, b] - base) for b in bs], axis=0)
                w = jnp.concatenate([near_ref[b, 0] for b in bs], axis=0)
                y = nt(x, w)
                tiles += [y[0:16, 0:BS], y[16:32, BS:]]
            out_ref[pl.ds(pl.multiple_of(48 * g, 16), 48), :] = pack4(tiles)
            return 0

        lax.fori_loop(q * SHARE // 4, (q + 1) * SHARE // 4, group, 0, unroll=True)
    for copy in copies[REP:]:
        copy.wait()


def first_local_kernel(cols_ref, tracers_ref, wet_ref, coupling_ref, blocks_ref,
                       out_ref, far_ref, share_ref, wet_share_ref, coupling_out_ref,
                       wet_v, cols_s, tracers_v, near_ref, sems, block_sems):
    me = lax.axis_index("rep")
    cells = SHARE * BS
    copies = fetch([
        (cols_ref, cols_s), (tracers_ref, tracers_v),
        (tracers_ref.at[:, pl.ds(pl.multiple_of(me * cells, cells), cells)], share_ref),
        (wet_ref.at[pl.ds(pl.multiple_of(me * SHARE, SHARE), SHARE)], wet_v),
        (coupling_ref, coupling_out_ref),
    ], sems)
    block_copies = fetch_blocks(blocks_ref, near_ref, far_ref, block_sems)
    for copy in copies:
        copy.wait()
    wet_share_ref[...] = wet_v[...].astype(F32)

    def load_tile(i):
        return tile16(tracers_v[:, pl.ds(pl.multiple_of(i * BS, BS), BS)])

    local_groups(block_copies, cols_s, load_tile, near_ref, out_ref)


def second_local_kernel(cols_ref, table_ref, blocks_ref, out_ref, far_ref, cols_s, near_ref, sems, block_sems):
    copies = fetch([(cols_ref, cols_s)], sems)
    block_copies = fetch_blocks(blocks_ref, near_ref, far_ref, block_sems)
    copies[0].wait()
    local_groups(block_copies, cols_s, lambda i: table_ref[i], near_ref, out_ref)


def remote_groups(cols_ref, spots_ref, local_ref, far_ref, pieces, outs, cols_s, spots_s, table_ref, sems):
    me = lax.axis_index("rep")
    first_block = (lax.axis_index("blk") - 2) * NBD
    copies = fetch([(cols_ref, cols_s), (spots_ref, spots_s)], sems)

    for lane_no, piece in enumerate(pieces):

        def spread(g, _, lane_no=lane_no, piece=piece):
            rows = piece[pl.ds(pl.multiple_of(48 * g, 16), 48), :].astype(F32)
            for m, tile in enumerate(unpack4(rows)):
                table_ref[lane_no * CAP + 4 * g + m] = tile16(tile)
            return 0

        lax.fori_loop(0, CAP // 4, spread, 0, unroll=4)

    def tile(k, b):
        c = cols_s[k, b] - first_block
        return table_ref[spots_s[lax.shift_right_logical(c, 7), c & (NBD - 1)]]

    for copy in copies:
        copy.wait()
    for step, out_ref in enumerate(outs):
        share = me ^ step

        def group(g, _, out_ref=out_ref, share=share):
            tiles = []
            for pair in range(2):
                bs = [share * SHARE + 4 * g + 2 * pair + half for half in range(2)]
                x = [jnp.concatenate([tile(1, b), tile(2, b)], axis=1) for b in bs]
                w = [jnp.concatenate([far_ref[b, 0], far_ref[b, 1]], axis=1) for b in bs]
                y = nt(jnp.concatenate(x, axis=0), jnp.concatenate(w, axis=0))
                tiles += [y[0:16, 0:BS], y[16:32, BS:]]
            there = pl.ds(pl.multiple_of((share * (SHARE // 4) + g) * 48, 16), 48)
            total = pack4(tiles) + local_ref[there, :]
            out_ref[pl.ds(pl.multiple_of(48 * g, 16), 48), :] = total.astype(out_ref.dtype)
            return 0

        lax.fori_loop(0, SHARE // 4, group, 0, unroll=True)


def first_remote_kernel(cols_ref, local_ref, far_ref, p0, p1, p2, p3, own_ref, o1, o2, o3, ispots_ref,
                        cols_s, spots_s, table_ref, spots_v, sems):
    pieces = (p0, p1, p2, p3)
    spots_v[...] = jnp.zeros((8, BS), I32)
    ispots_ref[...] = jnp.zeros((8, BS), I32)
    message_spots(pieces, spots_v, ispots_ref)
    remote_groups(cols_ref, spots_v, local_ref, far_ref, pieces, (own_ref, o1, o2, o3),
                  cols_s, spots_s, table_ref, sems)


def second_remote_kernel(cols_ref, local_ref, far_ref, p0, p1, p2, p3, spots_ref, own_ref, o1, o2, o3,
                         cols_s, spots_s, table_ref, sems):
    remote_groups(cols_ref, spots_ref, local_ref, far_ref, (p0, p1, p2, p3), (own_ref, o1, o2, o3),
                  cols_s, spots_s, table_ref, sems)


def middle_kernel(own_ref, g1, g2, g3, share_ref, coupling_ref, wet_ref,
                  before_ref, packed_ref, mid_ref):
    for g in range(SHARE // 4):
        rows = pl.ds(48 * g, 48)
        total = own_ref[rows, :] + g1[rows, :].astype(F32) + g2[rows, :].astype(F32) + g3[rows, :].astype(F32)
        for m, tile in enumerate(unpack4(total)):
            lanes = pl.ds((4 * g + m) * BS, BS)
            mid_ref[:, lanes] = share_ref[:, lanes] + tile
    pushed = lax.dot_general(coupling_ref[...], mid_ref[...], (((1,), (0,)), ((), ())),
                             precision=lax.Precision.HIGHEST, preferred_element_type=F32)
    for g in range(SHARE // 4):
        tiles = []
        for m in range(4):
            b = 4 * g + m
            lanes = pl.ds(b * BS, BS)
            tile = mid_ref[:, lanes] + wet_ref[b : b + 1, :] * jnp.tanh(pushed[:, b * BS : (b + 1) * BS])
            before_ref[:, lanes] = tile
            tiles.append(tile)
        packed_ref[pl.ds(48 * g, 48), :] = pack4(tiles).astype(BF16)


def second_kernel(sends_ref, own, g2, g3, g1, *rest):
    outs, table_ref, sends_s, sems = rest[0:4], rest[4], rest[5], rest[6]
    copies = fetch([(sends_ref, sends_s)], sems)
    me = lax.axis_index("rep")
    for step, packed in ((0, own), (2, g2), (3, g3), (1, g1)):
        share = me ^ step

        def spread(g, _, packed=packed, share=share):
            rows = packed[pl.ds(pl.multiple_of(48 * g, 16), 48), :].astype(F32)
            for m, tile in enumerate(unpack4(rows)):
                table_ref[share * SHARE + 4 * g + m] = tile16(tile)
            return 0

        lax.fori_loop(0, SHARE // 4, spread, 0, unroll=4)
    copies[0].wait()
    gather_lists(sends_s, lambda i: table_ref[i].astype(F32), outs)


def last_kernel(own_ref, g1, g2, g3, before_ref, wet_ref, out_ref):
    for g in range(SHARE // 4):
        rows = pl.ds(48 * g, 48)
        total = own_ref[rows, :] + g1[rows, :].astype(F32) + g2[rows, :].astype(F32) + g3[rows, :].astype(F32)
        for m, tile in enumerate(unpack4(total)):
            b = 4 * g + m
            lanes = pl.ds(b * BS, BS)
            out_ref[:, lanes] = wet_ref[b : b + 1, :] * (before_ref[:, lanes] + tile)


def sds(shape, dtype):
    return jax.ShapeDtypeStruct(shape, dtype)


def call(body, outs, in_specs, scratch, name, mib, flops=0, bytes_accessed=0):
    kernel = pl.pallas_call(
        body,
        out_shape=outs,
        in_specs=in_specs,
        out_specs=jax.tree.map(lambda _: VMEM, outs),
        scratch_shapes=scratch,
        compiler_params=pltpu.CompilerParams(vmem_limit_bytes=mib * MIB),
        cost_estimate=pl.CostEstimate(flops=flops, bytes_accessed=bytes_accessed, transcendentals=0),
        name=name,
    )

    def run(*operands):
        return kernel(*(
            pltpu.with_memory_space_constraint(x, pltpu.HBM) if spec is HBM else x
            for x, spec in zip(operands, in_specs)))

    return run


def swap_blk(messages):
    n = lax.axis_size("blk")
    partners = (
        lambda i: i ^ 1,
        lambda i: i + 1 if i & 1 else i - 1,
        lambda i: i + 2 if i & 2 else i - 2,
        lambda i: i ^ 2,
    )
    return [
        lax.ppermute(x, "blk", [(i, to(i)) for i in range(n) if 0 <= to(i) < n])
        for x, to in zip(messages, partners)
    ]


def swap_rep(x, distance):
    n = lax.axis_size("rep")
    return lax.ppermute(x, "rep", [(i, i ^ distance) for i in range(n)])


def lists_out(label_rows):
    return [sds((LIST_ROWS + label_rows, BS), BF16)] * 4


def dma(n):
    return pltpu.SemaphoreType.DMA((n,))


FAR = pltpu.VMEM((NBD, 2, BS, BS), BF16)
NEAR = pltpu.VMEM((NBD, 1, BS, BS), BF16)
COLS = pltpu.SMEM((3, BS), I32)
SENDS = pltpu.SMEM((4, CAP), I32)


def on_device(tracers, explicit_blocks, explicit_cols, explicit_sends,
              implicit_blocks, implicit_cols, implicit_sends, coupling, wet):
    ecols, icols = explicit_cols.T, implicit_cols.T
    esends, isends = explicit_sends.reshape(4, CAP), implicit_sends.reshape(4, CAP)
    wet = wet.reshape(NBD, BS)
    cells = SHARE * BS
    ints = sds((8, BS), I32)
    sends_v = pltpu.VMEM((4, CAP), I32)
    local_sum = sds((NBD * NTR, BS), F32)
    part = sds((SHARE_ROWS, BS), BF16)
    parts_out = [sds((SHARE_ROWS, BS), F32), part, part, part]
    remote_scratch = [COLS, pltpu.SMEM((8, BS), I32), pltpu.VMEM((4 * CAP, 16, BS), BF16)]

    outbound = call(
        first_kernel, lists_out(LABEL_ROWS), [HBM] * 3,
        [sends_v, sends_v, SENDS, pltpu.VMEM((NTR, NBD * BS), F32), dma(4)],
        "first_lists", 16,
    )(esends, isends, tracers)
    pieces = swap_blk(outbound)
    local, far, share, wet_share, coupling = call(
        first_local_kernel,
        [local_sum, FAR, sds((NTR, cells), F32), sds((SHARE, BS), F32), sds((NTR, NTR), F32)], [HBM] * 5,
        [pltpu.VMEM((SHARE, BS), I32), COLS, pltpu.VMEM((NTR, NBD * BS), F32), NEAR, dma(5), dma(2 * REP)],
        "first_local_product", 24, flops=50_000_000, bytes_accessed=13_000_000,
    )(ecols, tracers, wet, coupling, explicit_blocks)
    own, *parts, ispots = call(
        first_remote_kernel, parts_out + [ints], [HBM] + [VMEM] * 6,
        remote_scratch + [pltpu.VMEM((8, BS), I32), dma(2)],
        "first_remote_product", 16, flops=100_000_000, bytes_accessed=1_000_000,
    )(ecols, local, far, *pieces)
    got = [swap_rep(parts[k - 1], k) for k in (1, 3, 2)]
    before, packed = call(
        middle_kernel, [sds((NTR, cells), F32), part], [VMEM] * 7, [pltpu.VMEM((NTR, cells), F32)],
        "middle", 16,
    )(own, *got, share, coupling, wet_share)
    others = [swap_rep(packed, k) for k in (2, 3, 1)]
    *outbound, table = call(
        second_kernel, lists_out(0) + [sds((NBD, 16, BS), BF16)], [HBM] + [VMEM] * 4, [SENDS, dma(1)],
        "second_lists", 16,
    )(isends, packed, *others)
    pieces = swap_blk(outbound)
    local, far = call(
        second_local_kernel, [local_sum, FAR], [HBM, VMEM, HBM], [COLS, NEAR, dma(1), dma(2 * REP)],
        "second_local_product", 24, flops=50_000_000, bytes_accessed=13_000_000,
    )(icols, table, implicit_blocks)
    own, *parts = call(
        second_remote_kernel, parts_out, [HBM] + [VMEM] * 7, remote_scratch + [dma(2)],
        "second_remote_product", 16, flops=100_000_000, bytes_accessed=1_000_000,
    )(icols, local, far, *pieces, ispots)
    got = [swap_rep(parts[k - 1], k) for k in (1, 3, 2)]
    return call(
        last_kernel, sds((NTR, cells), F32), [VMEM] * 6, [], "last", 16,
    )(own, *got, before, wet_share)


def solution(mesh):
    in_specs = (
        P(None, "blk"),
        P("blk", "rep", None, None),
        P("blk", "rep"),
        P("blk", "rep", None, None),
        P("blk", "rep", None, None),
        P("blk", "rep"),
        P("blk", "rep", None, None),
        P(),
        P("blk"),
    )
    out_specs = P(None, ("blk", "rep"))
    return jax.shard_map(
        on_device, mesh=mesh, in_specs=in_specs, out_specs=out_specs, check_vma=False
    )
```

time: 75.3 us -> 69.9 us (0.928)
  Pallas kernels: 27.8 us -> 22.9 us
    pallas_call x8, Pallas kernels: 27.8 us -> 22.9 us  [run(): kernel(*(pltpu.with_memory_space_constraint(x, pltpu.HBM) if spec is HBM...]
  transfers between devices with their start and end apart: 17 -> 17, of which waited for: 9 -> 10; matrix products, arithmetic and copies ran while one was open for 0% -> 0% of each run, Pallas kernels for 14% -> 16%
where the time goes in v3:
time: 69.9 us; the launch traced here: 69.6 us
  starting transfers between devices  31 us (44%)
  Pallas kernels  22.9 us (33%)
  waiting for transfers between devices  15.5 us (22%)
    pallas_call x8, Pallas kernels, run(): kernel(*(pltpu.with_memory_space_constraint(x, pltpu.HBM) if spec is HBM...  22.9 us
    ppermute x8, starting transfers between devices, swap_blk(): lax.ppermute(x, 'blk', [(i, to(i)) for i in range(n) if 0 <= to(i) < n])  17 us
    ppermute x9, starting transfers between devices, swap_rep(): return lax.ppermute(x, 'rep', [(i, i ^ distance) for i in range(n)])  13.9 us
    ppermute x9, waiting for transfers between devices, swap_rep(): return lax.ppermute(x, 'rep', [(i, i ^ distance) for i in range(n)])  13.7 us
    ppermute x8, waiting for transfers between devices, swap_blk(): lax.ppermute(x, 'blk', [(i, to(i)) for i in range(n) if 0 <= to(i) < n])  1.8 us
  transfers between devices with their start and end apart: 17, of which 10 were waited for; matrix products, arithmetic and copies ran while one was open for 0% of the time, Pallas kernels for 16%

profile of v3, /device:TPU:6, one launch (start us, length us, event | category | flops | bytes accessed | tf_op | source)
XLA Modules:
  0.0 69.6 jit_solution(17245290985080634851)
XLA Ops:
  0.0 2.4 %first_lists.1 = (bf16[784,128]{1,0:T(8,128)(2,1)S(1)}, bf16[784,128]{1,0:T(8,128)(2,1)S(1)}, bf16[784,128]{1,0:T(8,128)(2,1)S(1)}, bf16[784,128]{1,0:T(8,128)(2,1)S(1)}) custom-call(s32[4,64]{1,0:T(4,128)} %bitcast.12, s32[4,64]{1,0:T(4,128)} %bitcast.6, f32[12,16384]{1,0:T(8,128)} %tracers_ref.3), custom_call_target="tpu_custom_call" | custom-call | tf_op jit(solution)/shard_map/first_lists/pallas_call | solution.py:284
  2.4 0.1 collective-permute-start
  2.5 5.3 %collective-permute-start.1 = (bf16[784,128]{1,0:T(8,128)(2,1)S(1)}, bf16[784,128]{1,0:T(8,128)(2,1)S(1)}, u32[]{:S(2)}, u32[]{:S(2)}) collective-permute-start(bf16[784,128]{1,0:T(8,128)(2,1)S(1)} %get-tuple-element.35), channel_id=1, source_target_pairs={{4,8},{8,4},{12,16},{16,12},{20,24},{24,20},{28,32},{32,28},{36,40... | collective-permute-start | bytes 602120 | tf_op jit(solution)/shard_map/ppermute | solution.py:300
  7.8 2.7 %collective-permute-start.2 = (bf16[784,128]{1,0:T(8,128)(2,1)S(1)}, bf16[784,128]{1,0:T(8,128)(2,1)S(1)}, u32[]{:S(2)}, u32[]{:S(2)}) collective-permute-start(bf16[784,128]{1,0:T(8,128)(2,1)S(1)} %get-tuple-element.36), channel_id=1, source_target_pairs={{8,16},{12,20},{16,8},{20,12},{24,32},{28,36},{32,24},{36,28},{40,... | collective-permute-start | bytes 602120 | tf_op jit(solution)/shard_map/ppermute | solution.py:300
  10.5 0.1 collective-permute-start.3
  10.6 6.2 %first_local_product.1 = (f32[1536,128]{1,0:T(8,128)S(1)}, bf16[128,2,128,128]{3,2,1,0:T(8,128)(2,1)S(1)}, f32[12,4096]{1,0:T(8,128)S(1)}, f32[32,128]{1,0:T(8,128)S(1)}, f32[12,12]{1,0:T(8,128)S(1)}) custom-call(s32[3,128]{1,0:T(4,128)} %bitcast.8, f32[12,16384]{1,0:T(8,128)} %tracers_ref.3, s32[128,128]{1,0:T(8,128)} %bitcast.5, f32[12,12]{1,0:T(8,128)} %coupling_ref.1, ...), custom_call_target="tpu_custom_call" | custom-call | flops 50000000 | bytes 13000000 | tf_op jit(solution)/shard_map/first_local_product/pallas_call | solution.py:284
  16.7 0.0 collective-permute-done.p0
  16.8 0.0 collective-permute-done.1.p1
  16.8 0.8 %collective-permute-done.2.p2 = bf16[784,128]{1,0:T(8,128)(2,1)S(1)} collective-permute-done((bf16[784,128]{1,0:T(8,128)(2,1)S(1)}, bf16[784,128]{1,0:T(8,128)(2,1)S(1)}, u32[]{:S(2)}, u32[]{:S(2)}) %collective-permute-start.2) | collective-permute-done | bytes 200736 | tf_op jit(solution)/shard_map/ppermute | solution.py:300
  17.5 0.0 collective-permute-done.3.p3
  17.5 3.4 %first_remote_product.1 = (f32[384,128]{1,0:T(8,128)S(1)}, bf16[384,128]{1,0:T(8,128)(2,1)S(1)}, bf16[384,128]{1,0:T(8,128)(2,1)S(1)}, bf16[384,128]{1,0:T(8,128)(2,1)S(1)}, s32[8,128]{1,0:T(8,128)S(1)}) custom-call(s32[3,128]{1,0:T(4,128)} %bitcast.9, f32[1536,128]{1,0:T(8,128)S(1)} %get-tuple-element.32.local_ref, ...), custom_call_target="tpu_custom_call" | custom-call | flops 100000000 | bytes 1000000 | tf_op jit(solution)/shard_map/first_remote_product/pallas_call | solution.py:284
  20.9 2.0 %collective-permute-start.4 = (bf16[384,128]{1,0:T(8,128)(2,1)S(1)}, bf16[384,128]{1,0:T(8,128)(2,1)S(1)}, u32[]{:S(2)}, u32[]{:S(2)}) collective-permute-start(bf16[384,128]{1,0:T(8,128)(2,1)S(1)} %get-tuple-element.39), channel_id=1, source_target_pairs={{0,1},{1,0},{2,3},{3,2},{4,5},{5,4},{6,7},{7,6},{8,9},{9,8},{10,11... | collective-permute-start | bytes 294920 | tf_op jit(solution)/shard_map/ppermute | solution.py:307
  22.9 2.5 %collective-permute-start.5 = (bf16[384,128]{1,0:T(8,128)(2,1)S(1)}, bf16[384,128]{1,0:T(8,128)(2,1)S(1)}, u32[]{:S(2)}, u32[]{:S(2)}) collective-permute-start(bf16[384,128]{1,0:T(8,128)(2,1)S(1)} %get-tuple-element.40), channel_id=1, source_target_pairs={{0,3},{1,2},{2,1},{3,0},{4,7},{5,6},{6,5},{7,4},{8,11},{9,10},{10,... | collective-permute-start | bytes 294920 | tf_op jit(solution)/shard_map/ppermute | solution.py:307
  25.4 1.1 %collective-permute-start.6 = (bf16[384,128]{1,0:T(8,128)(2,1)S(1)}, bf16[384,128]{1,0:T(8,128)(2,1)S(1)}, u32[]{:S(2)}, u32[]{:S(2)}) collective-permute-start(bf16[384,128]{1,0:T(8,128)(2,1)S(1)} %get-tuple-element.41), channel_id=1, source_target_pairs={{0,2},{1,3},{2,0},{3,1},{4,6},{5,7},{6,4},{7,5},{8,10},{9,11},{10,... | collective-permute-start | bytes 294920 | tf_op jit(solution)/shard_map/ppermute | solution.py:307
  26.5 0.0 collective-permute-done.4.g1
  26.5 2.9 %collective-permute-done.5.g2 = bf16[384,128]{1,0:T(8,128)(2,1)S(1)} collective-permute-done((bf16[384,128]{1,0:T(8,128)(2,1)S(1)}, bf16[384,128]{1,0:T(8,128)(2,1)S(1)}, u32[]{:S(2)}, u32[]{:S(2)}) %collective-permute-start.5) | collective-permute-done | bytes 98336 | tf_op jit(solution)/shard_map/ppermute | solution.py:307
  29.4 2.2 %collective-permute-done.6.g3 = bf16[384,128]{1,0:T(8,128)(2,1)S(1)} collective-permute-done((bf16[384,128]{1,0:T(8,128)(2,1)S(1)}, bf16[384,128]{1,0:T(8,128)(2,1)S(1)}, u32[]{:S(2)}, u32[]{:S(2)}) %collective-permute-start.6) | collective-permute-done | bytes 98336 | tf_op jit(solution)/shard_map/ppermute | solution.py:307
  31.5 0.5 middle.1
  32.0 1.1 %collective-permute-start.9 = (bf16[384,128]{1,0:T(8,128)(2,1)S(1)}, bf16[384,128]{1,0:T(8,128)(2,1)S(1)}, u32[]{:S(2)}, u32[]{:S(2)}) collective-permute-start(bf16[384,128]{1,0:T(8,128)(2,1)S(1)} %get-tuple-element.45.own), channel_id=1, source_target_pairs={{0,1},{1,0},{2,3},{3,2},{4,5},{5,4},{6,7},{7,6},{8,9},{9,8},{10,11... | collective-permute-start | bytes 294920 | tf_op jit(solution)/shard_map/ppermute | solution.py:307
  33.1 0.6 collective-permute-start.8
  33.7 2.4 %collective-permute-start.7 = (bf16[384,128]{1,0:T(8,128)(2,1)S(1)}, bf16[384,128]{1,0:T(8,128)(2,1)S(1)}, u32[]{:S(2)}, u32[]{:S(2)}) collective-permute-start(bf16[384,128]{1,0:T(8,128)(2,1)S(1)} %get-tuple-element.45.own), channel_id=1, source_target_pairs={{0,2},{1,3},{2,0},{3,1},{4,6},{5,7},{6,4},{7,5},{8,10},{9,11},{10,... | collective-permute-start | bytes 294920 | tf_op jit(solution)/shard_map/ppermute | solution.py:307
  36.2 0.9 %collective-permute-done.9.g1 = bf16[384,128]{1,0:T(8,128)(2,1)S(1)} collective-permute-done((bf16[384,128]{1,0:T(8,128)(2,1)S(1)}, bf16[384,128]{1,0:T(8,128)(2,1)S(1)}, u32[]{:S(2)}, u32[]{:S(2)}) %collective-permute-start.9) | collective-permute-done | bytes 98336 | tf_op jit(solution)/shard_map/ppermute | solution.py:307
  37.1 2.9 %collective-permute-done.8.g3 = bf16[384,128]{1,0:T(8,128)(2,1)S(1)} collective-permute-done((bf16[384,128]{1,0:T(8,128)(2,1)S(1)}, bf16[384,128]{1,0:T(8,128)(2,1)S(1)}, u32[]{:S(2)}, u32[]{:S(2)}) %collective-permute-start.8) | collective-permute-done | bytes 98336 | tf_op jit(solution)/shard_map/ppermute | solution.py:307
  40.0 0.0 collective-permute-done.7.g2
  40.0 1.7 %second_lists.1 = (bf16[768,128]{1,0:T(8,128)(2,1)S(1)}, bf16[768,128]{1,0:T(8,128)(2,1)S(1)}, bf16[768,128]{1,0:T(8,128)(2,1)S(1)}, bf16[768,128]{1,0:T(8,128)(2,1)S(1)}, bf16[128,16,128]{2,1,0:T(8,128)(2,1)S(1)}) custom-call(s32[4,64]{1,0:T(4,128)} %bitcast.7, bf16[384,128]{1,0:T(8,128)(2,1)S(1)} %get-tuple-element.45.own, ...), custom_call_target="tpu_custom_call" | custom-call | tf_op jit(solution)/shard_map/second_lists/pallas_call | solution.py:284
  41.7 0.1 collective-permute-start.10
  41.8 4.7 %collective-permute-start.11 = (bf16[768,128]{1,0:T(8,128)(2,1)S(1)}, bf16[768,128]{1,0:T(8,128)(2,1)S(1)}, u32[]{:S(2)}, u32[]{:S(2)}) collective-permute-start(bf16[768,128]{1,0:T(8,128)(2,1)S(1)} %get-tuple-element.50), channel_id=1, source_target_pairs={{4,8},{8,4},{12,16},{16,12},{20,24},{24,20},{28,32},{32,28},{36,40... | collective-permute-start | bytes 589832 | tf_op jit(solution)/shard_map/ppermute | solution.py:300
  46.5 4.0 %collective-permute-start.12 = (bf16[768,128]{1,0:T(8,128)(2,1)S(1)}, bf16[768,128]{1,0:T(8,128)(2,1)S(1)}, u32[]{:S(2)}, u32[]{:S(2)}) collective-permute-start(bf16[768,128]{1,0:T(8,128)(2,1)S(1)} %get-tuple-element.51), channel_id=1, source_target_pairs={{8,16},{12,20},{16,8},{20,12},{24,32},{28,36},{32,24},{36,28},{40,... | collective-permute-start | bytes 589832 | tf_op jit(solution)/shard_map/ppermute | solution.py:300
  50.6 0.1 collective-permute-start.13
  50.6 4.8 %second_local_product.1 = (f32[1536,128]{1,0:T(8,128)S(1)}, bf16[128,2,128,128]{3,2,1,0:T(8,128)(2,1)S(1)}) custom-call(s32[3,128]{1,0:T(4,128)} %bitcast.10, bf16[128,16,128]{2,1,0:T(8,128)(2,1)S(1)} %get-tuple-element.46.table_ref, bf16[128,3,128,128]{3,2,1,0:T(8,128)(2,1)} %blocks_ref.3), custom_call_target="tpu_custom_call" | custom-call | flops 50000000 | bytes 13000000 | tf_op jit(solution)/shard_map/second_local_product/pallas_call | solution.py:284
  55.4 0.0 collective-permute-done.10.p0
  55.4 0.0 collective-permute-done.11.p1
  55.4 0.7 %collective-permute-done.12.p2 = bf16[768,128]{1,0:T(8,128)(2,1)S(1)} collective-permute-done((bf16[768,128]{1,0:T(8,128)(2,1)S(1)}, bf16[768,128]{1,0:T(8,128)(2,1)S(1)}, u32[]{:S(2)}, u32[]{:S(2)}) %collective-permute-start.12) | collective-permute-done | bytes 196640 | tf_op jit(solution)/shard_map/ppermute | solution.py:300
  56.2 0.3 collective-permute-done.13.p3
  56.5 3.3 %second_remote_product.1 = (f32[384,128]{1,0:T(8,128)S(1)}, bf16[384,128]{1,0:T(8,128)(2,1)S(1)}, bf16[384,128]{1,0:T(8,128)(2,1)S(1)}, bf16[384,128]{1,0:T(8,128)(2,1)S(1)}) custom-call(s32[3,128]{1,0:T(4,128)} %bitcast.11, f32[1536,128]{1,0:T(8,128)S(1)} %get-tuple-element.47.local_ref, bf16[128,2,128,128]{3,2,1,0:T(8,128)(2,1)S(1)} %get-tuple-element.48.far_ref, ...), custom_call_target="tpu_custom_call" | custom-call | flops 100000000 | bytes 1000000 | tf_op jit(solution)/shard_map/second_remote_product/pallas_call | solution.py:284
  59.8 0.5 collective-permute-start.14
  60.2 2.5 %collective-permute-start.15 = (bf16[384,128]{1,0:T(8,128)(2,1)S(1)}, bf16[384,128]{1,0:T(8,128)(2,1)S(1)}, u32[]{:S(2)}, u32[]{:S(2)}) collective-permute-start(bf16[384,128]{1,0:T(8,128)(2,1)S(1)} %get-tuple-element.56), channel_id=1, source_target_pairs={{0,3},{1,2},{2,1},{3,0},{4,7},{5,6},{6,5},{7,4},{8,11},{9,10},{10,... | collective-permute-start | bytes 294920 | tf_op jit(solution)/shard_map/ppermute | solution.py:307
  62.7 1.2 %collective-permute-start.16 = (bf16[384,128]{1,0:T(8,128)(2,1)S(1)}, bf16[384,128]{1,0:T(8,128)(2,1)S(1)}, u32[]{:S(2)}, u32[]{:S(2)}) collective-permute-start(bf16[384,128]{1,0:T(8,128)(2,1)S(1)} %get-tuple-element.57), channel_id=1, source_target_pairs={{0,2},{1,3},{2,0},{3,1},{4,6},{5,7},{6,4},{7,5},{8,10},{9,11},{10,... | collective-permute-start | bytes 294920 | tf_op jit(solution)/shard_map/ppermute | solution.py:307
  63.9 0.8 %collective-permute-done.14.g1 = bf16[384,128]{1,0:T(8,128)(2,1)S(1)} collective-permute-done((bf16[384,128]{1,0:T(8,128)(2,1)S(1)}, bf16[384,128]{1,0:T(8,128)(2,1)S(1)}, u32[]{:S(2)}, u32[]{:S(2)}) %collective-permute-start.14) | collective-permute-done | bytes 98336 | tf_op jit(solution)/shard_map/ppermute | solution.py:307
  64.7 1.9 %collective-permute-done.15.g2 = bf16[384,128]{1,0:T(8,128)(2,1)S(1)} collective-permute-done((bf16[384,128]{1,0:T(8,128)(2,1)S(1)}, bf16[384,128]{1,0:T(8,128)(2,1)S(1)}, u32[]{:S(2)}, u32[]{:S(2)}) %collective-permute-start.15) | collective-permute-done | bytes 98336 | tf_op jit(solution)/shard_map/ppermute | solution.py:307
  66.7 2.1 %collective-permute-done.16.g3 = bf16[384,128]{1,0:T(8,128)(2,1)S(1)} collective-permute-done((bf16[384,128]{1,0:T(8,128)(2,1)S(1)}, bf16[384,128]{1,0:T(8,128)(2,1)S(1)}, u32[]{:S(2)}, u32[]{:S(2)}) %collective-permute-start.16) | collective-permute-done | bytes 98336 | tf_op jit(solution)/shard_map/ppermute | solution.py:307
  68.8 0.8 %last.1 = f32[12,4096]{1,0:T(8,128)} custom-call(f32[384,128]{1,0:T(8,128)S(1)} %get-tuple-element.54.own_ref, bf16[384,128]{1,0:T(8,128)(2,1)S(1)} %collective-permute-done.14.g1, bf16[384,128]{1,0:T(8,128)(2,1)S(1)} %collective-permute-done.15.g2, bf16[384,128]{1,0:T(8,128)(2,1)S(1)} %collective-permute-done.16.g3, ...), custom_call_target="tpu_custom_call" | custom-call | tf_op jit(solution)/shard_map/last/pallas_call | solution.py:284
Async XLA Ops:
  2.4 14.3 %collective-permute-start = (bf16[784,128]{1,0:T(8,128)(2,1)S(1)}, bf16[784,128]{1,0:T(8,128)(2,1)S(1)}, u32[]{:S(2)}, u32[]{:S(2)}) collective-permute-start(bf16[784,128]{1,0:T(8,128)(2,1)S(1)} %get-tuple-element.34), channel_id=1, source_target_pairs={{0,4},{4,0},{8,12},{12,8},{16,20},{20,16},{24,28},{28,24},{32,36},... | collective-permute-start | bytes 602120 | tf_op jit(solution)/shard_map/ppermute | solution.py:300
  2.5 14.2 %collective-permute-start.1 = (bf16[784,128]{1,0:T(8,128)(2,1)S(1)}, bf16[784,128]{1,0:T(8,128)(2,1)S(1)}, u32[]{:S(2)}, u32[]{:S(2)}) collective-permute-start(bf16[784,128]{1,0:T(8,128)(2,1)S(1)} %get-tuple-element.35), channel_id=1, source_target_pairs={{4,8},{8,4},{12,16},{16,12},{20,24},{24,20},{28,32},{32,28},{36,40... | collective-permute-start | bytes 602120 | tf_op jit(solution)/shard_map/ppermute | solution.py:300
  7.8 9.7 %collective-permute-start.2 = (bf16[784,128]{1,0:T(8,128)(2,1)S(1)}, bf16[784,128]{1,0:T(8,128)(2,1)S(1)}, u32[]{:S(2)}, u32[]{:S(2)}) collective-permute-start(bf16[784,128]{1,0:T(8,128)(2,1)S(1)} %get-tuple-element.36), channel_id=1, source_target_pairs={{8,16},{12,20},{16,8},{20,12},{24,32},{28,36},{32,24},{36,28},{40,... | collective-permute-start | bytes 602120 | tf_op jit(solution)/shard_map/ppermute | solution.py:300
  10.5 7.1 %collective-permute-start.3 = (bf16[784,128]{1,0:T(8,128)(2,1)S(1)}, bf16[784,128]{1,0:T(8,128)(2,1)S(1)}, u32[]{:S(2)}, u32[]{:S(2)}) collective-permute-start(bf16[784,128]{1,0:T(8,128)(2,1)S(1)} %get-tuple-element.37), channel_id=1, source_target_pairs={{0,8},{4,12},{8,0},{12,4},{16,24},{20,28},{24,16},{28,20},{32,40},... | collective-permute-start | bytes 602120 | tf_op jit(solution)/shard_map/ppermute | solution.py:300
  20.9 5.6 %collective-permute-start.4 = (bf16[384,128]{1,0:T(8,128)(2,1)S(1)}, bf16[384,128]{1,0:T(8,128)(2,1)S(1)}, u32[]{:S(2)}, u32[]{:S(2)}) collective-permute-start(bf16[384,128]{1,0:T(8,128)(2,1)S(1)} %get-tuple-element.39), channel_id=1, source_target_pairs={{0,1},{1,0},{2,3},{3,2},{4,5},{5,4},{6,7},{7,6},{8,9},{9,8},{10,11... | collective-permute-start | bytes 294920 | tf_op jit(solution)/shard_map/ppermute | solution.py:307
  22.9 6.5 %collective-permute-start.5 = (bf16[384,128]{1,0:T(8,128)(2,1)S(1)}, bf16[384,128]{1,0:T(8,128)(2,1)S(1)}, u32[]{:S(2)}, u32[]{:S(2)}) collective-permute-start(bf16[384,128]{1,0:T(8,128)(2,1)S(1)} %get-tuple-element.40), channel_id=1, source_target_pairs={{0,3},{1,2},{2,1},{3,0},{4,7},{5,6},{6,5},{7,4},{8,11},{9,10},{10,... | collective-permute-start | bytes 294920 | tf_op jit(solution)/shard_map/ppermute | solution.py:307
  25.4 6.1 %collective-permute-start.6 = (bf16[384,128]{1,0:T(8,128)(2,1)S(1)}, bf16[384,128]{1,0:T(8,128)(2,1)S(1)}, u32[]{:S(2)}, u32[]{:S(2)}) collective-permute-start(bf16[384,128]{1,0:T(8,128)(2,1)S(1)} %get-tuple-element.41), channel_id=1, source_target_pairs={{0,2},{1,3},{2,0},{3,1},{4,6},{5,7},{6,4},{7,5},{8,10},{9,11},{10,... | collective-permute-start | bytes 294920 | tf_op jit(solution)/shard_map/ppermute | solution.py:307
  32.0 5.1 %collective-permute-start.9 = (bf16[384,128]{1,0:T(8,128)(2,1)S(1)}, bf16[384,128]{1,0:T(8,128)(2,1)S(1)}, u32[]{:S(2)}, u32[]{:S(2)}) collective-permute-start(bf16[384,128]{1,0:T(8,128)(2,1)S(1)} %get-tuple-element.45.own), channel_id=1, source_target_pairs={{0,1},{1,0},{2,3},{3,2},{4,5},{5,4},{6,7},{7,6},{8,9},{9,8},{10,11... | collective-permute-start | bytes 294920 | tf_op jit(solution)/shard_map/ppermute | solution.py:307
  33.1 6.9 %collective-permute-start.8 = (bf16[384,128]{1,0:T(8,128)(2,1)S(1)}, bf16[384,128]{1,0:T(8,128)(2,1)S(1)}, u32[]{:S(2)}, u32[]{:S(2)}) collective-permute-start(bf16[384,128]{1,0:T(8,128)(2,1)S(1)} %get-tuple-element.45.own), channel_id=1, source_target_pairs={{0,3},{1,2},{2,1},{3,0},{4,7},{5,6},{6,5},{7,4},{8,11},{9,10},{10,... | collective-permute-start | bytes 294920 | tf_op jit(solution)/shard_map/ppermute | solution.py:307
  33.7 6.3 %collective-permute-start.7 = (bf16[384,128]{1,0:T(8,128)(2,1)S(1)}, bf16[384,128]{1,0:T(8,128)(2,1)S(1)}, u32[]{:S(2)}, u32[]{:S(2)}) collective-permute-start(bf16[384,128]{1,0:T(8,128)(2,1)S(1)} %get-tuple-element.45.own), channel_id=1, source_target_pairs={{0,2},{1,3},{2,0},{3,1},{4,6},{5,7},{6,4},{7,5},{8,10},{9,11},{10,... | collective-permute-start | bytes 294920 | tf_op jit(solution)/shard_map/ppermute | solution.py:307
  41.7 13.7 %collective-permute-start.10 = (bf16[768,128]{1,0:T(8,128)(2,1)S(1)}, bf16[768,128]{1,0:T(8,128)(2,1)S(1)}, u32[]{:S(2)}, u32[]{:S(2)}) collective-permute-start(bf16[768,128]{1,0:T(8,128)(2,1)S(1)} %get-tuple-element.49), channel_id=1, source_target_pairs={{0,4},{4,0},{8,12},{12,8},{16,20},{20,16},{24,28},{28,24},{32,36},... | collective-permute-start | bytes 589832 | tf_op jit(solution)/shard_map/ppermute | solution.py:300
  41.8 13.7 %collective-permute-start.11 = (bf16[768,128]{1,0:T(8,128)(2,1)S(1)}, bf16[768,128]{1,0:T(8,128)(2,1)S(1)}, u32[]{:S(2)}, u32[]{:S(2)}) collective-permute-start(bf16[768,128]{1,0:T(8,128)(2,1)S(1)} %get-tuple-element.50), channel_id=1, source_target_pairs={{4,8},{8,4},{12,16},{16,12},{20,24},{24,20},{28,32},{32,28},{36,40... | collective-permute-start | bytes 589832 | tf_op jit(solution)/shard_map/ppermute | solution.py:300
  46.5 9.7 %collective-permute-start.12 = (bf16[768,128]{1,0:T(8,128)(2,1)S(1)}, bf16[768,128]{1,0:T(8,128)(2,1)S(1)}, u32[]{:S(2)}, u32[]{:S(2)}) collective-permute-start(bf16[768,128]{1,0:T(8,128)(2,1)S(1)} %get-tuple-element.51), channel_id=1, source_target_pairs={{8,16},{12,20},{16,8},{20,12},{24,32},{28,36},{32,24},{36,28},{40,... | collective-permute-start | bytes 589832 | tf_op jit(solution)/shard_map/ppermute | solution.py:300
  50.6 5.9 %collective-permute-start.13 = (bf16[768,128]{1,0:T(8,128)(2,1)S(1)}, bf16[768,128]{1,0:T(8,128)(2,1)S(1)}, u32[]{:S(2)}, u32[]{:S(2)}) collective-permute-start(bf16[768,128]{1,0:T(8,128)(2,1)S(1)} %get-tuple-element.52), channel_id=1, source_target_pairs={{0,8},{4,12},{8,0},{12,4},{16,24},{20,28},{24,16},{28,20},{32,40},... | collective-permute-start | bytes 589832 | tf_op jit(solution)/shard_map/ppermute | solution.py:300
  59.8 5.0 %collective-permute-start.14 = (bf16[384,128]{1,0:T(8,128)(2,1)S(1)}, bf16[384,128]{1,0:T(8,128)(2,1)S(1)}, u32[]{:S(2)}, u32[]{:S(2)}) collective-permute-start(bf16[384,128]{1,0:T(8,128)(2,1)S(1)} %get-tuple-element.55), channel_id=1, source_target_pairs={{0,1},{1,0},{2,3},{3,2},{4,5},{5,4},{6,7},{7,6},{8,9},{9,8},{10,11... | collective-permute-start | bytes 294920 | tf_op jit(solution)/shard_map/ppermute | solution.py:307
  60.2 6.5 %collective-permute-start.15 = (bf16[384,128]{1,0:T(8,128)(2,1)S(1)}, bf16[384,128]{1,0:T(8,128)(2,1)S(1)}, u32[]{:S(2)}, u32[]{:S(2)}) collective-permute-start(bf16[384,128]{1,0:T(8,128)(2,1)S(1)} %get-tuple-element.56), channel_id=1, source_target_pairs={{0,3},{1,2},{2,1},{3,0},{4,7},{5,6},{6,5},{7,4},{8,11},{9,10},{10,... | collective-permute-start | bytes 294920 | tf_op jit(solution)/shard_map/ppermute | solution.py:307
  62.7 6.1 %collective-permute-start.16 = (bf16[384,128]{1,0:T(8,128)(2,1)S(1)}, bf16[384,128]{1,0:T(8,128)(2,1)S(1)}, u32[]{:S(2)}, u32[]{:S(2)}) collective-permute-start(bf16[384,128]{1,0:T(8,128)(2,1)S(1)} %get-tuple-element.57), channel_id=1, source_target_pairs={{0,2},{1,3},{2,0},{3,1},{4,6},{5,7},{6,4},{7,5},{8,10},{9,11},{10,... | collective-permute-start | bytes 294920 | tf_op jit(solution)/shard_map/ppermute | solution.py:307

commit v4 on v3

--- a/solution.py
+++ b/solution.py
@@ -14,6 +14,11 @@
 LIST_ROWS = CAP * NTR
 LABEL_ROWS = 16
 SHARE_ROWS = SHARE * NTR
+FIRST_ORDER = (2, 3, 1, 0)
+SECOND_ORDER = (2, 3, 1, 0)
+FIRST_SUM = (2, 3, 1)
+SECOND_SUM = (2, 3, 1)
+GATHER = (1, 3, 2)
 F32 = jnp.float32
 BF16 = jnp.bfloat16
 I32 = jnp.int32
@@ -75,7 +80,7 @@
             out_ref[rows, :] = pack4(tiles).astype(BF16)
             return 0
 
-        lax.fori_loop(0, CAP // 4, group, 0, unroll=4)
+        lax.fori_loop(0, CAP // 4, group, 0, unroll=True)
 
 
 def fetch(pairs, sems):
@@ -103,35 +108,52 @@
     gather_lists(esends_s, load_tile, outs)
 
 
+def share_rows(n):
+    return pl.ds(n * SHARE, SHARE)
+
+
+STEPS = (1, 2, 3)
+
+
 def fetch_blocks(blocks_ref, near_ref, far_ref, sems):
-    rows = [pl.ds(q * SHARE, SHARE) for q in range(REP)]
-    return fetch([(blocks_ref.at[r, pl.ds(0, 1)], near_ref.at[r]) for r in rows]
-                 + [(blocks_ref.at[r, pl.ds(1, 2)], far_ref.at[r]) for r in rows], sems)
+    me = lax.axis_index("rep")
+    rows = [(share_rows(me ^ step), share_rows(n)) for n, step in enumerate(STEPS)]
+    return fetch([(blocks_ref.at[r, pl.ds(0, 1)], near_ref.at[to]) for r, to in rows]
+                 + [(blocks_ref.at[r, pl.ds(1, 2)], far_ref.at[to]) for r, to in rows], sems)
+
+
+def packed_rows(n, g):
+    return pl.ds(pl.multiple_of(n * SHARE_ROWS + 48 * g, 16), 48)
 
 
 def local_groups(copies, cols_s, load_tile, near_ref, out_ref):
+    me = lax.axis_index("rep")
     base = lax.axis_index("blk") * NBD
-    for q in range(REP):
-        copies[q].wait()
-
-        def group(g, _):
+    for n, step in enumerate(STEPS):
+        copies[n].wait()
+
+        def group(g, _, n=n, step=step):
             tiles = []
             for pair in range(2):
-                bs = [4 * g + 2 * pair + half for half in range(2)]
-                x = jnp.concatenate([load_tile(cols_s[0, b] - base) for b in bs], axis=0)
-                w = jnp.concatenate([near_ref[b, 0] for b in bs], axis=0)
-                y = nt(x, w)
+                rows = [4 * g + 2 * pair + half for half in range(2)]
+                x = [load_tile(cols_s[0, (me ^ step) * SHARE + row] - base) for row in rows]
+                w = [near_ref[n * SHARE + row, 0] for row in rows]
+                y = nt(jnp.concatenate(x, axis=0), jnp.concatenate(w, axis=0))
                 tiles += [y[0:16, 0:BS], y[16:32, BS:]]
-            out_ref[pl.ds(pl.multiple_of(48 * g, 16), 48), :] = pack4(tiles)
+            out_ref[packed_rows(n, g), :] = pack4(tiles)
             return 0
 
-        lax.fori_loop(q * SHARE // 4, (q + 1) * SHARE // 4, group, 0, unroll=True)
-    for copy in copies[REP:]:
-        copy.wait()
+        lax.fori_loop(0, SHARE // 4, group, 0, unroll=True)
+    for copy in copies[len(STEPS):]:
+        copy.wait()
+
+
+def tracer_tile(tracers_v):
+    return lambda i: tile16(tracers_v[:, pl.ds(pl.multiple_of(i * BS, BS), BS)])
 
 
 def first_local_kernel(cols_ref, tracers_ref, wet_ref, coupling_ref, blocks_ref,
-                       out_ref, far_ref, share_ref, wet_share_ref, coupling_out_ref,
+                       out_ref, far_ref, cols_v, share_ref, wet_share_ref, coupling_out_ref,
                        wet_v, cols_s, tracers_v, near_ref, sems, block_sems):
     me = lax.axis_index("rep")
     cells = SHARE * BS
@@ -139,29 +161,36 @@
         (cols_ref, cols_s), (tracers_ref, tracers_v),
         (tracers_ref.at[:, pl.ds(pl.multiple_of(me * cells, cells), cells)], share_ref),
         (wet_ref.at[pl.ds(pl.multiple_of(me * SHARE, SHARE), SHARE)], wet_v),
-        (coupling_ref, coupling_out_ref),
+        (coupling_ref, coupling_out_ref), (cols_ref, cols_v),
     ], sems)
     block_copies = fetch_blocks(blocks_ref, near_ref, far_ref, block_sems)
     for copy in copies:
         copy.wait()
     wet_share_ref[...] = wet_v[...].astype(F32)
-
-    def load_tile(i):
-        return tile16(tracers_v[:, pl.ds(pl.multiple_of(i * BS, BS), BS)])
-
-    local_groups(block_copies, cols_s, load_tile, near_ref, out_ref)
-
-
-def second_local_kernel(cols_ref, table_ref, blocks_ref, out_ref, far_ref, cols_s, near_ref, sems, block_sems):
-    copies = fetch([(cols_ref, cols_s)], sems)
+    local_groups(block_copies, cols_s, tracer_tile(tracers_v), near_ref, out_ref)
+
+
+def second_local_kernel(cols_ref, table_ref, blocks_ref, out_ref, far_ref, cols_v,
+                        cols_s, near_ref, sems, block_sems):
+    copies = fetch([(cols_ref, cols_s), (cols_ref, cols_v)], sems)
     block_copies = fetch_blocks(blocks_ref, near_ref, far_ref, block_sems)
-    copies[0].wait()
+    for copy in copies:
+        copy.wait()
     local_groups(block_copies, cols_s, lambda i: table_ref[i], near_ref, out_ref)
 
 
-def remote_groups(cols_ref, spots_ref, local_ref, far_ref, pieces, outs, cols_s, spots_s, table_ref, sems):
-    me = lax.axis_index("rep")
+def remote_tile(cols_s, spots_s, table_ref):
     first_block = (lax.axis_index("blk") - 2) * NBD
+
+    def tile(k, b):
+        c = cols_s[k, b] - first_block
+        return table_ref[spots_s[lax.shift_right_logical(c, 7), c & (NBD - 1)]]
+
+    return tile
+
+
+def remote_groups(cols_ref, spots_ref, local_ref, far_ref, pieces, outs, table_ref, cols_s, spots_s, sems):
+    me = lax.axis_index("rep")
     copies = fetch([(cols_ref, cols_s), (spots_ref, spots_s)], sems)
 
     for lane_no, piece in enumerate(pieces):
@@ -172,47 +201,85 @@
                 table_ref[lane_no * CAP + 4 * g + m] = tile16(tile)
             return 0
 
-        lax.fori_loop(0, CAP // 4, spread, 0, unroll=4)
-
-    def tile(k, b):
-        c = cols_s[k, b] - first_block
-        return table_ref[spots_s[lax.shift_right_logical(c, 7), c & (NBD - 1)]]
-
-    for copy in copies:
-        copy.wait()
-    for step, out_ref in enumerate(outs):
+        lax.fori_loop(0, CAP // 4, spread, 0, unroll=True)
+
+    tile = remote_tile(cols_s, spots_s, table_ref)
+    for copy in copies:
+        copy.wait()
+    for n, (step, out_ref) in enumerate(zip(STEPS, outs)):
         share = me ^ step
 
-        def group(g, _, out_ref=out_ref, share=share):
+        def group(g, _, n=n, out_ref=out_ref, share=share):
             tiles = []
-            for pair in range(2):
-                bs = [share * SHARE + 4 * g + 2 * pair + half for half in range(2)]
-                x = [jnp.concatenate([tile(1, b), tile(2, b)], axis=1) for b in bs]
-                w = [jnp.concatenate([far_ref[b, 0], far_ref[b, 1]], axis=1) for b in bs]
-                y = nt(jnp.concatenate(x, axis=0), jnp.concatenate(w, axis=0))
-                tiles += [y[0:16, 0:BS], y[16:32, BS:]]
-            there = pl.ds(pl.multiple_of((share * (SHARE // 4) + g) * 48, 16), 48)
-            total = pack4(tiles) + local_ref[there, :]
-            out_ref[pl.ds(pl.multiple_of(48 * g, 16), 48), :] = total.astype(out_ref.dtype)
+            for m in range(4):
+                row = 4 * g + m
+                b = share * SHARE + row
+                h = n * SHARE + row
+                x = jnp.concatenate([tile(1, b), tile(2, b)], axis=1)
+                tiles.append(nt(x, jnp.concatenate([far_ref[h, 0], far_ref[h, 1]], axis=1)))
+            total = pack4(tiles) + local_ref[packed_rows(n, g), :]
+            out_ref[packed_rows(0, g), :] = total.astype(BF16)
             return 0
 
         lax.fori_loop(0, SHARE // 4, group, 0, unroll=True)
 
 
-def first_remote_kernel(cols_ref, local_ref, far_ref, p0, p1, p2, p3, own_ref, o1, o2, o3, ispots_ref,
-                        cols_s, spots_s, table_ref, spots_v, sems):
-    pieces = (p0, p1, p2, p3)
-    spots_v[...] = jnp.zeros((8, BS), I32)
+def in_order(pieces, order):
+    return tuple(pieces[order.index(m)] for m in range(4))
+
+
+def first_remote_kernel(cols_ref, local_ref, far_ref, p0, p1, p2, p3,
+                        o1, o2, o3, table_ref, espots_ref, ispots_ref, cols_s, spots_s, sems):
+    pieces = in_order((p0, p1, p2, p3), FIRST_ORDER)
+    espots_ref[...] = jnp.zeros((8, BS), I32)
     ispots_ref[...] = jnp.zeros((8, BS), I32)
-    message_spots(pieces, spots_v, ispots_ref)
-    remote_groups(cols_ref, spots_v, local_ref, far_ref, pieces, (own_ref, o1, o2, o3),
-                  cols_s, spots_s, table_ref, sems)
-
-
-def second_remote_kernel(cols_ref, local_ref, far_ref, p0, p1, p2, p3, spots_ref, own_ref, o1, o2, o3,
-                         cols_s, spots_s, table_ref, sems):
-    remote_groups(cols_ref, spots_ref, local_ref, far_ref, (p0, p1, p2, p3), (own_ref, o1, o2, o3),
-                  cols_s, spots_s, table_ref, sems)
+    message_spots(pieces, espots_ref, ispots_ref)
+    remote_groups(cols_ref, espots_ref, local_ref, far_ref, pieces, (o1, o2, o3),
+                  table_ref, cols_s, spots_s, sems)
+
+
+def second_remote_kernel(cols_ref, local_ref, far_ref, p0, p1, p2, p3, spots_ref,
+                         o1, o2, o3, table_ref, cols_s, spots_s, sems):
+    pieces = in_order((p0, p1, p2, p3), SECOND_ORDER)
+    remote_groups(cols_ref, spots_ref, local_ref, far_ref, pieces, (o1, o2, o3),
+                  table_ref, cols_s, spots_s, sems)
+
+
+def own_groups(cols_s, spots_s, load_tile, table_ref, held_ref, out_ref):
+    me = lax.axis_index("rep")
+    base = lax.axis_index("blk") * NBD
+    tile = remote_tile(cols_s, spots_s, table_ref)
+
+    def group(g, _):
+        tiles = []
+        for m in range(4):
+            row = 4 * g + m
+            b = me * SHARE + row
+            x = jnp.concatenate([load_tile(cols_s[0, b] - base), tile(1, b), tile(2, b)], axis=1)
+            tiles.append(nt(x, jnp.concatenate([held_ref[row, k] for k in range(3)], axis=1)))
+        out_ref[packed_rows(0, g), :] = pack4(tiles)
+        return 0
+
+    lax.fori_loop(0, SHARE // 4, group, 0, unroll=True)
+
+
+def first_own_kernel(cols_ref, spots_ref, blocks_ref, table_ref, tracers_ref,
+                     out_ref, cols_s, spots_s, held_ref, tracers_v, sems):
+    me = lax.axis_index("rep")
+    copies = fetch([(cols_ref, cols_s), (spots_ref, spots_s), (tracers_ref, tracers_v),
+                    (blocks_ref.at[share_rows(me)], held_ref)], sems)
+    for copy in copies:
+        copy.wait()
+    own_groups(cols_s, spots_s, tracer_tile(tracers_v), table_ref, held_ref, out_ref)
+
+
+def second_own_kernel(cols_ref, spots_ref, blocks_ref, table_ref, state_ref,
+                      out_ref, cols_s, spots_s, held_ref, sems):
+    me = lax.axis_index("rep")
+    copies = fetch([(cols_ref, cols_s), (spots_ref, spots_s), (blocks_ref.at[share_rows(me)], held_ref)], sems)
+    for copy in copies:
+        copy.wait()
+    own_groups(cols_s, spots_s, lambda i: state_ref[i], table_ref, held_ref, out_ref)
 
 
 def middle_kernel(own_ref, g1, g2, g3, share_ref, coupling_ref, wet_ref,
@@ -236,11 +303,11 @@
         packed_ref[pl.ds(48 * g, 48), :] = pack4(tiles).astype(BF16)
 
 
-def second_kernel(sends_ref, own, g2, g3, g1, *rest):
+def second_kernel(sends_ref, own, ga, gb, gc, *rest):
     outs, table_ref, sends_s, sems = rest[0:4], rest[4], rest[5], rest[6]
     copies = fetch([(sends_ref, sends_s)], sems)
     me = lax.axis_index("rep")
-    for step, packed in ((0, own), (2, g2), (3, g3), (1, g1)):
+    for step, packed in zip((0,) + GATHER, (own, ga, gb, gc)):
         share = me ^ step
 
         def spread(g, _, packed=packed, share=share):
@@ -249,7 +316,7 @@
                 table_ref[share * SHARE + 4 * g + m] = tile16(tile)
             return 0
 
-        lax.fori_loop(0, SHARE // 4, spread, 0, unroll=4)
+        lax.fori_loop(0, SHARE // 4, spread, 0, unroll=True)
     copies[0].wait()
     gather_lists(sends_s, lambda i: table_ref[i].astype(F32), outs)
 
@@ -315,8 +382,11 @@
     return pltpu.SemaphoreType.DMA((n,))
 
 
-FAR = pltpu.VMEM((NBD, 2, BS, BS), BF16)
-NEAR = pltpu.VMEM((NBD, 1, BS, BS), BF16)
+FAR = pltpu.VMEM((len(STEPS) * SHARE, 2, BS, BS), BF16)
+NEAR = pltpu.VMEM((len(STEPS) * SHARE, 1, BS, BS), BF16)
+HELD = pltpu.VMEM((SHARE, 3, BS, BS), BF16)
+SPOTS = pltpu.SMEM((8, BS), I32)
+STATE = pltpu.VMEM((NTR, NBD * BS), F32)
 COLS = pltpu.SMEM((3, BS), I32)
 SENDS = pltpu.SMEM((4, CAP), I32)
 
@@ -329,48 +399,57 @@
     cells = SHARE * BS
     ints = sds((8, BS), I32)
     sends_v = pltpu.VMEM((4, CAP), I32)
-    local_sum = sds((NBD * NTR, BS), F32)
+    local_sum = sds((len(STEPS) * SHARE_ROWS, BS), F32)
+    cols_out = sds((3, BS), I32)
+    own_sum = sds((SHARE_ROWS, BS), F32)
     part = sds((SHARE_ROWS, BS), BF16)
-    parts_out = [sds((SHARE_ROWS, BS), F32), part, part, part]
-    remote_scratch = [COLS, pltpu.SMEM((8, BS), I32), pltpu.VMEM((4 * CAP, 16, BS), BF16)]
+    parts_out = [part, part, part, sds((4 * CAP, 16, BS), BF16)]
 
     outbound = call(
         first_kernel, lists_out(LABEL_ROWS), [HBM] * 3,
-        [sends_v, sends_v, SENDS, pltpu.VMEM((NTR, NBD * BS), F32), dma(4)],
+        [sends_v, sends_v, SENDS, STATE, dma(4)],
         "first_lists", 16,
     )(esends, isends, tracers)
     pieces = swap_blk(outbound)
-    local, far, share, wet_share, coupling = call(
+    local, far, cols_v, share, wet_share, coupling = call(
         first_local_kernel,
-        [local_sum, FAR, sds((NTR, cells), F32), sds((SHARE, BS), F32), sds((NTR, NTR), F32)], [HBM] * 5,
-        [pltpu.VMEM((SHARE, BS), I32), COLS, pltpu.VMEM((NTR, NBD * BS), F32), NEAR, dma(5), dma(2 * REP)],
-        "first_local_product", 24, flops=50_000_000, bytes_accessed=13_000_000,
+        [local_sum, FAR, cols_out, sds((NTR, cells), F32), sds((SHARE, BS), F32), sds((NTR, NTR), F32)],
+        [HBM] * 5, [pltpu.VMEM((SHARE, BS), I32), COLS, STATE, NEAR, dma(6), dma(2 * len(STEPS))],
+        "first_local_product", 24, flops=50_000_000, bytes_accessed=10_000_000,
     )(ecols, tracers, wet, coupling, explicit_blocks)
-    own, *parts, ispots = call(
-        first_remote_kernel, parts_out + [ints], [HBM] + [VMEM] * 6,
-        remote_scratch + [pltpu.VMEM((8, BS), I32), dma(2)],
+    *parts, far_table, espots, ispots = call(
+        first_remote_kernel, parts_out + [ints, ints], [VMEM] * 7, [COLS, SPOTS, dma(2)],
         "first_remote_product", 16, flops=100_000_000, bytes_accessed=1_000_000,
-    )(ecols, local, far, *pieces)
-    got = [swap_rep(parts[k - 1], k) for k in (1, 3, 2)]
+    )(cols_v, local, far, *(pieces[m] for m in FIRST_ORDER))
+    got = [swap_rep(parts[k - 1], k) for k in FIRST_SUM]
+    own = call(
+        first_own_kernel, own_sum, [VMEM, VMEM, HBM, VMEM, HBM], [COLS, SPOTS, HELD, STATE, dma(4)],
+        "first_own_product", 16, flops=50_000_000, bytes_accessed=5_000_000,
+    )(cols_v, espots, explicit_blocks, far_table, tracers)
     before, packed = call(
         middle_kernel, [sds((NTR, cells), F32), part], [VMEM] * 7, [pltpu.VMEM((NTR, cells), F32)],
         "middle", 16,
     )(own, *got, share, coupling, wet_share)
-    others = [swap_rep(packed, k) for k in (2, 3, 1)]
+    others = [swap_rep(packed, k) for k in GATHER]
     *outbound, table = call(
         second_kernel, lists_out(0) + [sds((NBD, 16, BS), BF16)], [HBM] + [VMEM] * 4, [SENDS, dma(1)],
         "second_lists", 16,
     )(isends, packed, *others)
     pieces = swap_blk(outbound)
-    local, far = call(
-        second_local_kernel, [local_sum, FAR], [HBM, VMEM, HBM], [COLS, NEAR, dma(1), dma(2 * REP)],
-        "second_local_product", 24, flops=50_000_000, bytes_accessed=13_000_000,
+    local, far, cols_v = call(
+        second_local_kernel, [local_sum, FAR, cols_out], [HBM, VMEM, HBM],
+        [COLS, NEAR, dma(2), dma(2 * len(STEPS))],
+        "second_local_product", 24, flops=50_000_000, bytes_accessed=10_000_000,
     )(icols, table, implicit_blocks)
-    own, *parts = call(
-        second_remote_kernel, parts_out, [HBM] + [VMEM] * 7, remote_scratch + [dma(2)],
+    *parts, far_table = call(
+        second_remote_kernel, parts_out, [VMEM] * 8, [COLS, SPOTS, dma(2)],
         "second_remote_product", 16, flops=100_000_000, bytes_accessed=1_000_000,
-    )(icols, local, far, *pieces, ispots)
-    got = [swap_rep(parts[k - 1], k) for k in (1, 3, 2)]
+    )(cols_v, local, far, *(pieces[m] for m in SECOND_ORDER), ispots)
+    got = [swap_rep(parts[k - 1], k) for k in SECOND_SUM]
+    own = call(
+        second_own_kernel, own_sum, [VMEM, VMEM, HBM, VMEM, VMEM], [COLS, SPOTS, HELD, dma(3)],
+        "second_own_product", 16, flops=50_000_000, bytes_accessed=4_000_000,
+    )(cols_v, ispots, implicit_blocks, far_table, table)
     return call(
         last_kernel, sds((NTR, cells), F32), [VMEM] * 6, [], "last", 16,
     )(own, *got, before, wet_share)

time: 69.9 us -> 63.2 us (0.904)
  waiting for transfers between devices: 15.5 us -> 8.1 us
  Pallas kernels: 22.9 us -> 25 us
  starting transfers between devices: 31 us -> 29.7 us
    ppermute x9, waiting for transfers between devices: 13.7 us -> 7.35 us  [swap_rep(): return lax.ppermute(x, 'rep', [(i, i ^ distance) for i in range(n)])]
    pallas_call x8 -> x10, Pallas kernels: 22.9 us -> 25 us  [run(): kernel(*(pltpu.with_memory_space_constraint(x, pltpu.HBM) if spec is HBM...]
    ppermute x9, starting transfers between devices: 13.9 us -> 12.1 us  [swap_rep(): return lax.ppermute(x, 'rep', [(i, i ^ distance) for i in range(n)])]
    ppermute x8, waiting for transfers between devices: 1.8 us -> 0.76 us  [swap_blk(): lax.ppermute(x, 'blk', [(i, to(i)) for i in range(n) if 0 <= to(i) < n])]
  transfers between devices with their start and end apart: 17 -> 17, of which waited for: 10 -> 6; matrix products, arithmetic and copies ran while one was open for 0% -> 0% of each run, Pallas kernels for 16% -> 25%
where the time goes in v4:
time: 63.2 us; the launch traced here: 63 us
  starting transfers between devices  29.7 us (47%)
  Pallas kernels  25 us (40%)
  waiting for transfers between devices  8.1 us (13%)
    pallas_call x10, Pallas kernels, run(): kernel(*(pltpu.with_memory_space_constraint(x, pltpu.HBM) if spec is HBM...  25 us
    ppermute x8, starting transfers between devices, swap_blk(): lax.ppermute(x, 'blk', [(i, to(i)) for i in range(n) if 0 <= to(i) < n])  17.5 us
    ppermute x9, starting transfers between devices, swap_rep(): return lax.ppermute(x, 'rep', [(i, i ^ distance) for i in range(n)])  12.1 us
    ppermute x9, waiting for transfers between devices, swap_rep(): return lax.ppermute(x, 'rep', [(i, i ^ distance) for i in range(n)])  7.35 us
  transfers between devices with their start and end apart: 17, of which 6 were waited for; matrix products, arithmetic and copies ran while one was open for 0% of the time, Pallas kernels for 25%

profile of v4, /device:TPU:6, one launch (start us, length us, event | category | flops | bytes accessed | tf_op | source)
XLA Modules:
  0.0 63.0 jit_solution(1917997945210772325)
XLA Ops:
  0.0 1.8 %first_lists.1 = (bf16[784,128]{1,0:T(8,128)(2,1)S(1)}, bf16[784,128]{1,0:T(8,128)(2,1)S(1)}, bf16[784,128]{1,0:T(8,128)(2,1)S(1)}, bf16[784,128]{1,0:T(8,128)(2,1)S(1)}) custom-call(s32[4,64]{1,0:T(4,128)} %bitcast.8, s32[4,64]{1,0:T(4,128)} %bitcast.6, f32[12,16384]{1,0:T(8,128)} %tracers_ref.5), custom_call_target="tpu_custom_call" | custom-call | tf_op jit(solution)/shard_map/first_lists/pallas_call | solution.py:351
  1.8 5.2 %collective-permute-start = (bf16[784,128]{1,0:T(8,128)(2,1)S(1)}, bf16[784,128]{1,0:T(8,128)(2,1)S(1)}, u32[]{:S(2)}, u32[]{:S(2)}) collective-permute-start(bf16[784,128]{1,0:T(8,128)(2,1)S(1)} %get-tuple-element.38), channel_id=1, source_target_pairs={{8,16},{12,20},{16,8},{20,12},{24,32},{28,36},{32,24},{36,28},{40,... | collective-permute-start | bytes 602120 | tf_op jit(solution)/shard_map/ppermute | solution.py:367
  7.0 0.1 collective-permute-start.1
  7.1 2.0 %collective-permute-start.2 = (bf16[784,128]{1,0:T(8,128)(2,1)S(1)}, bf16[784,128]{1,0:T(8,128)(2,1)S(1)}, u32[]{:S(2)}, u32[]{:S(2)}) collective-permute-start(bf16[784,128]{1,0:T(8,128)(2,1)S(1)} %get-tuple-element.40), channel_id=1, source_target_pairs={{4,8},{8,4},{12,16},{16,12},{20,24},{24,20},{28,32},{32,28},{36,40... | collective-permute-start | bytes 602120 | tf_op jit(solution)/shard_map/ppermute | solution.py:367
  9.1 2.1 %collective-permute-start.3 = (bf16[784,128]{1,0:T(8,128)(2,1)S(1)}, bf16[784,128]{1,0:T(8,128)(2,1)S(1)}, u32[]{:S(2)}, u32[]{:S(2)}) collective-permute-start(bf16[784,128]{1,0:T(8,128)(2,1)S(1)} %get-tuple-element.41), channel_id=1, source_target_pairs={{0,4},{4,0},{8,12},{12,8},{16,20},{20,16},{24,28},{28,24},{32,36},... | collective-permute-start | bytes 602120 | tf_op jit(solution)/shard_map/ppermute | solution.py:367
  11.2 4.9 %first_local_product.1 = (f32[1152,128]{1,0:T(8,128)S(1)}, bf16[96,2,128,128]{3,2,1,0:T(8,128)(2,1)S(1)}, s32[3,128]{1,0:T(4,128)S(1)}, f32[12,4096]{1,0:T(8,128...) custom-call(s32[3,128]{1,0:T(4,128)} %bitcast.9, f32[12,16384]{1,0:T(8,128)} %tracers_ref.5, s32[128,128]{1,0:T(8,128)} %bitcast.5, ...), custom_call_target="tpu_custom_call" | custom-call | flops 50000000 | bytes 10000000 | tf_op jit(solution)/shard_map/first_local_product/pallas_call | solution.py:351
  16.1 0.0 collective-permute-done.p0
  16.1 0.0 collective-permute-done.1.p1
  16.1 0.1 collective-permute-done.2.p2
  16.2 0.0 collective-permute-done.3.p3
  16.2 2.7 %first_remote_product.1 = (bf16[384,128]{1,0:T(8,128)(2,1)S(1)}, bf16[384,128]{1,0:T(8,128)(2,1)S(1)}, bf16[384,128]{1,0:T(8,128)(2,1)S(1)}, bf16[256,16,128]{2,...) custom-call(s32[3,128]{1,0:T(4,128)S(1)} %get-tuple-element.35.cols_ref, ...), custom_call_target="tpu_custom_call" | custom-call | flops 100000000 | bytes 1000000 | tf_op jit(solution)/shard_map/first_remote_product/pallas_call | solution.py:351
  18.9 4.0 %collective-permute-start.4 = (bf16[384,128]{1,0:T(8,128)(2,1)S(1)}, bf16[384,128]{1,0:T(8,128)(2,1)S(1)}, u32[]{:S(2)}, u32[]{:S(2)}) collective-permute-start(bf16[384,128]{1,0:T(8,128)(2,1)S(1)} %get-tuple-element.44), channel_id=1, source_target_pairs={{0,2},{1,3},{2,0},{3,1},{4,6},{5,7},{6,4},{7,5},{8,10},{9,11},{10,... | collective-permute-start | bytes 294920 | tf_op jit(solution)/shard_map/ppermute | solution.py:374
  22.9 0.7 %collective-permute-start.5 = (bf16[384,128]{1,0:T(8,128)(2,1)S(1)}, bf16[384,128]{1,0:T(8,128)(2,1)S(1)}, u32[]{:S(2)}, u32[]{:S(2)}) collective-permute-start(bf16[384,128]{1,0:T(8,128)(2,1)S(1)} %get-tuple-element.45), channel_id=1, source_target_pairs={{0,3},{1,2},{2,1},{3,0},{4,7},{5,6},{6,5},{7,4},{8,11},{9,10},{10,... | collective-permute-start | bytes 294920 | tf_op jit(solution)/shard_map/ppermute | solution.py:374
  23.6 0.3 collective-permute-start.6
  23.9 3.5 %first_own_product.1.own_ref = f32[384,128]{1,0:T(8,128)S(1)} custom-call(s32[3,128]{1,0:T(4,128)S(1)} %get-tuple-element.35.cols_ref, s32[8,128]{1,0:T(8,128)S(1)} %get-tuple-element.42.spots_ref, bf16[128,3,128,128]{3,2,1,0:T(8,128)(2,1)} %blocks_ref.5, bf16[256,16,128]{2,1,0:T(8,128)(2,1)S(1)} %get-tuple-element.43.table_ref, f32[12,16384]{1,0:T(8,128)} %tracers_ref.5), custom_call_target="tpu_custom_call" | custom-call | flops 50000000 | bytes 5000000 | tf_op jit(solution)/shard_map/first_own_product/pallas_call | solution.py:351
  27.4 0.0 collective-permute-done.4.g1
  27.4 1.3 %collective-permute-done.5.g2 = bf16[384,128]{1,0:T(8,128)(2,1)S(1)} collective-permute-done((bf16[384,128]{1,0:T(8,128)(2,1)S(1)}, bf16[384,128]{1,0:T(8,128)(2,1)S(1)}, u32[]{:S(2)}, u32[]{:S(2)}) %collective-permute-start.5) | collective-permute-done | bytes 98336 | tf_op jit(solution)/shard_map/ppermute | solution.py:374
  28.7 0.0 collective-permute-done.6.g3
  28.7 0.5 middle.1
  29.2 2.4 %collective-permute-start.9 = (bf16[384,128]{1,0:T(8,128)(2,1)S(1)}, bf16[384,128]{1,0:T(8,128)(2,1)S(1)}, u32[]{:S(2)}, u32[]{:S(2)}) collective-permute-start(bf16[384,128]{1,0:T(8,128)(2,1)S(1)} %get-tuple-element.50.own), channel_id=1, source_target_pairs={{0,2},{1,3},{2,0},{3,1},{4,6},{5,7},{6,4},{7,5},{8,10},{9,11},{10,... | collective-permute-start | bytes 294920 | tf_op jit(solution)/shard_map/ppermute | solution.py:374
  31.6 1.1 %collective-permute-start.8 = (bf16[384,128]{1,0:T(8,128)(2,1)S(1)}, bf16[384,128]{1,0:T(8,128)(2,1)S(1)}, u32[]{:S(2)}, u32[]{:S(2)}) collective-permute-start(bf16[384,128]{1,0:T(8,128)(2,1)S(1)} %get-tuple-element.50.own), channel_id=1, source_target_pairs={{0,3},{1,2},{2,1},{3,0},{4,7},{5,6},{6,5},{7,4},{8,11},{9,10},{10,... | collective-permute-start | bytes 294920 | tf_op jit(solution)/shard_map/ppermute | solution.py:374
  32.8 0.0 collective-permute-start.7
  32.8 2.7 %collective-permute-done.9.gc = bf16[384,128]{1,0:T(8,128)(2,1)S(1)} collective-permute-done((bf16[384,128]{1,0:T(8,128)(2,1)S(1)}, bf16[384,128]{1,0:T(8,128)(2,1)S(1)}, u32[]{:S(2)}, u32[]{:S(2)}) %collective-permute-start.9) | collective-permute-done | bytes 98336 | tf_op jit(solution)/shard_map/ppermute | solution.py:374
  35.5 2.0 %collective-permute-done.8.gb = bf16[384,128]{1,0:T(8,128)(2,1)S(1)} collective-permute-done((bf16[384,128]{1,0:T(8,128)(2,1)S(1)}, bf16[384,128]{1,0:T(8,128)(2,1)S(1)}, u32[]{:S(2)}, u32[]{:S(2)}) %collective-permute-start.8) | collective-permute-done | bytes 98336 | tf_op jit(solution)/shard_map/ppermute | solution.py:374
  37.4 0.0 collective-permute-done.7.ga
  37.5 1.1 %second_lists.1 = (bf16[768,128]{1,0:T(8,128)(2,1)S(1)}, bf16[768,128]{1,0:T(8,128)(2,1)S(1)}, bf16[768,128]{1,0:T(8,128)(2,1)S(1)}, bf16[768,128]{1,0:T(8,128)(2,1)S(1)}, bf16[128,16,128]{2,1,0:T(8,128)(2,1)S(1)}) custom-call(s32[4,64]{1,0:T(4,128)} %bitcast.7, bf16[384,128]{1,0:T(8,128)(2,1)S(1)} %get-tuple-element.50.own, ...), custom_call_target="tpu_custom_call" | custom-call | tf_op jit(solution)/shard_map/second_lists/pallas_call | solution.py:351
  38.6 4.0 %collective-permute-start.10 = (bf16[768,128]{1,0:T(8,128)(2,1)S(1)}, bf16[768,128]{1,0:T(8,128)(2,1)S(1)}, u32[]{:S(2)}, u32[]{:S(2)}) collective-permute-start(bf16[768,128]{1,0:T(8,128)(2,1)S(1)} %get-tuple-element.56), channel_id=1, source_target_pairs={{8,16},{12,20},{16,8},{20,12},{24,32},{28,36},{32,24},{36,28},{40,... | collective-permute-start | bytes 589832 | tf_op jit(solution)/shard_map/ppermute | solution.py:367
  42.6 0.1 collective-permute-start.11
  42.7 2.0 %collective-permute-start.12 = (bf16[768,128]{1,0:T(8,128)(2,1)S(1)}, bf16[768,128]{1,0:T(8,128)(2,1)S(1)}, u32[]{:S(2)}, u32[]{:S(2)}) collective-permute-start(bf16[768,128]{1,0:T(8,128)(2,1)S(1)} %get-tuple-element.58), channel_id=1, source_target_pairs={{4,8},{8,4},{12,16},{16,12},{20,24},{24,20},{28,32},{32,28},{36,40... | collective-permute-start | bytes 589832 | tf_op jit(solution)/shard_map/ppermute | solution.py:367
  44.7 2.1 %collective-permute-start.13 = (bf16[768,128]{1,0:T(8,128)(2,1)S(1)}, bf16[768,128]{1,0:T(8,128)(2,1)S(1)}, u32[]{:S(2)}, u32[]{:S(2)}) collective-permute-start(bf16[768,128]{1,0:T(8,128)(2,1)S(1)} %get-tuple-element.59), channel_id=1, source_target_pairs={{0,4},{4,0},{8,12},{12,8},{16,20},{20,16},{24,28},{28,24},{32,36},... | collective-permute-start | bytes 589832 | tf_op jit(solution)/shard_map/ppermute | solution.py:367
  46.8 4.3 %second_local_product.1 = (f32[1152,128]{1,0:T(8,128)S(1)}, bf16[96,2,128,128]{3,2,1,0:T(8,128)(2,1)S(1)}, s32[3,128]{1,0:T(4,128)S(1)}) custom-call(s32[3,128]{1,0:T(4,128)} %bitcast.10, bf16[128,16,128]{2,1,0:T(8,128)(2,1)S(1)} %get-tuple-element.51.table_ref.state_ref, bf16[128,3,128,128]{3,2,1,0:T(8,128)(2,1)} %blocks_ref.7), custom_call_target="tpu_custom_call" | custom-call | flops 50000000 | bytes 10000000 | tf_op jit(solution)/shard_map/second_local_product/pallas_call | solution.py:351
  51.1 0.0 collective-permute-done.10.p0
  51.1 0.0 collective-permute-done.11.p1
  51.1 0.6 %collective-permute-done.12.p2 = bf16[768,128]{1,0:T(8,128)(2,1)S(1)} collective-permute-done((bf16[768,128]{1,0:T(8,128)(2,1)S(1)}, bf16[768,128]{1,0:T(8,128)(2,1)S(1)}, u32[]{:S(2)}, u32[]{:S(2)}) %collective-permute-start.12) | collective-permute-done | bytes 196640 | tf_op jit(solution)/shard_map/ppermute | solution.py:367
  51.7 0.0 collective-permute-done.13.p3
  51.8 2.4 %second_remote_product.1 = (bf16[384,128]{1,0:T(8,128)(2,1)S(1)}, bf16[384,128]{1,0:T(8,128)(2,1)S(1)}, bf16[384,128]{1,0:T(8,128)(2,1)S(1)}, bf16[256,16,128]{2,1,0:T(8,128)(2,1)S(1)}) custom-call(s32[3,128]{1,0:T(4,128)S(1)} %get-tuple-element.52.cols_ref, f32[1152,128]{1,0:T(8,128)S(1)} %get-tuple-element.54.local_ref, ...), custom_call_target="tpu_custom_call" | custom-call | flops 100000000 | bytes 1000000 | tf_op jit(solution)/shard_map/second_remote_product/pallas_call | solution.py:351
  54.2 1.9 %collective-permute-start.14 = (bf16[384,128]{1,0:T(8,128)(2,1)S(1)}, bf16[384,128]{1,0:T(8,128)(2,1)S(1)}, u32[]{:S(2)}, u32[]{:S(2)}) collective-permute-start(bf16[384,128]{1,0:T(8,128)(2,1)S(1)} %get-tuple-element.61), channel_id=1, source_target_pairs={{0,2},{1,3},{2,0},{3,1},{4,6},{5,7},{6,4},{7,5},{8,10},{9,11},{10,... | collective-permute-start | bytes 294920 | tf_op jit(solution)/shard_map/ppermute | solution.py:374
  56.1 1.4 %collective-permute-start.15 = (bf16[384,128]{1,0:T(8,128)(2,1)S(1)}, bf16[384,128]{1,0:T(8,128)(2,1)S(1)}, u32[]{:S(2)}, u32[]{:S(2)}) collective-permute-start(bf16[384,128]{1,0:T(8,128)(2,1)S(1)} %get-tuple-element.62), channel_id=1, source_target_pairs={{0,3},{1,2},{2,1},{3,0},{4,7},{5,6},{6,5},{7,4},{8,11},{9,10},{10,... | collective-permute-start | bytes 294920 | tf_op jit(solution)/shard_map/ppermute | solution.py:374
  57.5 0.2 collective-permute-start.16
  57.7 3.1 %second_own_product.1.own_ref = f32[384,128]{1,0:T(8,128)S(1)} custom-call(s32[3,128]{1,0:T(4,128)S(1)} %get-tuple-element.52.cols_ref, s32[8,128]{1,0:T(8,128)S(1)} %get-tuple-element.53.spots_ref, bf16[128,3,128,128]{3,2,1,0:T(8,128)(2,1)} %blocks_ref.7, bf16[256,16,128]{2,1,0:T(8,128)(2,1)S(1)} %get-tuple-element.60.table_ref, ...), custom_call_target="tpu_custom_call" | custom-call | flops 50000000 | bytes 4000000 | tf_op jit(solution)/shard_map/second_own_product/pallas_call | solution.py:351
  60.9 0.0 collective-permute-done.14.g1
  60.9 1.3 %collective-permute-done.15.g2 = bf16[384,128]{1,0:T(8,128)(2,1)S(1)} collective-permute-done((bf16[384,128]{1,0:T(8,128)(2,1)S(1)}, bf16[384,128]{1,0:T(8,128)(2,1)S(1)}, u32[]{:S(2)}, u32[]{:S(2)}) %collective-permute-start.15) | collective-permute-done | bytes 98336 | tf_op jit(solution)/shard_map/ppermute | solution.py:374
  62.2 0.0 collective-permute-done.16.g3
  62.2 0.8 %last.1 = f32[12,4096]{1,0:T(8,128)} custom-call(f32[384,128]{1,0:T(8,128)S(1)} %second_own_product.1.own_ref, bf16[384,128]{1,0:T(8,128)(2,1)S(1)} %collective-permute-done.14.g1, bf16[384,128]{1,0:T(8,128)(2,1)S(1)} %collective-permute-done.15.g2, bf16[384,128]{1,0:T(8,128)(2,1)S(1)} %collective-permute-done.16.g3, ...), custom_call_target="tpu_custom_call" | custom-call | tf_op jit(solution)/shard_map/last/pallas_call | solution.py:351
Async XLA Ops:
  1.8 14.3 %collective-permute-start = (bf16[784,128]{1,0:T(8,128)(2,1)S(1)}, bf16[784,128]{1,0:T(8,128)(2,1)S(1)}, u32[]{:S(2)}, u32[]{:S(2)}) collective-permute-start(bf16[784,128]{1,0:T(8,128)(2,1)S(1)} %get-tuple-element.38), channel_id=1, source_target_pairs={{8,16},{12,20},{16,8},{20,12},{24,32},{28,36},{32,24},{36,28},{40,... | collective-permute-start | bytes 602120 | tf_op jit(solution)/shard_map/ppermute | solution.py:367
  7.0 9.1 %collective-permute-start.1 = (bf16[784,128]{1,0:T(8,128)(2,1)S(1)}, bf16[784,128]{1,0:T(8,128)(2,1)S(1)}, u32[]{:S(2)}, u32[]{:S(2)}) collective-permute-start(bf16[784,128]{1,0:T(8,128)(2,1)S(1)} %get-tuple-element.39), channel_id=1, source_target_pairs={{0,8},{4,12},{8,0},{12,4},{16,24},{20,28},{24,16},{28,20},{32,40},... | collective-permute-start | bytes 602120 | tf_op jit(solution)/shard_map/ppermute | solution.py:367
  7.1 9.1 %collective-permute-start.2 = (bf16[784,128]{1,0:T(8,128)(2,1)S(1)}, bf16[784,128]{1,0:T(8,128)(2,1)S(1)}, u32[]{:S(2)}, u32[]{:S(2)}) collective-permute-start(bf16[784,128]{1,0:T(8,128)(2,1)S(1)} %get-tuple-element.40), channel_id=1, source_target_pairs={{4,8},{8,4},{12,16},{16,12},{20,24},{24,20},{28,32},{32,28},{36,40... | collective-permute-start | bytes 602120 | tf_op jit(solution)/shard_map/ppermute | solution.py:367
  9.1 7.2 %collective-permute-start.3 = (bf16[784,128]{1,0:T(8,128)(2,1)S(1)}, bf16[784,128]{1,0:T(8,128)(2,1)S(1)}, u32[]{:S(2)}, u32[]{:S(2)}) collective-permute-start(bf16[784,128]{1,0:T(8,128)(2,1)S(1)} %get-tuple-element.41), channel_id=1, source_target_pairs={{0,4},{4,0},{8,12},{12,8},{16,20},{20,16},{24,28},{28,24},{32,36},... | collective-permute-start | bytes 602120 | tf_op jit(solution)/shard_map/ppermute | solution.py:367
  18.9 8.4 %collective-permute-start.4 = (bf16[384,128]{1,0:T(8,128)(2,1)S(1)}, bf16[384,128]{1,0:T(8,128)(2,1)S(1)}, u32[]{:S(2)}, u32[]{:S(2)}) collective-permute-start(bf16[384,128]{1,0:T(8,128)(2,1)S(1)} %get-tuple-element.44), channel_id=1, source_target_pairs={{0,2},{1,3},{2,0},{3,1},{4,6},{5,7},{6,4},{7,5},{8,10},{9,11},{10,... | collective-permute-start | bytes 294920 | tf_op jit(solution)/shard_map/ppermute | solution.py:374
  22.9 5.8 %collective-permute-start.5 = (bf16[384,128]{1,0:T(8,128)(2,1)S(1)}, bf16[384,128]{1,0:T(8,128)(2,1)S(1)}, u32[]{:S(2)}, u32[]{:S(2)}) collective-permute-start(bf16[384,128]{1,0:T(8,128)(2,1)S(1)} %get-tuple-element.45), channel_id=1, source_target_pairs={{0,3},{1,2},{2,1},{3,0},{4,7},{5,6},{6,5},{7,4},{8,11},{9,10},{10,... | collective-permute-start | bytes 294920 | tf_op jit(solution)/shard_map/ppermute | solution.py:374
  23.6 5.1 %collective-permute-start.6 = (bf16[384,128]{1,0:T(8,128)(2,1)S(1)}, bf16[384,128]{1,0:T(8,128)(2,1)S(1)}, u32[]{:S(2)}, u32[]{:S(2)}) collective-permute-start(bf16[384,128]{1,0:T(8,128)(2,1)S(1)} %get-tuple-element.46), channel_id=1, source_target_pairs={{0,1},{1,0},{2,3},{3,2},{4,5},{5,4},{6,7},{7,6},{8,9},{9,8},{10,11... | collective-permute-start | bytes 294920 | tf_op jit(solution)/shard_map/ppermute | solution.py:374
  29.2 6.3 %collective-permute-start.9 = (bf16[384,128]{1,0:T(8,128)(2,1)S(1)}, bf16[384,128]{1,0:T(8,128)(2,1)S(1)}, u32[]{:S(2)}, u32[]{:S(2)}) collective-permute-start(bf16[384,128]{1,0:T(8,128)(2,1)S(1)} %get-tuple-element.50.own), channel_id=1, source_target_pairs={{0,2},{1,3},{2,0},{3,1},{4,6},{5,7},{6,4},{7,5},{8,10},{9,11},{10,... | collective-permute-start | bytes 294920 | tf_op jit(solution)/shard_map/ppermute | solution.py:374
  31.6 5.8 %collective-permute-start.8 = (bf16[384,128]{1,0:T(8,128)(2,1)S(1)}, bf16[384,128]{1,0:T(8,128)(2,1)S(1)}, u32[]{:S(2)}, u32[]{:S(2)}) collective-permute-start(bf16[384,128]{1,0:T(8,128)(2,1)S(1)} %get-tuple-element.50.own), channel_id=1, source_target_pairs={{0,3},{1,2},{2,1},{3,0},{4,7},{5,6},{6,5},{7,4},{8,11},{9,10},{10,... | collective-permute-start | bytes 294920 | tf_op jit(solution)/shard_map/ppermute | solution.py:374
  32.8 4.7 %collective-permute-start.7 = (bf16[384,128]{1,0:T(8,128)(2,1)S(1)}, bf16[384,128]{1,0:T(8,128)(2,1)S(1)}, u32[]{:S(2)}, u32[]{:S(2)}) collective-permute-start(bf16[384,128]{1,0:T(8,128)(2,1)S(1)} %get-tuple-element.50.own), channel_id=1, source_target_pairs={{0,1},{1,0},{2,3},{3,2},{4,5},{5,4},{6,7},{7,6},{8,9},{9,8},{10,11... | collective-permute-start | bytes 294920 | tf_op jit(solution)/shard_map/ppermute | solution.py:374
  38.6 12.5 %collective-permute-start.10 = (bf16[768,128]{1,0:T(8,128)(2,1)S(1)}, bf16[768,128]{1,0:T(8,128)(2,1)S(1)}, u32[]{:S(2)}, u32[]{:S(2)}) collective-permute-start(bf16[768,128]{1,0:T(8,128)(2,1)S(1)} %get-tuple-element.56), channel_id=1, source_target_pairs={{8,16},{12,20},{16,8},{20,12},{24,32},{28,36},{32,24},{36,28},{40,... | collective-permute-start | bytes 589832 | tf_op jit(solution)/shard_map/ppermute | solution.py:367
  42.6 8.5 %collective-permute-start.11 = (bf16[768,128]{1,0:T(8,128)(2,1)S(1)}, bf16[768,128]{1,0:T(8,128)(2,1)S(1)}, u32[]{:S(2)}, u32[]{:S(2)}) collective-permute-start(bf16[768,128]{1,0:T(8,128)(2,1)S(1)} %get-tuple-element.57), channel_id=1, source_target_pairs={{0,8},{4,12},{8,0},{12,4},{16,24},{20,28},{24,16},{28,20},{32,40},... | collective-permute-start | bytes 589832 | tf_op jit(solution)/shard_map/ppermute | solution.py:367
  42.7 9.1 %collective-permute-start.12 = (bf16[768,128]{1,0:T(8,128)(2,1)S(1)}, bf16[768,128]{1,0:T(8,128)(2,1)S(1)}, u32[]{:S(2)}, u32[]{:S(2)}) collective-permute-start(bf16[768,128]{1,0:T(8,128)(2,1)S(1)} %get-tuple-element.58), channel_id=1, source_target_pairs={{4,8},{8,4},{12,16},{16,12},{20,24},{24,20},{28,32},{32,28},{36,40... | collective-permute-start | bytes 589832 | tf_op jit(solution)/shard_map/ppermute | solution.py:367
  44.7 7.1 %collective-permute-start.13 = (bf16[768,128]{1,0:T(8,128)(2,1)S(1)}, bf16[768,128]{1,0:T(8,128)(2,1)S(1)}, u32[]{:S(2)}, u32[]{:S(2)}) collective-permute-start(bf16[768,128]{1,0:T(8,128)(2,1)S(1)} %get-tuple-element.59), channel_id=1, source_target_pairs={{0,4},{4,0},{8,12},{12,8},{16,20},{20,16},{24,28},{28,24},{32,36},... | collective-permute-start | bytes 589832 | tf_op jit(solution)/shard_map/ppermute | solution.py:367
  54.2 6.7 %collective-permute-start.14 = (bf16[384,128]{1,0:T(8,128)(2,1)S(1)}, bf16[384,128]{1,0:T(8,128)(2,1)S(1)}, u32[]{:S(2)}, u32[]{:S(2)}) collective-permute-start(bf16[384,128]{1,0:T(8,128)(2,1)S(1)} %get-tuple-element.61), channel_id=1, source_target_pairs={{0,2},{1,3},{2,0},{3,1},{4,6},{5,7},{6,4},{7,5},{8,10},{9,11},{10,... | collective-permute-start | bytes 294920 | tf_op jit(solution)/shard_map/ppermute | solution.py:374
  56.1 6.1 %collective-permute-start.15 = (bf16[384,128]{1,0:T(8,128)(2,1)S(1)}, bf16[384,128]{1,0:T(8,128)(2,1)S(1)}, u32[]{:S(2)}, u32[]{:S(2)}) collective-permute-start(bf16[384,128]{1,0:T(8,128)(2,1)S(1)} %get-tuple-element.62), channel_id=1, source_target_pairs={{0,3},{1,2},{2,1},{3,0},{4,7},{5,6},{6,5},{7,4},{8,11},{9,10},{10,... | collective-permute-start | bytes 294920 | tf_op jit(solution)/shard_map/ppermute | solution.py:374
  57.5 4.6 %collective-permute-start.16 = (bf16[384,128]{1,0:T(8,128)(2,1)S(1)}, bf16[384,128]{1,0:T(8,128)(2,1)S(1)}, u32[]{:S(2)}, u32[]{:S(2)}) collective-permute-start(bf16[384,128]{1,0:T(8,128)(2,1)S(1)} %get-tuple-element.63), channel_id=1, source_target_pairs={{0,1},{1,0},{2,3},{3,2},{4,5},{5,4},{6,7},{7,6},{8,9},{9,8},{10,11... | collective-permute-start | bytes 294920 | tf_op jit(solution)/shard_map/ppermute | solution.py:374

commit v5 on v4

v5 whole, which is shorter than its diff:
```python
import jax
import jax.numpy as jnp
from jax import lax
from jax.experimental import pallas as pl
from jax.experimental.pallas import tpu as pltpu
from jax.sharding import PartitionSpec as P

NTR = 12
BS = 128
NBD = 128
CAP = 64
REP = 4
SHARE = NBD // REP
LIST_ROWS = CAP * NTR
LABEL_ROWS = 16
SHARE_ROWS = SHARE * NTR
FIRST_ORDER = (3, 2, 0, 1)
SECOND_ORDER = (3, 2, 0, 1)
LAST = 1
FIRST_SUM = (2, 3, 1)
SECOND_SUM = (2, 3, 1)
GATHER = (1, 3, 2)
F32 = jnp.float32
BF16 = jnp.bfloat16
I32 = jnp.int32
MIB = 1 << 20

VMEM = pl.BlockSpec(memory_space=pltpu.VMEM)
HBM = pl.BlockSpec(memory_space=pltpu.HBM)
PINNED = pl.BlockSpec(memory_space=pltpu.VMEM)


def nt(a, b):
    return lax.dot_general(a, b, (((1,), (1,)), ((), ())), preferred_element_type=F32)


def pack4(tiles):
    return jnp.concatenate([t[0:8] for t in tiles] + [t[8:12] for t in tiles], axis=0)


def unpack4(rows):
    return [
        jnp.concatenate([rows[8 * m : 8 * m + 8], rows[32 + 4 * m : 36 + 4 * m]], axis=0)
        for m in range(4)
    ]


def tile16(t):
    return jnp.concatenate([t, jnp.zeros((4, BS), F32)], axis=0).astype(BF16)


def route_lanes():
    me = lax.axis_index("blk")
    core = me & 1
    odd = lax.shift_right_logical(me, 1) & 1
    return (2 - core, 1 + core, 3 * odd, 3 - 3 * odd)


def message_spots(pieces, messages, espots_ref, ispots_ref):
    me = lax.axis_index("blk")
    core = me & 1
    odd = lax.shift_right_logical(me, 1) & 1
    sub = lax.broadcasted_iota(I32, (BS, BS), 0).astype(F32)
    spot = lax.broadcasted_iota(I32, (8, BS), 1)
    kind = lax.broadcasted_iota(I32, (8, BS), 0)
    spot = jnp.where(lax.shift_right_logical(spot, 6) == kind, spot & (CAP - 1), 0)
    spot = spot.astype(F32).astype(BF16)
    rows = (3 - 2 * core, 1 + 2 * core, 4 * odd, 4 - 4 * odd)
    for piece, n in zip(pieces, messages):
        row = rows[n]
        labels = piece[LIST_ROWS : LIST_ROWS + LABEL_ROWS, :].astype(F32)[0:1]
        listed = jnp.where(sub == labels, 1.0, 0.0).astype(BF16)
        found = nt(spot, listed).astype(I32) + n * CAP
        espots_ref[pl.ds(row, 1), :] = found[0:1]
        ispots_ref[pl.ds(row, 1), :] = found[1:2]


def gather_lists(order_ref, load_tile, out_refs):
    for lane_no, out_ref in zip(route_lanes(), out_refs):

        def group(g, _, lane_no=lane_no, out_ref=out_ref):
            tiles = [load_tile(jnp.maximum(order_ref[lane_no, 4 * g + m], 0)) for m in range(4)]
            rows = pl.ds(pl.multiple_of(48 * g, 16), 48)
            out_ref[rows, :] = pack4(tiles).astype(BF16)
            return 0

        lax.fori_loop(0, CAP // 4, group, 0, unroll=True)


def fetch(pairs, sems):
    copies = [pltpu.make_async_copy(src, dst, sems.at[n]) for n, (src, dst) in enumerate(pairs)]
    for copy in copies:
        copy.start()
    return copies


def first_kernel(esends_ref, isends_ref, tracers_ref, *rest):
    outs = rest[0:4]
    esends_v, isends_v, esends_s, tracers_v, sems = rest[4:]
    copies = fetch([(esends_ref, esends_s), (tracers_ref, tracers_v),
                    (esends_ref, esends_v), (isends_ref, isends_v)], sems)
    for copy in copies:
        copy.wait()
    for lane_no, out_ref in zip(route_lanes(), outs):
        row = pl.ds(lane_no, 1)
        labels = jnp.concatenate([esends_v[row, :], isends_v[row, :]], axis=1).astype(F32)
        out_ref[LIST_ROWS : LIST_ROWS + LABEL_ROWS, :] = jnp.broadcast_to(labels, (LABEL_ROWS, BS)).astype(BF16)

    def load_tile(i):
        return tracers_v[:, pl.ds(pl.multiple_of(i * BS, BS), BS)]

    gather_lists(esends_s, load_tile, outs)


def share_rows(n):
    return pl.ds(n * SHARE, SHARE)


STEPS = (1, 2, 3)


def packed_rows(n, g):
    return pl.ds(pl.multiple_of(n * SHARE_ROWS + 48 * g, 16), 48)


def local_groups(cols_s, load_tile, blocks_ref, out_ref):
    me = lax.axis_index("rep")
    base = lax.axis_index("blk") * NBD
    for n, step in enumerate(STEPS):

        def group(g, _, n=n, step=step):
            tiles = []
            for pair in range(2):
                rows = [4 * g + 2 * pair + half for half in range(2)]
                bs = [(me ^ step) * SHARE + row for row in rows]
                x = [load_tile(cols_s[0, b] - base) for b in bs]
                w = [blocks_ref[b, 0] for b in bs]
                y = nt(jnp.concatenate(x, axis=0), jnp.concatenate(w, axis=0))
                tiles += [y[0:16, 0:BS], y[16:32, BS:]]
            out_ref[packed_rows(n, g), :] = pack4(tiles)
            return 0

        lax.fori_loop(0, SHARE // 4, group, 0, unroll=True)


def tracer_tile(tracers_v):
    return lambda i: tile16(tracers_v[:, pl.ds(pl.multiple_of(i * BS, BS), BS)])


def first_local_kernel(cols_ref, tracers_ref, wet_ref, coupling_ref, blocks_ref,
                       out_ref, cols_v, share_ref, wet_share_ref, coupling_out_ref,
                       wet_v, cols_s, tracers_v, sems):
    me = lax.axis_index("rep")
    cells = SHARE * BS
    copies = fetch([
        (cols_ref, cols_s), (tracers_ref, tracers_v),
        (tracers_ref.at[:, pl.ds(pl.multiple_of(me * cells, cells), cells)], share_ref),
        (wet_ref.at[pl.ds(pl.multiple_of(me * SHARE, SHARE), SHARE)], wet_v),
        (coupling_ref, coupling_out_ref), (cols_ref, cols_v),
    ], sems)
    for copy in copies:
        copy.wait()
    wet_share_ref[...] = wet_v[...].astype(F32)
    local_groups(cols_s, tracer_tile(tracers_v), blocks_ref, out_ref)


def second_local_kernel(cols_ref, table_ref, blocks_ref, out_ref, cols_v, cols_s, sems):
    copies = fetch([(cols_ref, cols_s), (cols_ref, cols_v)], sems)
    for copy in copies:
        copy.wait()
    local_groups(cols_s, lambda i: table_ref[i], blocks_ref, out_ref)


def remote_tile(cols_s, spots_s, table_ref):
    first_block = (lax.axis_index("blk") - 2) * NBD

    def tile(k, b):
        c = cols_s[k, b] - first_block
        return table_ref[spots_s[lax.shift_right_logical(c, 7), c & (NBD - 1)]]

    return tile


def spread_pieces(pieces, messages, table_ref):
    for piece, message in zip(pieces, messages):

        def spread(g, _, message=message, piece=piece):
            rows = piece[pl.ds(pl.multiple_of(48 * g, 16), 48), :].astype(F32)
            for m, tile in enumerate(unpack4(rows)):
                table_ref[message * CAP + 4 * g + m] = tile16(tile)
            return 0

        lax.fori_loop(0, CAP // 4, spread, 0, unroll=True)


def remote_groups(cols_ref, spots_ref, local_ref, blocks_ref, piece, outs, table_ref, cols_s, spots_s, sems):
    me = lax.axis_index("rep")
    copies = fetch([(cols_ref, cols_s), (spots_ref, spots_s)], sems)
    spread_pieces((piece,), (LAST,), table_ref)
    tile = remote_tile(cols_s, spots_s, table_ref)
    for copy in copies:
        copy.wait()
    for n, (step, out_ref) in enumerate(zip(STEPS, outs)):
        share = me ^ step

        def group(g, _, n=n, out_ref=out_ref, share=share):
            tiles = []
            for m in range(4):
                row = 4 * g + m
                b = share * SHARE + row
                x = jnp.concatenate([tile(1, b), tile(2, b)], axis=1)
                tiles.append(nt(x, jnp.concatenate([blocks_ref[b, 1], blocks_ref[b, 2]], axis=1)))
            total = pack4(tiles) + local_ref[packed_rows(n, g), :]
            out_ref[packed_rows(0, g), :] = total.astype(BF16)
            return 0

        lax.fori_loop(0, SHARE // 4, group, 0, unroll=True)


def early(order):
    return tuple(m for m in order if m != LAST)


def first_spread_kernel(p0, p1, p2, table_ref, espots_ref, ispots_ref):
    messages = early(FIRST_ORDER)
    espots_ref[...] = jnp.zeros((8, BS), I32)
    ispots_ref[...] = jnp.zeros((8, BS), I32)
    message_spots((p0, p1, p2), messages, espots_ref, ispots_ref)
    spread_pieces((p0, p1, p2), messages, table_ref)


def second_spread_kernel(p0, p1, p2, table_ref):
    spread_pieces((p0, p1, p2), early(SECOND_ORDER), table_ref)


def first_remote_kernel(cols_ref, local_ref, blocks_ref, piece, table_in, espots_in, ispots_in,
                        o1, o2, o3, table_ref, espots_ref, ispots_ref, cols_s, spots_s, sems):
    espots_ref[...] = espots_in[...]
    ispots_ref[...] = ispots_in[...]
    message_spots((piece,), (LAST,), espots_ref, ispots_ref)
    remote_groups(cols_ref, espots_ref, local_ref, blocks_ref, piece, (o1, o2, o3),
                  table_ref, cols_s, spots_s, sems)


def second_remote_kernel(cols_ref, local_ref, blocks_ref, piece, table_in, spots_ref,
                         o1, o2, o3, table_ref, cols_s, spots_s, sems):
    remote_groups(cols_ref, spots_ref, local_ref, blocks_ref, piece, (o1, o2, o3),
                  table_ref, cols_s, spots_s, sems)


def own_groups(cols_s, spots_s, load_tile, table_ref, blocks_ref, out_ref):
    me = lax.axis_index("rep")
    base = lax.axis_index("blk") * NBD
    tile = remote_tile(cols_s, spots_s, table_ref)

    def group(g, _):
        tiles = []
        for m in range(4):
            row = 4 * g + m
            b = me * SHARE + row
            x = jnp.concatenate([load_tile(cols_s[0, b] - base), tile(1, b), tile(2, b)], axis=1)
            tiles.append(nt(x, jnp.concatenate([blocks_ref[b, k] for k in range(3)], axis=1)))
        out_ref[packed_rows(0, g), :] = pack4(tiles)
        return 0

    lax.fori_loop(0, SHARE // 4, group, 0, unroll=True)


def first_own_kernel(cols_ref, spots_ref, blocks_ref, table_ref, tracers_ref,
                     out_ref, cols_s, spots_s, tracers_v, sems):
    copies = fetch([(cols_ref, cols_s), (spots_ref, spots_s), (tracers_ref, tracers_v)], sems)
    for copy in copies:
        copy.wait()
    own_groups(cols_s, spots_s, tracer_tile(tracers_v), table_ref, blocks_ref, out_ref)


def second_own_kernel(cols_ref, spots_ref, blocks_ref, table_ref, state_ref,
                      out_ref, cols_s, spots_s, sems):
    copies = fetch([(cols_ref, cols_s), (spots_ref, spots_s)], sems)
    for copy in copies:
        copy.wait()
    own_groups(cols_s, spots_s, lambda i: state_ref[i], table_ref, blocks_ref, out_ref)


def middle_kernel(own_ref, g1, g2, g3, share_ref, coupling_ref, wet_ref,
                  before_ref, packed_ref, mid_ref):
    for g in range(SHARE // 4):
        rows = pl.ds(48 * g, 48)
        total = own_ref[rows, :] + g1[rows, :].astype(F32) + g2[rows, :].astype(F32) + g3[rows, :].astype(F32)
        for m, tile in enumerate(unpack4(total)):
            lanes = pl.ds((4 * g + m) * BS, BS)
            mid_ref[:, lanes] = share_ref[:, lanes] + tile
    pushed = lax.dot_general(coupling_ref[...], mid_ref[...], (((1,), (0,)), ((), ())),
                             precision=lax.Precision.HIGHEST, preferred_element_type=F32)
    for g in range(SHARE // 4):
        tiles = []
        for m in range(4):
            b = 4 * g + m
            lanes = pl.ds(b * BS, BS)
            tile = mid_ref[:, lanes] + wet_ref[b : b + 1, :] * jnp.tanh(pushed[:, b * BS : (b + 1) * BS])
            before_ref[:, lanes] = tile
            tiles.append(tile)
        packed_ref[pl.ds(48 * g, 48), :] = pack4(tiles).astype(BF16)


def second_kernel(sends_ref, own, ga, gb, gc, *rest):
    outs, table_ref, sends_s, sems = rest[0:4], rest[4], rest[5], rest[6]
    copies = fetch([(sends_ref, sends_s)], sems)
    me = lax.axis_index("rep")
    for step, packed in zip((0,) + GATHER, (own, ga, gb, gc)):
        share = me ^ step

        def spread(g, _, packed=packed, share=share):
            rows = packed[pl.ds(pl.multiple_of(48 * g, 16), 48), :].astype(F32)
            for m, tile in enumerate(unpack4(rows)):
                table_ref[share * SHARE + 4 * g + m] = tile16(tile)
            return 0

        lax.fori_loop(0, SHARE // 4, spread, 0, unroll=True)
    copies[0].wait()
    gather_lists(sends_s, lambda i: table_ref[i].astype(F32), outs)


def last_kernel(own_ref, g1, g2, g3, before_ref, wet_ref, out_ref, out_v, sems):
    copies = []
    for g in range(SHARE // 4):
        rows = pl.ds(48 * g, 48)
        total = own_ref[rows, :] + g1[rows, :].astype(F32) + g2[rows, :].astype(F32) + g3[rows, :].astype(F32)
        for m, tile in enumerate(unpack4(total)):
            b = 4 * g + m
            lanes = pl.ds(b * BS, BS)
            out_v[:, lanes] = wet_ref[b : b + 1, :] * (before_ref[:, lanes] + tile)
        if g % 2:
            lanes = pl.ds((g - 1) * 4 * BS, 8 * BS)
            copies.append(pltpu.make_async_copy(out_v.at[:, lanes], out_ref.at[:, lanes], sems.at[g // 2]))
            copies[-1].start()
    for copy in copies:
        copy.wait()


def sds(shape, dtype):
    return jax.ShapeDtypeStruct(shape, dtype)


def call(body, outs, in_specs, scratch, name, mib, flops=0, bytes_accessed=0, aliases=(), out_spec=VMEM):
    kernel = pl.pallas_call(
        body,
        out_shape=outs,
        in_specs=in_specs,
        out_specs=jax.tree.map(lambda _: out_spec, outs),
        scratch_shapes=scratch,
        input_output_aliases=dict(aliases),
        compiler_params=pltpu.CompilerParams(vmem_limit_bytes=mib * MIB),
        cost_estimate=pl.CostEstimate(flops=flops, bytes_accessed=bytes_accessed, transcendentals=0),
        name=name,
    )

    def run(*operands):
        return kernel(*(
            pltpu.with_memory_space_constraint(x, pltpu.HBM if spec is HBM else pltpu.VMEM)
            if spec is HBM else x
            for x, spec in zip(operands, in_specs)))

    return run


def swap_blk(messages):
    n = lax.axis_size("blk")
    partners = (
        lambda i: i ^ 1,
        lambda i: i + 1 if i & 1 else i - 1,
        lambda i: i + 2 if i & 2 else i - 2,
        lambda i: i ^ 2,
    )
    return [
        lax.ppermute(x, "blk", [(i, to(i)) for i in range(n) if 0 <= to(i) < n])
        for x, to in zip(messages, partners)
    ]


def swap_rep(x, distance):
    n = lax.axis_size("rep")
    return lax.ppermute(x, "rep", [(i, i ^ distance) for i in range(n)])


def lists_out(label_rows):
    return [sds((LIST_ROWS + label_rows, BS), BF16)] * 4


def dma(n):
    return pltpu.SemaphoreType.DMA((n,))


BLOCKS = pltpu.VMEM((NBD, 3, BS, BS), BF16)
SPOTS = pltpu.SMEM((8, BS), I32)
STATE = pltpu.VMEM((NTR, NBD * BS), F32)
COLS = pltpu.SMEM((3, BS), I32)
SENDS = pltpu.SMEM((4, CAP), I32)


def on_device(tracers, explicit_blocks, explicit_cols, explicit_sends,
              implicit_blocks, implicit_cols, implicit_sends, coupling, wet):
    ecols, icols = explicit_cols.T, implicit_cols.T
    esends, isends = explicit_sends.reshape(4, CAP), implicit_sends.reshape(4, CAP)
    wet = wet.reshape(NBD, BS)
    cells = SHARE * BS
    ints = sds((8, BS), I32)
    sends_v = pltpu.VMEM((4, CAP), I32)
    local_sum = sds((len(STEPS) * SHARE_ROWS, BS), F32)
    cols_out = sds((3, BS), I32)
    own_sum = sds((SHARE_ROWS, BS), F32)
    part = sds((SHARE_ROWS, BS), BF16)
    tiles = sds((4 * CAP, 16, BS), BF16)
    parts_out = [part, part, part, tiles]

    outbound = call(
        first_kernel, lists_out(LABEL_ROWS), [HBM] * 3,
        [sends_v, sends_v, SENDS, STATE, dma(4)],
        "first_lists", 16, flops=20_000_000_000, bytes_accessed=50_000_000,
    )(esends, isends, tracers)
    pieces = swap_blk(outbound)
    local, cols_v, share, wet_share, coupling = call(
        first_local_kernel,
        [local_sum, cols_out, sds((NTR, cells), F32), sds((SHARE, BS), F32), sds((NTR, NTR), F32)],
        [HBM] * 4 + [PINNED], [pltpu.VMEM((SHARE, BS), I32), COLS, STATE, dma(6)],
        "first_local_product", 16, flops=50_000_000, bytes_accessed=1_000_000,
    )(ecols, tracers, wet, coupling, explicit_blocks)
    far_table, espots, ispots = call(
        first_spread_kernel, [tiles, ints, ints], [VMEM] * 3, [], "first_spread", 8,
    )(*(pieces[m] for m in early(FIRST_ORDER)))
    *parts, far_table, espots, ispots = call(
        first_remote_kernel, parts_out + [ints, ints], [VMEM, VMEM, PINNED] + [VMEM] * 4, [COLS, SPOTS, dma(2)],
        "first_remote_product", 16, flops=100_000_000, bytes_accessed=1_000_000, aliases=((4, 3),),
    )(cols_v, local, explicit_blocks, pieces[LAST], far_table, espots, ispots)
    got = [swap_rep(parts[k - 1], k) for k in FIRST_SUM]
    own = call(
        first_own_kernel, own_sum, [VMEM, VMEM, PINNED, VMEM, HBM], [COLS, SPOTS, STATE, dma(3)],
        "first_own_product", 16, flops=50_000_000, bytes_accessed=1_000_000,
    )(cols_v, espots, explicit_blocks, far_table, tracers)
    before, packed = call(
        middle_kernel, [sds((NTR, cells), F32), part], [VMEM] * 7, [pltpu.VMEM((NTR, cells), F32)],
        "middle", 16,
    )(own, *got, share, coupling, wet_share)
    others = [swap_rep(packed, k) for k in GATHER]
    *outbound, table = call(
        second_kernel, lists_out(0) + [sds((NBD, 16, BS), BF16)], [HBM] + [VMEM] * 4, [SENDS, dma(1)],
        "second_lists", 16,
    )(isends, packed, *others)
    pieces = swap_blk(outbound)
    local, cols_v = call(
        second_local_kernel, [local_sum, cols_out], [HBM, VMEM, PINNED], [COLS, dma(2)],
        "second_local_product", 16, flops=50_000_000, bytes_accessed=1_000_000,
    )(icols, table, implicit_blocks)
    far_table = call(
        second_spread_kernel, tiles, [VMEM] * 3, [], "second_spread", 8,
    )(*(pieces[m] for m in early(SECOND_ORDER)))
    *parts, far_table = call(
        second_remote_kernel, parts_out, [VMEM, VMEM, PINNED] + [VMEM] * 3, [COLS, SPOTS, dma(2)],
        "second_remote_product", 16, flops=100_000_000, bytes_accessed=1_000_000, aliases=((4, 3),),
    )(cols_v, local, implicit_blocks, pieces[LAST], far_table, ispots)
    got = [swap_rep(parts[k - 1], k) for k in SECOND_SUM]
    own = call(
        second_own_kernel, own_sum, [VMEM, VMEM, PINNED, VMEM, VMEM], [COLS, SPOTS, dma(2)],
        "second_own_product", 16, flops=50_000_000, bytes_accessed=1_000_000,
    )(cols_v, ispots, implicit_blocks, far_table, table)
    return call(
        last_kernel, sds((NTR, cells), F32), [VMEM] * 6, [pltpu.VMEM((NTR, cells), F32), dma(SHARE // 8)],
        "last", 16, out_spec=HBM,
    )(own, *got, before, wet_share)


def solution(mesh):
    in_specs = (
        P(None, "blk"),
        P("blk", "rep", None, None),
        P("blk", "rep"),
        P("blk", "rep", None, None),
        P("blk", "rep", None, None),
        P("blk", "rep"),
        P("blk", "rep", None, None),
        P(),
        P("blk"),
    )
    out_specs = P(None, ("blk", "rep"))
    return jax.shard_map(
        on_device, mesh=mesh, in_specs=in_specs, out_specs=out_specs, check_vma=False
    )
```

time: 63.2 us -> 63.2 us (level)
  Pallas kernels: 25 us -> 18.5 us
  waiting for transfers between devices: 8.1 us -> 14 us
    pallas_call x10 -> x12, Pallas kernels: 25 us -> 18.5 us  [run(): kernel(*(pltpu.with_memory_space_constraint(x, pltpu.HBM if spec is HBM e...]
    ppermute x8, waiting for transfers between devices: 0.76 us -> 4.76 us  [swap_blk(): lax.ppermute(x, 'blk', [(i, to(i)) for i in range(n) if 0 <= to(i) < n])]
    ppermute x9, waiting for transfers between devices: 7.35 us -> 9.25 us  [swap_rep(): return lax.ppermute(x, 'rep', [(i, i ^ distance) for i in range(n)])]
  transfers between devices with their start and end apart: 17 -> 17, of which waited for: 6 -> 8; matrix products, arithmetic and copies ran while one was open for 0% -> 0% of each run, Pallas kernels for 25% -> 15%
where the time goes in v5:
time: 63.2 us; the launch traced here: 63 us
  starting transfers between devices  30.2 us (48%)
  Pallas kernels  18.5 us (29%)
  waiting for transfers between devices  14 us (22%)
    pallas_call x12, Pallas kernels, run(): kernel(*(pltpu.with_memory_space_constraint(x, pltpu.HBM if spec is HBM e...  18.5 us
    ppermute x8, starting transfers between devices, swap_blk(): lax.ppermute(x, 'blk', [(i, to(i)) for i in range(n) if 0 <= to(i) < n])  18.1 us
    ppermute x9, starting transfers between devices, swap_rep(): return lax.ppermute(x, 'rep', [(i, i ^ distance) for i in range(n)])  12.1 us
    ppermute x9, waiting for transfers between devices, swap_rep(): return lax.ppermute(x, 'rep', [(i, i ^ distance) for i in range(n)])  9.25 us
    ppermute x8, waiting for transfers between devices, swap_blk(): lax.ppermute(x, 'blk', [(i, to(i)) for i in range(n) if 0 <= to(i) < n])  4.76 us
  transfers between devices with their start and end apart: 17, of which 8 were waited for; matrix products, arithmetic and copies ran while one was open for 0% of the time, Pallas kernels for 15%

profile of v5, /device:TPU:6, one launch (start us, length us, event | category | flops | bytes accessed | tf_op | source)
XLA Modules:
  0.0 63.0 jit_solution(9712428697732226903)
XLA Ops:
  0.0 2.0 %first_lists.1 = (bf16[784,128]{1,0:T(8,128)(2,1)S(1)}, bf16[784,128]{1,0:T(8,128)(2,1)S(1)}, bf16[784,128]{1,0:T(8,128)(2,1)S(1)}, bf16[784,128]{1,0:T(8,128)(2,1)S(1)}) custom-call(s32[4,64]{1,0:T(4,128)} %bitcast.12, s32[4,64]{1,0:T(4,128)} %bitcast.9, f32[12,16384]{1,0:T(8,128)} %tracers_ref.5), custom_call_target="tpu_custom_call" | custom-call | flops 20000000000 | bytes 50000000 | tf_op jit(solution)/shard_map/first_lists/pallas_call | solution.py:359
  2.0 1.7 %collective-permute-start.1 = (bf16[784,128]{1,0:T(8,128)(2,1)S(1)}, bf16[784,128]{1,0:T(8,128)(2,1)S(1)}, u32[]{:S(2)}, u32[]{:S(2)}) collective-permute-start(bf16[784,128]{1,0:T(8,128)(2,1)S(1)} %get-tuple-element.39), channel_id=1, source_target_pairs={{0,8},{4,12},{8,0},{12,4},{16,24},{20,28},{24,16},{28,20},{32,40},... | collective-permute-start | bytes 602120 | tf_op jit(solution)/shard_map/ppermute | solution.py:376
  3.6 4.6 %collective-permute-start.2 = (bf16[784,128]{1,0:T(8,128)(2,1)S(1)}, bf16[784,128]{1,0:T(8,128)(2,1)S(1)}, u32[]{:S(2)}, u32[]{:S(2)}) collective-permute-start(bf16[784,128]{1,0:T(8,128)(2,1)S(1)} %get-tuple-element.40), channel_id=1, source_target_pairs={{8,16},{12,20},{16,8},{20,12},{24,32},{28,36},{32,24},{36,28},{40,... | collective-permute-start | bytes 602120 | tf_op jit(solution)/shard_map/ppermute | solution.py:376
  8.2 0.1 collective-permute-start.3
  8.3 3.6 %collective-permute-start = (bf16[784,128]{1,0:T(8,128)(2,1)S(1)}, bf16[784,128]{1,0:T(8,128)(2,1)S(1)}, u32[]{:S(2)}, u32[]{:S(2)}) collective-permute-start(bf16[784,128]{1,0:T(8,128)(2,1)S(1)} %get-tuple-element.38), channel_id=1, source_target_pairs={{4,8},{8,4},{12,16},{16,12},{20,24},{24,20},{28,32},{32,28},{36,40... | collective-permute-start | bytes 602120 | tf_op jit(solution)/shard_map/ppermute | solution.py:376
  11.9 0.0 copy-done
  11.9 2.5 %first_local_product.1 = (f32[1152,128]{1,0:T(8,128)S(1)}, s32[3,128]{1,0:T(4,128)S(1)}, f32[12,4096]{1,0:T(8,128)S(1)}, f32[32,128]{1,0:T(8,128)S(1)}, f32[12,12]{1,0:T(8,128)S(1)}) custom-call(s32[3,128]{1,0:T(4,128)} %bitcast.8, f32[12,16384]{1,0:T(8,128)} %tracers_ref.5, s32[128,128]{1,0:T(8,128)} %bitcast.7, f32[12,12]{1,0:T(8,128)} %coupling_ref.1, ...), custom_call_target="tpu_custom_call" | custom-call | flops 50000000 | bytes 1000000 | tf_op jit(solution)/shard_map/first_local_product/pallas_call | solution.py:359
  14.4 0.0 collective-permute-done.1.p0
  14.4 0.0 collective-permute-done.2.p1
  14.5 0.0 collective-permute-done.3.p2
  14.5 0.2 first_spread.1
  14.7 2.8 %collective-permute-done.piece = bf16[784,128]{1,0:T(8,128)(2,1)S(1)} collective-permute-done((bf16[784,128]{1,0:T(8,128)(2,1)S(1)}, bf16[784,128]{1,0:T(8,128)(2,1)S(1)}, u32[]{:S(2)}, u32[]{:S(2)}) %collective-permute-start) | collective-permute-done | bytes 200736 | tf_op jit(solution)/shard_map/ppermute | solution.py:376
  17.5 2.6 %first_remote_product.1 = (bf16[384,128]{1,0:T(8,128)(2,1)S(1)}, bf16[384,128]{1,0:T(8,128)(2,1)S(1)}, bf16[384,128]{1,0:T(8,128)(2,1)S(1)}, bf16[256,16,128]{2,...) custom-call(s32[3,128]{1,0:T(4,128)S(1)} %get-tuple-element.36.cols_ref, ...), custom_call_target="tpu_custom_call", output_to_operand_aliasing={{3}: (4, {})} | custom-call | flops 100000000 | bytes 1000000 | tf_op jit(solution)/shard_map/first_remote_product/pallas_call | solution.py:359
  20.0 4.0 %collective-permute-start.4 = (bf16[384,128]{1,0:T(8,128)(2,1)S(1)}, bf16[384,128]{1,0:T(8,128)(2,1)S(1)}, u32[]{:S(2)}, u32[]{:S(2)}) collective-permute-start(bf16[384,128]{1,0:T(8,128)(2,1)S(1)} %get-tuple-element.47), channel_id=1, source_target_pairs={{0,2},{1,3},{2,0},{3,1},{4,6},{5,7},{6,4},{7,5},{8,10},{9,11},{10,... | collective-permute-start | bytes 294920 | tf_op jit(solution)/shard_map/ppermute | solution.py:383
  24.0 0.7 %collective-permute-start.5 = (bf16[384,128]{1,0:T(8,128)(2,1)S(1)}, bf16[384,128]{1,0:T(8,128)(2,1)S(1)}, u32[]{:S(2)}, u32[]{:S(2)}) collective-permute-start(bf16[384,128]{1,0:T(8,128)(2,1)S(1)} %get-tuple-element.48), channel_id=1, source_target_pairs={{0,3},{1,2},{2,1},{3,0},{4,7},{5,6},{6,5},{7,4},{8,11},{9,10},{10,... | collective-permute-start | bytes 294920 | tf_op jit(solution)/shard_map/ppermute | solution.py:383
  24.7 0.3 collective-permute-start.6
  25.0 2.6 %first_own_product.1.own_ref = f32[384,128]{1,0:T(8,128)S(1)} custom-call(s32[3,128]{1,0:T(4,128)S(1)} %get-tuple-element.36.cols_ref, s32[8,128]{1,0:T(8,128)S(1)} %get-tuple-element.45.spots_ref, bf16[128,3,128,128]{3,2,1,0:T(8,128)(2,1)S(1)} %copy-done, bf16[256,16,128]{2,1,0:T(8,128)(2,1)S(1)} %get-tuple-element.46.table_ref, f32[12,16384]{1,0:T(8,128)} %tracers_ref.5), custom_call_target="tpu_custom_call" | custom-call | flops 50000000 | bytes 1000000 | tf_op jit(solution)/shard_map/first_own_product/pallas_call | solution.py:359
  27.6 0.0 collective-permute-done.4.g1
  27.6 2.2 %collective-permute-done.5.g2 = bf16[384,128]{1,0:T(8,128)(2,1)S(1)} collective-permute-done((bf16[384,128]{1,0:T(8,128)(2,1)S(1)}, bf16[384,128]{1,0:T(8,128)(2,1)S(1)}, u32[]{:S(2)}, u32[]{:S(2)}) %collective-permute-start.5) | collective-permute-done | bytes 98336 | tf_op jit(solution)/shard_map/ppermute | solution.py:383
  29.8 0.0 collective-permute-done.6.g3
  29.8 0.5 middle.1
  30.3 2.0 %collective-permute-start.9 = (bf16[384,128]{1,0:T(8,128)(2,1)S(1)}, bf16[384,128]{1,0:T(8,128)(2,1)S(1)}, u32[]{:S(2)}, u32[]{:S(2)}) collective-permute-start(bf16[384,128]{1,0:T(8,128)(2,1)S(1)} %get-tuple-element.53.own), channel_id=1, source_target_pairs={{0,2},{1,3},{2,0},{3,1},{4,6},{5,7},{6,4},{7,5},{8,10},{9,11},{10,... | collective-permute-start | bytes 294920 | tf_op jit(solution)/shard_map/ppermute | solution.py:383
  32.2 0.9 %collective-permute-start.8 = (bf16[384,128]{1,0:T(8,128)(2,1)S(1)}, bf16[384,128]{1,0:T(8,128)(2,1)S(1)}, u32[]{:S(2)}, u32[]{:S(2)}) collective-permute-start(bf16[384,128]{1,0:T(8,128)(2,1)S(1)} %get-tuple-element.53.own), channel_id=1, source_target_pairs={{0,3},{1,2},{2,1},{3,0},{4,7},{5,6},{6,5},{7,4},{8,11},{9,10},{10,... | collective-permute-start | bytes 294920 | tf_op jit(solution)/shard_map/ppermute | solution.py:383
  33.1 0.7 %collective-permute-start.7 = (bf16[384,128]{1,0:T(8,128)(2,1)S(1)}, bf16[384,128]{1,0:T(8,128)(2,1)S(1)}, u32[]{:S(2)}, u32[]{:S(2)}) collective-permute-start(bf16[384,128]{1,0:T(8,128)(2,1)S(1)} %get-tuple-element.53.own), channel_id=1, source_target_pairs={{0,1},{1,0},{2,3},{3,2},{4,5},{5,4},{6,7},{7,6},{8,9},{9,8},{10,11... | collective-permute-start | bytes 294920 | tf_op jit(solution)/shard_map/ppermute | solution.py:383
  33.9 3.5 %collective-permute-done.9.gc = bf16[384,128]{1,0:T(8,128)(2,1)S(1)} collective-permute-done((bf16[384,128]{1,0:T(8,128)(2,1)S(1)}, bf16[384,128]{1,0:T(8,128)(2,1)S(1)}, u32[]{:S(2)}, u32[]{:S(2)}) %collective-permute-start.9) | collective-permute-done | bytes 98336 | tf_op jit(solution)/shard_map/ppermute | solution.py:383
  37.4 0.9 %collective-permute-done.8.gb = bf16[384,128]{1,0:T(8,128)(2,1)S(1)} collective-permute-done((bf16[384,128]{1,0:T(8,128)(2,1)S(1)}, bf16[384,128]{1,0:T(8,128)(2,1)S(1)}, u32[]{:S(2)}, u32[]{:S(2)}) %collective-permute-start.8) | collective-permute-done | bytes 98336 | tf_op jit(solution)/shard_map/ppermute | solution.py:383
  38.3 0.0 collective-permute-done.7.ga
  38.3 1.1 %second_lists.1 = (bf16[768,128]{1,0:T(8,128)(2,1)S(1)}, bf16[768,128]{1,0:T(8,128)(2,1)S(1)}, bf16[768,128]{1,0:T(8,128)(2,1)S(1)}, bf16[768,128]{1,0:T(8,128)(2,1)S(1)}, bf16[128,16,128]{2,1,0:T(8,128)(2,1)S(1)}) custom-call(s32[4,64]{1,0:T(4,128)} %bitcast.10, bf16[384,128]{1,0:T(8,128)(2,1)S(1)} %get-tuple-element.53.own, ...), custom_call_target="tpu_custom_call" | custom-call | tf_op jit(solution)/shard_map/second_lists/pallas_call | solution.py:359
  39.5 0.1 collective-permute-start.11
  39.6 3.0 %collective-permute-start.12 = (bf16[768,128]{1,0:T(8,128)(2,1)S(1)}, bf16[768,128]{1,0:T(8,128)(2,1)S(1)}, u32[]{:S(2)}, u32[]{:S(2)}) collective-permute-start(bf16[768,128]{1,0:T(8,128)(2,1)S(1)} %get-tuple-element.60), channel_id=1, source_target_pairs={{8,16},{12,20},{16,8},{20,12},{24,32},{28,36},{32,24},{36,28},{40,... | collective-permute-start | bytes 589832 | tf_op jit(solution)/shard_map/ppermute | solution.py:376
  42.6 0.1 collective-permute-start.13
  42.7 5.0 %collective-permute-start.10 = (bf16[768,128]{1,0:T(8,128)(2,1)S(1)}, bf16[768,128]{1,0:T(8,128)(2,1)S(1)}, u32[]{:S(2)}, u32[]{:S(2)}) collective-permute-start(bf16[768,128]{1,0:T(8,128)(2,1)S(1)} %get-tuple-element.58), channel_id=1, source_target_pairs={{4,8},{8,4},{12,16},{16,12},{20,24},{24,20},{28,32},{32,28},{36,40... | collective-permute-start | bytes 589832 | tf_op jit(solution)/shard_map/ppermute | solution.py:376
  47.7 0.0 slice-done
  47.8 1.9 %second_local_product.1 = (f32[1152,128]{1,0:T(8,128)S(1)}, s32[3,128]{1,0:T(4,128)S(1)}) custom-call(s32[3,128]{1,0:T(4,128)} %bitcast.11, bf16[128,16,128]{2,1,0:T(8,128)(2,1)S(1)} %get-tuple-element.54.table_ref.state_ref, bf16[128,3,128,128]{3,2,1,0:T(8,128)(2,1)S(1)} %bitcast.6), custom_call_target="tpu_custom_call" | custom-call | flops 50000000 | bytes 1000000 | tf_op jit(solution)/shard_map/second_local_product/pallas_call | solution.py:359
  49.7 0.0 collective-permute-done.11.p0
  49.7 0.0 collective-permute-done.12.p1
  49.7 0.0 collective-permute-done.13.p2
  49.7 0.1 second_spread.1.table_in
  49.8 2.0 %collective-permute-done.10.piece = bf16[768,128]{1,0:T(8,128)(2,1)S(1)} collective-permute-done((bf16[768,128]{1,0:T(8,128)(2,1)S(1)}, bf16[768,128]{1,0:T(8,128)(2,1)S(1)}, u32[]{:S(2)}, u32[]{:S(2)}) %collective-permute-start.10) | collective-permute-done | bytes 196640 | tf_op jit(solution)/shard_map/ppermute | solution.py:376
  51.8 2.4 %second_remote_product.1 = (bf16[384,128]{1,0:T(8,128)(2,1)S(1)}, bf16[384,128]{1,0:T(8,128)(2,1)S(1)}, bf16[384,128]{1,0:T(8,128)(2,1)S(1)}, bf16[256,16,128]{2,1,0:T(8,128)(2,1)S(1)}) custom-call(s32[3,128]{1,0:T(4,128)S(1)} %get-tuple-element.55.cols_ref, f32[1152,128]{1,0:T(8,128)S(1)} %get-tuple-element.57.local_ref, ...), custom_call_target="tpu_custom_call", output_to_operand_aliasing={{3}: (4, {})} | custom-call | flops 100000000 | bytes 1000000 | tf_op jit(solution)/shard_map/second_remote_product/pallas_call | solution.py:359
  54.2 1.8 %collective-permute-start.14 = (bf16[384,128]{1,0:T(8,128)(2,1)S(1)}, bf16[384,128]{1,0:T(8,128)(2,1)S(1)}, u32[]{:S(2)}, u32[]{:S(2)}) collective-permute-start(bf16[384,128]{1,0:T(8,128)(2,1)S(1)} %get-tuple-element.63), channel_id=1, source_target_pairs={{0,2},{1,3},{2,0},{3,1},{4,6},{5,7},{6,4},{7,5},{8,10},{9,11},{10,... | collective-permute-start | bytes 294920 | tf_op jit(solution)/shard_map/ppermute | solution.py:383
  56.0 1.6 %collective-permute-start.15 = (bf16[384,128]{1,0:T(8,128)(2,1)S(1)}, bf16[384,128]{1,0:T(8,128)(2,1)S(1)}, u32[]{:S(2)}, u32[]{:S(2)}) collective-permute-start(bf16[384,128]{1,0:T(8,128)(2,1)S(1)} %get-tuple-element.64), channel_id=1, source_target_pairs={{0,3},{1,2},{2,1},{3,0},{4,7},{5,6},{6,5},{7,4},{8,11},{9,10},{10,... | collective-permute-start | bytes 294920 | tf_op jit(solution)/shard_map/ppermute | solution.py:383
  57.6 0.2 collective-permute-start.16
  57.8 1.8 %second_own_product.1.own_ref = f32[384,128]{1,0:T(8,128)S(1)} custom-call(s32[3,128]{1,0:T(4,128)S(1)} %get-tuple-element.55.cols_ref, s32[8,128]{1,0:T(8,128)S(1)} %get-tuple-element.56.spots_ref, bf16[128,3,128,128]{3,2,1,0:T(8,128)(2,1)S(1)} %bitcast.6, bf16[256,16,128]{2,1,0:T(8,128)(2,1)S(1)} %get-tuple-element.62.table_ref, ...), custom_call_target="tpu_custom_call" | custom-call | flops 50000000 | bytes 1000000 | tf_op jit(solution)/shard_map/second_own_product/pallas_call | solution.py:359
  59.6 1.8 %collective-permute-done.14.g1 = bf16[384,128]{1,0:T(8,128)(2,1)S(1)} collective-permute-done((bf16[384,128]{1,0:T(8,128)(2,1)S(1)}, bf16[384,128]{1,0:T(8,128)(2,1)S(1)}, u32[]{:S(2)}, u32[]{:S(2)}) %collective-permute-start.14) | collective-permute-done | bytes 98336 | tf_op jit(solution)/shard_map/ppermute | solution.py:383
  61.4 0.8 %collective-permute-done.15.g2 = bf16[384,128]{1,0:T(8,128)(2,1)S(1)} collective-permute-done((bf16[384,128]{1,0:T(8,128)(2,1)S(1)}, bf16[384,128]{1,0:T(8,128)(2,1)S(1)}, u32[]{:S(2)}, u32[]{:S(2)}) %collective-permute-start.15) | collective-permute-done | bytes 98336 | tf_op jit(solution)/shard_map/ppermute | solution.py:383
  62.2 0.1 collective-permute-done.16.g3
  62.2 0.8 %last.1 = f32[12,4096]{1,0:T(8,128)} custom-call(f32[384,128]{1,0:T(8,128)S(1)} %second_own_product.1.own_ref, bf16[384,128]{1,0:T(8,128)(2,1)S(1)} %collective-permute-done.14.g1, bf16[384,128]{1,0:T(8,128)(2,1)S(1)} %collective-permute-done.15.g2, bf16[384,128]{1,0:T(8,128)(2,1)S(1)} %collective-permute-done.16.g3, ...), custom_call_target="tpu_custom_call" | custom-call | tf_op jit(solution)/shard_map/last/pallas_call | solution.py:359
  (7 shorter events, 0.0 us)
Async XLA Ops:
  0.0 11.9 %copy-start = (bf16[128,3,128,128]{3,2,1,0:T(8,128)(2,1)S(1)}, bf16[128,3,128,128]{3,2,1,0:T(8,128)(2,1)}, u32[]{:S(2)}) copy-start(bf16[128,3,128,128]{3,2,1,0:T(8,128)(2,1)} %blocks_ref.8) | copy-start | bytes 37748740
  2.0 12.5 %collective-permute-start.1 = (bf16[784,128]{1,0:T(8,128)(2,1)S(1)}, bf16[784,128]{1,0:T(8,128)(2,1)S(1)}, u32[]{:S(2)}, u32[]{:S(2)}) collective-permute-start(bf16[784,128]{1,0:T(8,128)(2,1)S(1)} %get-tuple-element.39), channel_id=1, source_target_pairs={{0,8},{4,12},{8,0},{12,4},{16,24},{20,28},{24,16},{28,20},{32,40},... | collective-permute-start | bytes 602120 | tf_op jit(solution)/shard_map/ppermute | solution.py:376
  3.6 10.8 %collective-permute-start.2 = (bf16[784,128]{1,0:T(8,128)(2,1)S(1)}, bf16[784,128]{1,0:T(8,128)(2,1)S(1)}, u32[]{:S(2)}, u32[]{:S(2)}) collective-permute-start(bf16[784,128]{1,0:T(8,128)(2,1)S(1)} %get-tuple-element.40), channel_id=1, source_target_pairs={{8,16},{12,20},{16,8},{20,12},{24,32},{28,36},{32,24},{36,28},{40,... | collective-permute-start | bytes 602120 | tf_op jit(solution)/shard_map/ppermute | solution.py:376
  8.2 6.2 %collective-permute-start.3 = (bf16[784,128]{1,0:T(8,128)(2,1)S(1)}, bf16[784,128]{1,0:T(8,128)(2,1)S(1)}, u32[]{:S(2)}, u32[]{:S(2)}) collective-permute-start(bf16[784,128]{1,0:T(8,128)(2,1)S(1)} %get-tuple-element.41), channel_id=1, source_target_pairs={{0,4},{4,0},{8,12},{12,8},{16,20},{20,16},{24,28},{28,24},{32,36},... | collective-permute-start | bytes 602120 | tf_op jit(solution)/shard_map/ppermute | solution.py:376
  8.3 9.1 %collective-permute-start = (bf16[784,128]{1,0:T(8,128)(2,1)S(1)}, bf16[784,128]{1,0:T(8,128)(2,1)S(1)}, u32[]{:S(2)}, u32[]{:S(2)}) collective-permute-start(bf16[784,128]{1,0:T(8,128)(2,1)S(1)} %get-tuple-element.38), channel_id=1, source_target_pairs={{4,8},{8,4},{12,16},{16,12},{20,24},{24,20},{28,32},{32,28},{36,40... | collective-permute-start | bytes 602120 | tf_op jit(solution)/shard_map/ppermute | solution.py:376
  17.5 30.2 %slice-start = ((s8[12582912]{0:T(1024)(128)(4,1)}), s8[4194304]{0:T(1024)(128)(4,1)S(1)}, s32[]{:S(2)}) async-start(s8[12582912]{0:T(1024)(128)(4,1)} %bitcast.5), calls=%async_computation | async-start | bytes 8388608
  17.5 30.3 %slice-start.1 = ((s8[12582912]{0:T(1024)(128)(4,1)}), s8[4194304]{0:T(1024)(128)(4,1)S(1)}, s32[]{:S(2)}) async-start(s8[12582912]{0:T(1024)(128)(4,1)} %bitcast.5), calls=%async_computation.1 | async-start | bytes 8388608
  20.0 7.6 %collective-permute-start.4 = (bf16[384,128]{1,0:T(8,128)(2,1)S(1)}, bf16[384,128]{1,0:T(8,128)(2,1)S(1)}, u32[]{:S(2)}, u32[]{:S(2)}) collective-permute-start(bf16[384,128]{1,0:T(8,128)(2,1)S(1)} %get-tuple-element.47), channel_id=1, source_target_pairs={{0,2},{1,3},{2,0},{3,1},{4,6},{5,7},{6,4},{7,5},{8,10},{9,11},{10,... | collective-permute-start | bytes 294920 | tf_op jit(solution)/shard_map/ppermute | solution.py:383
  24.0 5.8 %collective-permute-start.5 = (bf16[384,128]{1,0:T(8,128)(2,1)S(1)}, bf16[384,128]{1,0:T(8,128)(2,1)S(1)}, u32[]{:S(2)}, u32[]{:S(2)}) collective-permute-start(bf16[384,128]{1,0:T(8,128)(2,1)S(1)} %get-tuple-element.48), channel_id=1, source_target_pairs={{0,3},{1,2},{2,1},{3,0},{4,7},{5,6},{6,5},{7,4},{8,11},{9,10},{10,... | collective-permute-start | bytes 294920 | tf_op jit(solution)/shard_map/ppermute | solution.py:383
  24.7 5.1 %collective-permute-start.6 = (bf16[384,128]{1,0:T(8,128)(2,1)S(1)}, bf16[384,128]{1,0:T(8,128)(2,1)S(1)}, u32[]{:S(2)}, u32[]{:S(2)}) collective-permute-start(bf16[384,128]{1,0:T(8,128)(2,1)S(1)} %get-tuple-element.49), channel_id=1, source_target_pairs={{0,1},{1,0},{2,3},{3,2},{4,5},{5,4},{6,7},{7,6},{8,9},{9,8},{10,11... | collective-permute-start | bytes 294920 | tf_op jit(solution)/shard_map/ppermute | solution.py:383
  25.0 22.7 %slice-start.2 = ((s8[12582912]{0:T(1024)(128)(4,1)}), s8[4194304]{0:T(1024)(128)(4,1)S(1)}, s32[]{:S(2)}) async-start(s8[12582912]{0:T(1024)(128)(4,1)} %bitcast.5), calls=%async_computation.2 | async-start | bytes 8388608
  30.3 7.1 %collective-permute-start.9 = (bf16[384,128]{1,0:T(8,128)(2,1)S(1)}, bf16[384,128]{1,0:T(8,128)(2,1)S(1)}, u32[]{:S(2)}, u32[]{:S(2)}) collective-permute-start(bf16[384,128]{1,0:T(8,128)(2,1)S(1)} %get-tuple-element.53.own), channel_id=1, source_target_pairs={{0,2},{1,3},{2,0},{3,1},{4,6},{5,7},{6,4},{7,5},{8,10},{9,11},{10,... | collective-permute-start | bytes 294920 | tf_op jit(solution)/shard_map/ppermute | solution.py:383
  32.2 6.1 %collective-permute-start.8 = (bf16[384,128]{1,0:T(8,128)(2,1)S(1)}, bf16[384,128]{1,0:T(8,128)(2,1)S(1)}, u32[]{:S(2)}, u32[]{:S(2)}) collective-permute-start(bf16[384,128]{1,0:T(8,128)(2,1)S(1)} %get-tuple-element.53.own), channel_id=1, source_target_pairs={{0,3},{1,2},{2,1},{3,0},{4,7},{5,6},{6,5},{7,4},{8,11},{9,10},{10,... | collective-permute-start | bytes 294920 | tf_op jit(solution)/shard_map/ppermute | solution.py:383
  33.1 5.2 %collective-permute-start.7 = (bf16[384,128]{1,0:T(8,128)(2,1)S(1)}, bf16[384,128]{1,0:T(8,128)(2,1)S(1)}, u32[]{:S(2)}, u32[]{:S(2)}) collective-permute-start(bf16[384,128]{1,0:T(8,128)(2,1)S(1)} %get-tuple-element.53.own), channel_id=1, source_target_pairs={{0,1},{1,0},{2,3},{3,2},{4,5},{5,4},{6,7},{7,6},{8,9},{9,8},{10,11... | collective-permute-start | bytes 294920 | tf_op jit(solution)/shard_map/ppermute | solution.py:383
  39.5 10.2 %collective-permute-start.11 = (bf16[768,128]{1,0:T(8,128)(2,1)S(1)}, bf16[768,128]{1,0:T(8,128)(2,1)S(1)}, u32[]{:S(2)}, u32[]{:S(2)}) collective-permute-start(bf16[768,128]{1,0:T(8,128)(2,1)S(1)} %get-tuple-element.59), channel_id=1, source_target_pairs={{0,8},{4,12},{8,0},{12,4},{16,24},{20,28},{24,16},{28,20},{32,40},... | collective-permute-start | bytes 589832 | tf_op jit(solution)/shard_map/ppermute | solution.py:376
  39.6 10.1 %collective-permute-start.12 = (bf16[768,128]{1,0:T(8,128)(2,1)S(1)}, bf16[768,128]{1,0:T(8,128)(2,1)S(1)}, u32[]{:S(2)}, u32[]{:S(2)}) collective-permute-start(bf16[768,128]{1,0:T(8,128)(2,1)S(1)} %get-tuple-element.60), channel_id=1, source_target_pairs={{8,16},{12,20},{16,8},{20,12},{24,32},{28,36},{32,24},{36,28},{40,... | collective-permute-start | bytes 589832 | tf_op jit(solution)/shard_map/ppermute | solution.py:376
  42.6 7.1 %collective-permute-start.13 = (bf16[768,128]{1,0:T(8,128)(2,1)S(1)}, bf16[768,128]{1,0:T(8,128)(2,1)S(1)}, u32[]{:S(2)}, u32[]{:S(2)}) collective-permute-start(bf16[768,128]{1,0:T(8,128)(2,1)S(1)} %get-tuple-element.61), channel_id=1, source_target_pairs={{0,4},{4,0},{8,12},{12,8},{16,20},{20,16},{24,28},{28,24},{32,36},... | collective-permute-start | bytes 589832 | tf_op jit(solution)/shard_map/ppermute | solution.py:376
  42.7 9.1 %collective-permute-start.10 = (bf16[768,128]{1,0:T(8,128)(2,1)S(1)}, bf16[768,128]{1,0:T(8,128)(2,1)S(1)}, u32[]{:S(2)}, u32[]{:S(2)}) collective-permute-start(bf16[768,128]{1,0:T(8,128)(2,1)S(1)} %get-tuple-element.58), channel_id=1, source_target_pairs={{4,8},{8,4},{12,16},{16,12},{20,24},{24,20},{28,32},{32,28},{36,40... | collective-permute-start | bytes 589832 | tf_op jit(solution)/shard_map/ppermute | solution.py:376
  54.2 7.2 %collective-permute-start.14 = (bf16[384,128]{1,0:T(8,128)(2,1)S(1)}, bf16[384,128]{1,0:T(8,128)(2,1)S(1)}, u32[]{:S(2)}, u32[]{:S(2)}) collective-permute-start(bf16[384,128]{1,0:T(8,128)(2,1)S(1)} %get-tuple-element.63), channel_id=1, source_target_pairs={{0,2},{1,3},{2,0},{3,1},{4,6},{5,7},{6,4},{7,5},{8,10},{9,11},{10,... | collective-permute-start | bytes 294920 | tf_op jit(solution)/shard_map/ppermute | solution.py:383
  56.0 6.1 %collective-permute-start.15 = (bf16[384,128]{1,0:T(8,128)(2,1)S(1)}, bf16[384,128]{1,0:T(8,128)(2,1)S(1)}, u32[]{:S(2)}, u32[]{:S(2)}) collective-permute-start(bf16[384,128]{1,0:T(8,128)(2,1)S(1)} %get-tuple-element.64), channel_id=1, source_target_pairs={{0,3},{1,2},{2,1},{3,0},{4,7},{5,6},{6,5},{7,4},{8,11},{9,10},{10,... | collective-permute-start | bytes 294920 | tf_op jit(solution)/shard_map/ppermute | solution.py:383
  57.6 4.6 %collective-permute-start.16 = (bf16[384,128]{1,0:T(8,128)(2,1)S(1)}, bf16[384,128]{1,0:T(8,128)(2,1)S(1)}, u32[]{:S(2)}, u32[]{:S(2)}) collective-permute-start(bf16[384,128]{1,0:T(8,128)(2,1)S(1)} %get-tuple-element.65), channel_id=1, source_target_pairs={{0,1},{1,0},{2,3},{3,2},{4,5},{5,4},{6,7},{7,6},{8,9},{9,8},{10,11... | collective-permute-start | bytes 294920 | tf_op jit(solution)/shard_map/ppermute | solution.py:383

commit v6 on v4

--- a/solution.py
+++ b/solution.py
@@ -15,7 +15,7 @@
 LABEL_ROWS = 16
 SHARE_ROWS = SHARE * NTR
 FIRST_ORDER = (2, 3, 1, 0)
-SECOND_ORDER = (2, 3, 1, 0)
+SECOND_ORDER = (2, 3, 0, 1)
 FIRST_SUM = (2, 3, 1)
 SECOND_SUM = (2, 3, 1)
 GATHER = (1, 3, 2)

time: 63.2 us -> 63.3 us (level)
  transfers between devices with their start and end apart: 17 -> 17, of which waited for: 6 -> 7; matrix products, arithmetic and copies ran while one was open for 0% -> 0% of each run, Pallas kernels for 25% -> 25%
where the time goes in v6:
time: 63.3 us; the launch traced here: 63 us
  starting transfers between devices  29.7 us (47%)
  Pallas kernels  25 us (39%)
  waiting for transfers between devices  8.09 us (13%)
    pallas_call x10, Pallas kernels, run(): kernel(*(pltpu.with_memory_space_constraint(x, pltpu.HBM) if spec is HBM...  25 us
    ppermute x8, starting transfers between devices, swap_blk(): lax.ppermute(x, 'blk', [(i, to(i)) for i in range(n) if 0 <= to(i) < n])  17.6 us
    ppermute x9, starting transfers between devices, swap_rep(): return lax.ppermute(x, 'rep', [(i, i ^ distance) for i in range(n)])  12.1 us
    ppermute x9, waiting for transfers between devices, swap_rep(): return lax.ppermute(x, 'rep', [(i, i ^ distance) for i in range(n)])  7.33 us
  transfers between devices with their start and end apart: 17, of which 7 were waited for; matrix products, arithmetic and copies ran while one was open for 0% of the time, Pallas kernels for 25%

profile of v6, /device:TPU:6, one launch (start us, length us, event | category | flops | bytes accessed | tf_op | source)
XLA Modules:
  0.0 63.0 jit_solution(6188303222619887587)
XLA Ops:
  0.0 1.8 %first_lists.1 = (bf16[784,128]{1,0:T(8,128)(2,1)S(1)}, bf16[784,128]{1,0:T(8,128)(2,1)S(1)}, bf16[784,128]{1,0:T(8,128)(2,1)S(1)}, bf16[784,128]{1,0:T(8,128)(2,1)S(1)}) custom-call(s32[4,64]{1,0:T(4,128)} %bitcast.8, s32[4,64]{1,0:T(4,128)} %bitcast.6, f32[12,16384]{1,0:T(8,128)} %tracers_ref.5), custom_call_target="tpu_custom_call" | custom-call | tf_op jit(solution)/shard_map/first_lists/pallas_call | solution.py:351
  1.8 5.2 %collective-permute-start = (bf16[784,128]{1,0:T(8,128)(2,1)S(1)}, bf16[784,128]{1,0:T(8,128)(2,1)S(1)}, u32[]{:S(2)}, u32[]{:S(2)}) collective-permute-start(bf16[784,128]{1,0:T(8,128)(2,1)S(1)} %get-tuple-element.38), channel_id=1, source_target_pairs={{8,16},{12,20},{16,8},{20,12},{24,32},{28,36},{32,24},{36,28},{40,... | collective-permute-start | bytes 602120 | tf_op jit(solution)/shard_map/ppermute | solution.py:367
  7.0 0.1 collective-permute-start.1
  7.1 2.0 %collective-permute-start.2 = (bf16[784,128]{1,0:T(8,128)(2,1)S(1)}, bf16[784,128]{1,0:T(8,128)(2,1)S(1)}, u32[]{:S(2)}, u32[]{:S(2)}) collective-permute-start(bf16[784,128]{1,0:T(8,128)(2,1)S(1)} %get-tuple-element.40), channel_id=1, source_target_pairs={{4,8},{8,4},{12,16},{16,12},{20,24},{24,20},{28,32},{32,28},{36,40... | collective-permute-start | bytes 602120 | tf_op jit(solution)/shard_map/ppermute | solution.py:367
  9.1 2.1 %collective-permute-start.3 = (bf16[784,128]{1,0:T(8,128)(2,1)S(1)}, bf16[784,128]{1,0:T(8,128)(2,1)S(1)}, u32[]{:S(2)}, u32[]{:S(2)}) collective-permute-start(bf16[784,128]{1,0:T(8,128)(2,1)S(1)} %get-tuple-element.41), channel_id=1, source_target_pairs={{0,4},{4,0},{8,12},{12,8},{16,20},{20,16},{24,28},{28,24},{32,36},... | collective-permute-start | bytes 602120 | tf_op jit(solution)/shard_map/ppermute | solution.py:367
  11.2 4.9 %first_local_product.1 = (f32[1152,128]{1,0:T(8,128)S(1)}, bf16[96,2,128,128]{3,2,1,0:T(8,128)(2,1)S(1)}, s32[3,128]{1,0:T(4,128)S(1)}, f32[12,4096]{1,0:T(8,128...) custom-call(s32[3,128]{1,0:T(4,128)} %bitcast.9, f32[12,16384]{1,0:T(8,128)} %tracers_ref.5, s32[128,128]{1,0:T(8,128)} %bitcast.5, ...), custom_call_target="tpu_custom_call" | custom-call | flops 50000000 | bytes 10000000 | tf_op jit(solution)/shard_map/first_local_product/pallas_call | solution.py:351
  16.1 0.0 collective-permute-done.p0
  16.1 0.0 collective-permute-done.1.p1
  16.2 0.1 collective-permute-done.2.p2
  16.2 0.0 collective-permute-done.3.p3
  16.2 2.7 %first_remote_product.1 = (bf16[384,128]{1,0:T(8,128)(2,1)S(1)}, bf16[384,128]{1,0:T(8,128)(2,1)S(1)}, bf16[384,128]{1,0:T(8,128)(2,1)S(1)}, bf16[256,16,128]{2,...) custom-call(s32[3,128]{1,0:T(4,128)S(1)} %get-tuple-element.35.cols_ref, ...), custom_call_target="tpu_custom_call" | custom-call | flops 100000000 | bytes 1000000 | tf_op jit(solution)/shard_map/first_remote_product/pallas_call | solution.py:351
  18.9 4.0 %collective-permute-start.4 = (bf16[384,128]{1,0:T(8,128)(2,1)S(1)}, bf16[384,128]{1,0:T(8,128)(2,1)S(1)}, u32[]{:S(2)}, u32[]{:S(2)}) collective-permute-start(bf16[384,128]{1,0:T(8,128)(2,1)S(1)} %get-tuple-element.44), channel_id=1, source_target_pairs={{0,2},{1,3},{2,0},{3,1},{4,6},{5,7},{6,4},{7,5},{8,10},{9,11},{10,... | collective-permute-start | bytes 294920 | tf_op jit(solution)/shard_map/ppermute | solution.py:374
  22.9 0.7 %collective-permute-start.5 = (bf16[384,128]{1,0:T(8,128)(2,1)S(1)}, bf16[384,128]{1,0:T(8,128)(2,1)S(1)}, u32[]{:S(2)}, u32[]{:S(2)}) collective-permute-start(bf16[384,128]{1,0:T(8,128)(2,1)S(1)} %get-tuple-element.45), channel_id=1, source_target_pairs={{0,3},{1,2},{2,1},{3,0},{4,7},{5,6},{6,5},{7,4},{8,11},{9,10},{10,... | collective-permute-start | bytes 294920 | tf_op jit(solution)/shard_map/ppermute | solution.py:374
  23.6 0.3 collective-permute-start.6
  23.9 3.5 %first_own_product.1.own_ref = f32[384,128]{1,0:T(8,128)S(1)} custom-call(s32[3,128]{1,0:T(4,128)S(1)} %get-tuple-element.35.cols_ref, s32[8,128]{1,0:T(8,128)S(1)} %get-tuple-element.42.spots_ref, bf16[128,3,128,128]{3,2,1,0:T(8,128)(2,1)} %blocks_ref.5, bf16[256,16,128]{2,1,0:T(8,128)(2,1)S(1)} %get-tuple-element.43.table_ref, f32[12,16384]{1,0:T(8,128)} %tracers_ref.5), custom_call_target="tpu_custom_call" | custom-call | flops 50000000 | bytes 5000000 | tf_op jit(solution)/shard_map/first_own_product/pallas_call | solution.py:351
  27.4 0.0 collective-permute-done.4.g1
  27.4 1.3 %collective-permute-done.5.g2 = bf16[384,128]{1,0:T(8,128)(2,1)S(1)} collective-permute-done((bf16[384,128]{1,0:T(8,128)(2,1)S(1)}, bf16[384,128]{1,0:T(8,128)(2,1)S(1)}, u32[]{:S(2)}, u32[]{:S(2)}) %collective-permute-start.5) | collective-permute-done | bytes 98336 | tf_op jit(solution)/shard_map/ppermute | solution.py:374
  28.7 0.0 collective-permute-done.6.g3
  28.7 0.5 middle.1
  29.2 2.4 %collective-permute-start.9 = (bf16[384,128]{1,0:T(8,128)(2,1)S(1)}, bf16[384,128]{1,0:T(8,128)(2,1)S(1)}, u32[]{:S(2)}, u32[]{:S(2)}) collective-permute-start(bf16[384,128]{1,0:T(8,128)(2,1)S(1)} %get-tuple-element.50.own), channel_id=1, source_target_pairs={{0,2},{1,3},{2,0},{3,1},{4,6},{5,7},{6,4},{7,5},{8,10},{9,11},{10,... | collective-permute-start | bytes 294920 | tf_op jit(solution)/shard_map/ppermute | solution.py:374
  31.6 1.1 %collective-permute-start.8 = (bf16[384,128]{1,0:T(8,128)(2,1)S(1)}, bf16[384,128]{1,0:T(8,128)(2,1)S(1)}, u32[]{:S(2)}, u32[]{:S(2)}) collective-permute-start(bf16[384,128]{1,0:T(8,128)(2,1)S(1)} %get-tuple-element.50.own), channel_id=1, source_target_pairs={{0,3},{1,2},{2,1},{3,0},{4,7},{5,6},{6,5},{7,4},{8,11},{9,10},{10,... | collective-permute-start | bytes 294920 | tf_op jit(solution)/shard_map/ppermute | solution.py:374
  32.8 0.0 collective-permute-start.7
  32.8 2.7 %collective-permute-done.9.gc = bf16[384,128]{1,0:T(8,128)(2,1)S(1)} collective-permute-done((bf16[384,128]{1,0:T(8,128)(2,1)S(1)}, bf16[384,128]{1,0:T(8,128)(2,1)S(1)}, u32[]{:S(2)}, u32[]{:S(2)}) %collective-permute-start.9) | collective-permute-done | bytes 98336 | tf_op jit(solution)/shard_map/ppermute | solution.py:374
  35.5 2.0 %collective-permute-done.8.gb = bf16[384,128]{1,0:T(8,128)(2,1)S(1)} collective-permute-done((bf16[384,128]{1,0:T(8,128)(2,1)S(1)}, bf16[384,128]{1,0:T(8,128)(2,1)S(1)}, u32[]{:S(2)}, u32[]{:S(2)}) %collective-permute-start.8) | collective-permute-done | bytes 98336 | tf_op jit(solution)/shard_map/ppermute | solution.py:374
  37.4 0.0 collective-permute-done.7.ga
  37.4 1.1 %second_lists.1 = (bf16[768,128]{1,0:T(8,128)(2,1)S(1)}, bf16[768,128]{1,0:T(8,128)(2,1)S(1)}, bf16[768,128]{1,0:T(8,128)(2,1)S(1)}, bf16[768,128]{1,0:T(8,128)(2,1)S(1)}, bf16[128,16,128]{2,1,0:T(8,128)(2,1)S(1)}) custom-call(s32[4,64]{1,0:T(4,128)} %bitcast.7, bf16[384,128]{1,0:T(8,128)(2,1)S(1)} %get-tuple-element.50.own, ...), custom_call_target="tpu_custom_call" | custom-call | tf_op jit(solution)/shard_map/second_lists/pallas_call | solution.py:351
  38.6 4.0 %collective-permute-start.10 = (bf16[768,128]{1,0:T(8,128)(2,1)S(1)}, bf16[768,128]{1,0:T(8,128)(2,1)S(1)}, u32[]{:S(2)}, u32[]{:S(2)}) collective-permute-start(bf16[768,128]{1,0:T(8,128)(2,1)S(1)} %get-tuple-element.56), channel_id=1, source_target_pairs={{8,16},{12,20},{16,8},{20,12},{24,32},{28,36},{32,24},{36,28},{40,... | collective-permute-start | bytes 589832 | tf_op jit(solution)/shard_map/ppermute | solution.py:367
  42.6 0.1 collective-permute-start.11
  42.7 0.1 collective-permute-start.12
  42.7 4.1 %collective-permute-start.13 = (bf16[768,128]{1,0:T(8,128)(2,1)S(1)}, bf16[768,128]{1,0:T(8,128)(2,1)S(1)}, u32[]{:S(2)}, u32[]{:S(2)}) collective-permute-start(bf16[768,128]{1,0:T(8,128)(2,1)S(1)} %get-tuple-element.59), channel_id=1, source_target_pairs={{4,8},{8,4},{12,16},{16,12},{20,24},{24,20},{28,32},{32,28},{36,40... | collective-permute-start | bytes 589832 | tf_op jit(solution)/shard_map/ppermute | solution.py:367
  46.8 4.3 %second_local_product.1 = (f32[1152,128]{1,0:T(8,128)S(1)}, bf16[96,2,128,128]{3,2,1,0:T(8,128)(2,1)S(1)}, s32[3,128]{1,0:T(4,128)S(1)}) custom-call(s32[3,128]{1,0:T(4,128)} %bitcast.10, bf16[128,16,128]{2,1,0:T(8,128)(2,1)S(1)} %get-tuple-element.51.table_ref.state_ref, bf16[128,3,128,128]{3,2,1,0:T(8,128)(2,1)} %blocks_ref.7), custom_call_target="tpu_custom_call" | custom-call | flops 50000000 | bytes 10000000 | tf_op jit(solution)/shard_map/second_local_product/pallas_call | solution.py:351
  51.2 0.0 collective-permute-done.10.p0
  51.2 0.0 collective-permute-done.11.p1
  51.2 0.0 collective-permute-done.12.p2
  51.2 0.7 %collective-permute-done.13.p3 = bf16[768,128]{1,0:T(8,128)(2,1)S(1)} collective-permute-done((bf16[768,128]{1,0:T(8,128)(2,1)S(1)}, bf16[768,128]{1,0:T(8,128)(2,1)S(1)}, u32[]{:S(2)}, u32[]{:S(2)}) %collective-permute-start.13) | collective-permute-done | bytes 196640 | tf_op jit(solution)/shard_map/ppermute | solution.py:367
  51.8 2.4 %second_remote_product.1 = (bf16[384,128]{1,0:T(8,128)(2,1)S(1)}, bf16[384,128]{1,0:T(8,128)(2,1)S(1)}, bf16[384,128]{1,0:T(8,128)(2,1)S(1)}, bf16[256,16,128]{2,1,0:T(8,128)(2,1)S(1)}) custom-call(s32[3,128]{1,0:T(4,128)S(1)} %get-tuple-element.52.cols_ref, f32[1152,128]{1,0:T(8,128)S(1)} %get-tuple-element.54.local_ref, ...), custom_call_target="tpu_custom_call" | custom-call | flops 100000000 | bytes 1000000 | tf_op jit(solution)/shard_map/second_remote_product/pallas_call | solution.py:351
  54.2 1.9 %collective-permute-start.14 = (bf16[384,128]{1,0:T(8,128)(2,1)S(1)}, bf16[384,128]{1,0:T(8,128)(2,1)S(1)}, u32[]{:S(2)}, u32[]{:S(2)}) collective-permute-start(bf16[384,128]{1,0:T(8,128)(2,1)S(1)} %get-tuple-element.61), channel_id=1, source_target_pairs={{0,2},{1,3},{2,0},{3,1},{4,6},{5,7},{6,4},{7,5},{8,10},{9,11},{10,... | collective-permute-start | bytes 294920 | tf_op jit(solution)/shard_map/ppermute | solution.py:374
  56.2 1.5 %collective-permute-start.15 = (bf16[384,128]{1,0:T(8,128)(2,1)S(1)}, bf16[384,128]{1,0:T(8,128)(2,1)S(1)}, u32[]{:S(2)}, u32[]{:S(2)}) collective-permute-start(bf16[384,128]{1,0:T(8,128)(2,1)S(1)} %get-tuple-element.62), channel_id=1, source_target_pairs={{0,3},{1,2},{2,1},{3,0},{4,7},{5,6},{6,5},{7,4},{8,11},{9,10},{10,... | collective-permute-start | bytes 294920 | tf_op jit(solution)/shard_map/ppermute | solution.py:374
  57.6 0.2 collective-permute-start.16
  57.8 3.1 %second_own_product.1.own_ref = f32[384,128]{1,0:T(8,128)S(1)} custom-call(s32[3,128]{1,0:T(4,128)S(1)} %get-tuple-element.52.cols_ref, s32[8,128]{1,0:T(8,128)S(1)} %get-tuple-element.53.spots_ref, bf16[128,3,128,128]{3,2,1,0:T(8,128)(2,1)} %blocks_ref.7, bf16[256,16,128]{2,1,0:T(8,128)(2,1)S(1)} %get-tuple-element.60.table_ref, ...), custom_call_target="tpu_custom_call" | custom-call | flops 50000000 | bytes 4000000 | tf_op jit(solution)/shard_map/second_own_product/pallas_call | solution.py:351
  60.9 0.0 collective-permute-done.14.g1
  61.0 1.1 %collective-permute-done.15.g2 = bf16[384,128]{1,0:T(8,128)(2,1)S(1)} collective-permute-done((bf16[384,128]{1,0:T(8,128)(2,1)S(1)}, bf16[384,128]{1,0:T(8,128)(2,1)S(1)}, u32[]{:S(2)}, u32[]{:S(2)}) %collective-permute-start.15) | collective-permute-done | bytes 98336 | tf_op jit(solution)/shard_map/ppermute | solution.py:374
  62.1 0.2 collective-permute-done.16.g3
  62.3 0.8 %last.1 = f32[12,4096]{1,0:T(8,128)} custom-call(f32[384,128]{1,0:T(8,128)S(1)} %second_own_product.1.own_ref, bf16[384,128]{1,0:T(8,128)(2,1)S(1)} %collective-permute-done.14.g1, bf16[384,128]{1,0:T(8,128)(2,1)S(1)} %collective-permute-done.15.g2, bf16[384,128]{1,0:T(8,128)(2,1)S(1)} %collective-permute-done.16.g3, ...), custom_call_target="tpu_custom_call" | custom-call | tf_op jit(solution)/shard_map/last/pallas_call | solution.py:351
Async XLA Ops:
  1.8 14.3 %collective-permute-start = (bf16[784,128]{1,0:T(8,128)(2,1)S(1)}, bf16[784,128]{1,0:T(8,128)(2,1)S(1)}, u32[]{:S(2)}, u32[]{:S(2)}) collective-permute-start(bf16[784,128]{1,0:T(8,128)(2,1)S(1)} %get-tuple-element.38), channel_id=1, source_target_pairs={{8,16},{12,20},{16,8},{20,12},{24,32},{28,36},{32,24},{36,28},{40,... | collective-permute-start | bytes 602120 | tf_op jit(solution)/shard_map/ppermute | solution.py:367
  7.0 9.1 %collective-permute-start.1 = (bf16[784,128]{1,0:T(8,128)(2,1)S(1)}, bf16[784,128]{1,0:T(8,128)(2,1)S(1)}, u32[]{:S(2)}, u32[]{:S(2)}) collective-permute-start(bf16[784,128]{1,0:T(8,128)(2,1)S(1)} %get-tuple-element.39), channel_id=1, source_target_pairs={{0,8},{4,12},{8,0},{12,4},{16,24},{20,28},{24,16},{28,20},{32,40},... | collective-permute-start | bytes 602120 | tf_op jit(solution)/shard_map/ppermute | solution.py:367
  7.1 9.1 %collective-permute-start.2 = (bf16[784,128]{1,0:T(8,128)(2,1)S(1)}, bf16[784,128]{1,0:T(8,128)(2,1)S(1)}, u32[]{:S(2)}, u32[]{:S(2)}) collective-permute-start(bf16[784,128]{1,0:T(8,128)(2,1)S(1)} %get-tuple-element.40), channel_id=1, source_target_pairs={{4,8},{8,4},{12,16},{16,12},{20,24},{24,20},{28,32},{32,28},{36,40... | collective-permute-start | bytes 602120 | tf_op jit(solution)/shard_map/ppermute | solution.py:367
  9.1 7.2 %collective-permute-start.3 = (bf16[784,128]{1,0:T(8,128)(2,1)S(1)}, bf16[784,128]{1,0:T(8,128)(2,1)S(1)}, u32[]{:S(2)}, u32[]{:S(2)}) collective-permute-start(bf16[784,128]{1,0:T(8,128)(2,1)S(1)} %get-tuple-element.41), channel_id=1, source_target_pairs={{0,4},{4,0},{8,12},{12,8},{16,20},{20,16},{24,28},{28,24},{32,36},... | collective-permute-start | bytes 602120 | tf_op jit(solution)/shard_map/ppermute | solution.py:367
  18.9 8.4 %collective-permute-start.4 = (bf16[384,128]{1,0:T(8,128)(2,1)S(1)}, bf16[384,128]{1,0:T(8,128)(2,1)S(1)}, u32[]{:S(2)}, u32[]{:S(2)}) collective-permute-start(bf16[384,128]{1,0:T(8,128)(2,1)S(1)} %get-tuple-element.44), channel_id=1, source_target_pairs={{0,2},{1,3},{2,0},{3,1},{4,6},{5,7},{6,4},{7,5},{8,10},{9,11},{10,... | collective-permute-start | bytes 294920 | tf_op jit(solution)/shard_map/ppermute | solution.py:374
  22.9 5.8 %collective-permute-start.5 = (bf16[384,128]{1,0:T(8,128)(2,1)S(1)}, bf16[384,128]{1,0:T(8,128)(2,1)S(1)}, u32[]{:S(2)}, u32[]{:S(2)}) collective-permute-start(bf16[384,128]{1,0:T(8,128)(2,1)S(1)} %get-tuple-element.45), channel_id=1, source_target_pairs={{0,3},{1,2},{2,1},{3,0},{4,7},{5,6},{6,5},{7,4},{8,11},{9,10},{10,... | collective-permute-start | bytes 294920 | tf_op jit(solution)/shard_map/ppermute | solution.py:374
  23.6 5.1 %collective-permute-start.6 = (bf16[384,128]{1,0:T(8,128)(2,1)S(1)}, bf16[384,128]{1,0:T(8,128)(2,1)S(1)}, u32[]{:S(2)}, u32[]{:S(2)}) collective-permute-start(bf16[384,128]{1,0:T(8,128)(2,1)S(1)} %get-tuple-element.46), channel_id=1, source_target_pairs={{0,1},{1,0},{2,3},{3,2},{4,5},{5,4},{6,7},{7,6},{8,9},{9,8},{10,11... | collective-permute-start | bytes 294920 | tf_op jit(solution)/shard_map/ppermute | solution.py:374
  29.2 6.3 %collective-permute-start.9 = (bf16[384,128]{1,0:T(8,128)(2,1)S(1)}, bf16[384,128]{1,0:T(8,128)(2,1)S(1)}, u32[]{:S(2)}, u32[]{:S(2)}) collective-permute-start(bf16[384,128]{1,0:T(8,128)(2,1)S(1)} %get-tuple-element.50.own), channel_id=1, source_target_pairs={{0,2},{1,3},{2,0},{3,1},{4,6},{5,7},{6,4},{7,5},{8,10},{9,11},{10,... | collective-permute-start | bytes 294920 | tf_op jit(solution)/shard_map/ppermute | solution.py:374
  31.6 5.8 %collective-permute-start.8 = (bf16[384,128]{1,0:T(8,128)(2,1)S(1)}, bf16[384,128]{1,0:T(8,128)(2,1)S(1)}, u32[]{:S(2)}, u32[]{:S(2)}) collective-permute-start(bf16[384,128]{1,0:T(8,128)(2,1)S(1)} %get-tuple-element.50.own), channel_id=1, source_target_pairs={{0,3},{1,2},{2,1},{3,0},{4,7},{5,6},{6,5},{7,4},{8,11},{9,10},{10,... | collective-permute-start | bytes 294920 | tf_op jit(solution)/shard_map/ppermute | solution.py:374
  32.8 4.7 %collective-permute-start.7 = (bf16[384,128]{1,0:T(8,128)(2,1)S(1)}, bf16[384,128]{1,0:T(8,128)(2,1)S(1)}, u32[]{:S(2)}, u32[]{:S(2)}) collective-permute-start(bf16[384,128]{1,0:T(8,128)(2,1)S(1)} %get-tuple-element.50.own), channel_id=1, source_target_pairs={{0,1},{1,0},{2,3},{3,2},{4,5},{5,4},{6,7},{7,6},{8,9},{9,8},{10,11... | collective-permute-start | bytes 294920 | tf_op jit(solution)/shard_map/ppermute | solution.py:374
  38.6 12.6 %collective-permute-start.10 = (bf16[768,128]{1,0:T(8,128)(2,1)S(1)}, bf16[768,128]{1,0:T(8,128)(2,1)S(1)}, u32[]{:S(2)}, u32[]{:S(2)}) collective-permute-start(bf16[768,128]{1,0:T(8,128)(2,1)S(1)} %get-tuple-element.56), channel_id=1, source_target_pairs={{8,16},{12,20},{16,8},{20,12},{24,32},{28,36},{32,24},{36,28},{40,... | collective-permute-start | bytes 589832 | tf_op jit(solution)/shard_map/ppermute | solution.py:367
  42.6 8.6 %collective-permute-start.11 = (bf16[768,128]{1,0:T(8,128)(2,1)S(1)}, bf16[768,128]{1,0:T(8,128)(2,1)S(1)}, u32[]{:S(2)}, u32[]{:S(2)}) collective-permute-start(bf16[768,128]{1,0:T(8,128)(2,1)S(1)} %get-tuple-element.57), channel_id=1, source_target_pairs={{0,8},{4,12},{8,0},{12,4},{16,24},{20,28},{24,16},{28,20},{32,40},... | collective-permute-start | bytes 589832 | tf_op jit(solution)/shard_map/ppermute | solution.py:367
  42.7 8.5 %collective-permute-start.12 = (bf16[768,128]{1,0:T(8,128)(2,1)S(1)}, bf16[768,128]{1,0:T(8,128)(2,1)S(1)}, u32[]{:S(2)}, u32[]{:S(2)}) collective-permute-start(bf16[768,128]{1,0:T(8,128)(2,1)S(1)} %get-tuple-element.58), channel_id=1, source_target_pairs={{0,4},{4,0},{8,12},{12,8},{16,20},{20,16},{24,28},{28,24},{32,36},... | collective-permute-start | bytes 589832 | tf_op jit(solution)/shard_map/ppermute | solution.py:367
  42.7 9.1 %collective-permute-start.13 = (bf16[768,128]{1,0:T(8,128)(2,1)S(1)}, bf16[768,128]{1,0:T(8,128)(2,1)S(1)}, u32[]{:S(2)}, u32[]{:S(2)}) collective-permute-start(bf16[768,128]{1,0:T(8,128)(2,1)S(1)} %get-tuple-element.59), channel_id=1, source_target_pairs={{4,8},{8,4},{12,16},{16,12},{20,24},{24,20},{28,32},{32,28},{36,40... | collective-permute-start | bytes 589832 | tf_op jit(solution)/shard_map/ppermute | solution.py:367
  54.2 6.7 %collective-permute-start.14 = (bf16[384,128]{1,0:T(8,128)(2,1)S(1)}, bf16[384,128]{1,0:T(8,128)(2,1)S(1)}, u32[]{:S(2)}, u32[]{:S(2)}) collective-permute-start(bf16[384,128]{1,0:T(8,128)(2,1)S(1)} %get-tuple-element.61), channel_id=1, source_target_pairs={{0,2},{1,3},{2,0},{3,1},{4,6},{5,7},{6,4},{7,5},{8,10},{9,11},{10,... | collective-permute-start | bytes 294920 | tf_op jit(solution)/shard_map/ppermute | solution.py:374
  56.2 5.9 %collective-permute-start.15 = (bf16[384,128]{1,0:T(8,128)(2,1)S(1)}, bf16[384,128]{1,0:T(8,128)(2,1)S(1)}, u32[]{:S(2)}, u32[]{:S(2)}) collective-permute-start(bf16[384,128]{1,0:T(8,128)(2,1)S(1)} %get-tuple-element.62), channel_id=1, source_target_pairs={{0,3},{1,2},{2,1},{3,0},{4,7},{5,6},{6,5},{7,4},{8,11},{9,10},{10,... | collective-permute-start | bytes 294920 | tf_op jit(solution)/shard_map/ppermute | solution.py:374
  57.6 4.6 %collective-permute-start.16 = (bf16[384,128]{1,0:T(8,128)(2,1)S(1)}, bf16[384,128]{1,0:T(8,128)(2,1)S(1)}, u32[]{:S(2)}, u32[]{:S(2)}) collective-permute-start(bf16[384,128]{1,0:T(8,128)(2,1)S(1)} %get-tuple-element.63), channel_id=1, source_target_pairs={{0,1},{1,0},{2,3},{3,2},{4,5},{5,4},{6,7},{7,6},{8,9},{9,8},{10,11... | collective-permute-start | bytes 294920 | tf_op jit(solution)/shard_map/ppermute | solution.py:374
